TPU v7x, 32 devices: a whole 2x2x4 slice. The times are simulated.
32 devices in a mesh: stripe: 2 (over x), tile: 16 (over z, y, core).
Axes of the slice: x: 2, y: 2, z: 4, core: 2. Of those that a mesh axis runs over, the one named last changes fastest.
Arguments:
- mask_tiles: float32 [32, 1024, 1024], P(('stripe', 'tile')), parts along dimension 0, may hold values from -1 to 1
- target_grid: float32 [32, 16384], P(('stripe', 'tile')), parts along dimension 0, may hold values from 0 to 1
- kernels: float32 [16, 2, 24, 64, 96], P('tile'), may hold values from -48 to 48
- kern_weight: float32 [24], replicated, may hold values from 0.05 to 1
- owner_list: int32 [32, 1], P('stripe'), parts along dimension 0, may hold values from 0 to 15, as said below
Outputs:
- mask_out: float32 [32, 1024, 1024], P(('stripe', 'tile')), parts along dimension 0
- owner_error: float32 [32], P(('stripe', 'tile')), parts along dimension 0
There are 2 independent parts, one for each index of `stripe`. A program takes and returns all parts, laid end to end along the dimension named above; an argument that names none is the same for every part. Nothing has to cross between parts.
Inputs may be any that keep to these rules, and one draw needn't show every extreme that they name: `owner_list`: every owner is named by 0 to 2 tiles of a stripe, and some owner by exactly 2.
All inputs are finite; a program needn't handle non-finite values.
Results may differ from a plain program's by a relative error of at most 0.0001.
Values sent between devices are 32-bit elements; how exact they have to be, the bound alone decides.
No kernel may reach another device: no remote copies, remote signals or barrier semaphores. Data moves between devices by JAX's collectives and lax.ppermute only.
A program may use at most 128 MiB of HBM per device.

v0:
```python
import math

import jax
import jax.numpy as jnp
import numpy as np
from jax import lax
from jax.experimental import pallas as pl
from jax.experimental.pallas import tpu as pltpu
from jax.sharding import PartitionSpec as P

AMBIT = 256
GRID_X = 192
GRID_Y = 128
CORE_X = 128
RESIST_SLOPE = 3.0
RESIST_LEVEL = 1.2
DIFFUSE_RATE = 0.2
STEP_SIZE = 1.0

LANES = 128
ROWS = 72
ROWS_PAD = 80
F32 = jnp.float32
BF16 = jnp.bfloat16


def halves_np(table):
    table = np.asarray(table, np.float32)
    top = table.astype(BF16)
    rest = (table - top.astype(np.float32)).astype(BF16)
    return top, rest


def halves(value):
    top = value.astype(BF16)
    rest = (value - top.astype(F32)).astype(BF16)
    return top, rest


def mm(left, right):
    return jnp.dot(left, right, preferred_element_type=F32)


def real_waves(places, period, most, width):
    angles = 2.0 * np.pi * np.outer(places, np.arange(most + 1)) / period
    waves = np.concatenate([np.cos(angles), np.sin(angles[:, 1:])], axis=1)
    return np.pad(waves, ((0, 0), (0, width - waves.shape[1])))


def signed_picks(count, width):
    freqs = np.arange(count) - count // 2
    most = count // 2
    even = np.zeros((count, width))
    odd = np.zeros((count, width))
    for at, freq in enumerate(freqs):
        even[at, abs(freq)] = 1.0
        if freq != 0:
            odd[at, most + abs(freq)] = np.sign(freq)
    return even, odd


def mask_tables(tile_px, freq_y, freq_x):
    win = tile_px + 2 * AMBIT
    mid_x = (GRID_X - 1) / 2 * (win // GRID_X)
    mid_y = (GRID_Y - 1) / 2 * (tile_px // GRID_Y)
    cols = real_waves(np.arange(win) - mid_x, win, freq_x // 2, LANES)
    rows = real_waves(np.arange(tile_px) - mid_y, tile_px, freq_y // 2, ROWS_PAD)
    return cols, rows


def spectrum_kernel(mask_ref, own_ref, low_ref, high_ref, rows_ref, out_ref, total):
    step = pl.program_id(0)

    @pl.when(step == 0)
    def _():
        total[...] = jnp.zeros_like(total)

    top, rest = halves(mask_ref[0])
    own_table = own_ref[...]
    low_table = low_ref[...]
    high_table = high_ref[...]
    width = top.shape[1]

    def columns(top_part, rest_part, table):
        both = mm(top_part, table)
        return both[:, :LANES] + both[:, LANES:] + mm(rest_part, table[:, :LANES])

    parts = (
        columns(top, rest, own_table),
        columns(top[:, :AMBIT], rest[:, :AMBIT], low_table),
        columns(top[:, width - AMBIT :], rest[:, width - AMBIT :], high_table),
    )
    for part, terms in enumerate(parts):
        total[part] += mm(rows_ref[...], jnp.concatenate(halves(terms), axis=1))

    @pl.when(step == pl.num_programs(0) - 1)
    def _():
        for part in range(3):
            out_ref[part] = (
                total[part, :ROWS, :LANES]
                + total[part, :ROWS, LANES:]
                + total[part, ROWS_PAD : ROWS_PAD + ROWS, :LANES]
            )


def mask_spectrum(mask_tiles, cols, rows):
    tile_px = mask_tiles.shape[1]
    block = 256
    stack = [
        np.concatenate(halves_np(part), axis=1)
        for part in (
            cols[AMBIT : AMBIT + tile_px],
            cols[AMBIT + tile_px :],
            cols[:AMBIT],
        )
    ]
    row_stack = np.concatenate(halves_np(rows.T), axis=0)
    full = lambda arr: pl.BlockSpec(arr.shape, lambda i: (0,) * arr.ndim)
    return pl.pallas_call(
        spectrum_kernel,
        grid=(tile_px // block,),
        in_specs=[pl.BlockSpec((1, block, tile_px), lambda i: (0, i, 0))]
        + [full(part) for part in stack]
        + [pl.BlockSpec((2 * ROWS_PAD, block), lambda i: (0, i))],
        out_specs=pl.BlockSpec((3, ROWS, LANES), lambda i: (0, 0, 0)),
        out_shape=jax.ShapeDtypeStruct((3, ROWS, LANES), F32),
        scratch_shapes=[pltpu.VMEM((3, 2 * ROWS_PAD, 2 * LANES), F32)],
        compiler_params=pltpu.CompilerParams(vmem_limit_bytes=24 * 2**20),
        name="mask_spectrum",
    )(mask_tiles, *[jnp.asarray(part) for part in stack], jnp.asarray(row_stack))


def update_kernel(tile_ref, mask_ref, own_ref, low_ref, high_ref, cols_ref, rows_ref, out_ref, held):
    step = pl.program_id(0)

    @pl.when(step == 0)
    def _():
        def spread(packet, table):
            top, rest = halves(packet)
            both = mm(jnp.concatenate([top, rest], axis=1), jnp.concatenate([table[:LANES], table[:LANES]], axis=0))
            return both + mm(top, table[LANES:])

        width = out_ref.shape[2]
        wide = spread(own_ref[0], cols_ref[:, AMBIT : AMBIT + width])
        left = spread(low_ref[0], cols_ref[:, AMBIT + width :])
        right = spread(high_ref[0], cols_ref[:, :AMBIT])
        wide = jnp.concatenate(
            [
                wide[:, :AMBIT] + left,
                wide[:, AMBIT : width - AMBIT],
                wide[:, width - AMBIT :] + right,
            ],
            axis=1,
        )
        wide = jnp.concatenate([wide, jnp.zeros((ROWS_PAD - ROWS, width), F32)], axis=0)
        top, rest = halves(wide)
        held[:ROWS_PAD] = top
        held[ROWS_PAD : 2 * ROWS_PAD] = rest
        held[2 * ROWS_PAD :] = top

    out_ref[0] = mask_ref[0] - STEP_SIZE * mm(rows_ref[...], held[...])


def mask_update(mask_tiles, own, low, high, cols, rows):
    tile_px = mask_tiles.shape[1]
    block = 256
    col_stack = np.concatenate(halves_np(cols.T), axis=0)
    top, rest = halves_np(rows)
    row_stack = np.concatenate([top, top, rest], axis=1)
    return pl.pallas_call(
        update_kernel,
        grid=(tile_px // block,),
        in_specs=[
            pl.BlockSpec(memory_space=pltpu.SMEM),
            pl.BlockSpec((1, block, tile_px), lambda i: (0, i, 0)),
            pl.BlockSpec((1, ROWS, LANES), lambda i: (0, 0, 0)),
            pl.BlockSpec((1, ROWS, LANES), lambda i: (0, 0, 0)),
            pl.BlockSpec((1, ROWS, LANES), lambda i: (0, 0, 0)),
            pl.BlockSpec(col_stack.shape, lambda i: (0, 0)),
            pl.BlockSpec((block, row_stack.shape[1]), lambda i: (i, 0)),
        ],
        out_specs=pl.BlockSpec((1, block, tile_px), lambda i: (0, i, 0)),
        out_shape=jax.ShapeDtypeStruct(mask_tiles.shape, F32),
        scratch_shapes=[pltpu.VMEM((3 * ROWS_PAD, tile_px), BF16)],
        compiler_params=pltpu.CompilerParams(vmem_limit_bytes=24 * 2**20),
        name="mask_update",
    )(
        jnp.zeros((1,), jnp.int32),
        mask_tiles,
        own,
        low,
        high,
        jnp.asarray(col_stack),
        jnp.asarray(row_stack),
    )


def image_tables(freq_y, freq_x):
    places_v = np.arange(GRID_X) - (GRID_X - 1) / 2
    freqs_b = np.arange(freq_x) - (freq_x - 1) / 2
    beta = 2.0 * np.pi * np.outer(freqs_b, places_v) / GRID_X
    first = (GRID_X - CORE_X) // 2

    def block(lane_of):
        table = np.zeros((2 * LANES, 2 * LANES))
        for place, lane in lane_of:
            table[:freq_x, lane] = np.cos(beta[:, place])
            table[:freq_x, LANES + lane] = np.sin(beta[:, place])
            table[LANES : LANES + freq_x, lane] = -np.sin(beta[:, place])
            table[LANES : LANES + freq_x, LANES + lane] = np.cos(beta[:, place])
        return table

    core = block([(first + lane, lane) for lane in range(CORE_X)])
    last = first + CORE_X
    rim = block(
        [(first - 2, LANES - 2), (first - 1, LANES - 1), (last, 0), (last + 1, 1)]
    )
    places_u = np.arange(GRID_Y // 2) + 0.5
    freqs_a = np.arange(freq_y) - (freq_y - 1) / 2
    alpha = 2.0 * np.pi * np.outer(places_u, freqs_a) / GRID_Y
    rows = np.concatenate([np.cos(alpha), np.sin(alpha)], axis=0)
    return core, rim, rows


def pick_tables(freq_y, freq_x):
    col_even, col_odd = signed_picks(freq_x, LANES)
    row_even, row_odd = signed_picks(freq_y, ROWS)
    lanes = np.zeros((LANES, 2 * LANES))
    lanes[:, :freq_x] = col_even.T
    lanes[:, LANES : LANES + freq_x] = col_odd.T
    rows = np.block([[row_even, -row_odd], [-row_odd, -row_even]])
    return lanes, rows


def imaging_kernel(
    me_ref, owner_ref, weight_ref, packets_ref, targets_ref, kern_ref,
    core_ref, core_t_ref, rim_ref, rim_t_ref, rows_ref, rows_t_ref,
    lanes_ref, lanes_t_ref, pick_ref, pick_t_ref, turn_ref,
    slopes_ref, error_ref,
    spec, field, rim_field, rim_lanes, rim_slope, slope_acc, scale_ref,
):
    me = me_ref[0]
    tiles = owner_ref.shape[0]
    kern_count, freq_y, freq_x = kern_ref.shape[2:]

    def find(tile, carry):
        count, first, second = carry
        mine = owner_ref[tile, 0] == me
        first = jnp.where(mine & (count == 0), tile, first)
        second = jnp.where(mine & (count == 1), tile, second)
        return count + mine.astype(jnp.int32), first, second

    zero = jnp.int32(0)
    count, first, second = lax.fori_loop(0, tiles, find, (zero, zero, zero))
    slots = (first, second)

    def pair(value):
        top, rest = halves(value)
        return jnp.concatenate([top, rest], axis=0)

    for slot in range(2):
        packet = packets_ref[slots[slot]]
        packet = jnp.where(slot < count, packet, jnp.zeros_like(packet))
        both = mm(pair(packet), lanes_ref[...])
        both = both[:ROWS] + both[ROWS:]
        tall = jnp.concatenate([both[:, :LANES], both[:, LANES:]], axis=0)
        top, rest = halves(tall)
        spec[slot] = mm(pick_ref[...], top) + mm(pick_ref[...], rest)

    half = GRID_Y // 2
    lane = lax.broadcasted_iota(jnp.int32, (freq_y, LANES), 1)
    live_lane = lane < freq_x

    def kern_at(k):
        def one(part):
            raw = kern_ref[0, part, k]
            wide = jnp.concatenate([raw, jnp.zeros((freq_y, LANES - freq_x), F32)], axis=1)
            return wide
        return one(0), one(1)

    def to_image(stack):
        top, rest = halves(stack)
        return mm(rows_ref[...], jnp.concatenate([top, rest, top], axis=0))

    def from_image(stack):
        top, rest = halves(stack)
        return mm(rows_t_ref[...], jnp.concatenate([top, rest, top], axis=0))

    def thrice(top, rest, table_ref):
        return (
            mm(top, table_ref[: 2 * LANES])
            + mm(rest, table_ref[: 2 * LANES])
            + mm(top, table_ref[2 * LANES :])
        )

    def waves(stack):
        even_re, even_im = stack[:half, :LANES], stack[:half, LANES:]
        odd_re, odd_im = stack[half:, :LANES], stack[half:, LANES:]
        return even_re - odd_im, even_im + odd_re, even_re + odd_im, even_im - odd_re

    def unwaves(plus_re, plus_im, minus_re, minus_im):
        above = jnp.concatenate([plus_re + minus_re, plus_im + minus_im], axis=1)
        below = jnp.concatenate([plus_im - minus_im, minus_re - plus_re], axis=1)
        return jnp.concatenate([above, below], axis=0)

    rim_lanes[...] = jnp.zeros_like(rim_lanes)

    def forward(k, sums):
        kern_re, kern_im = kern_at(k)
        weight = weight_ref[k]
        new = []
        for slot in range(2):
            spec_re, spec_im = spec[slot, :freq_y], spec[slot, freq_y:]
            wave = jnp.concatenate(
                [kern_re * spec_re - kern_im * spec_im, kern_re * spec_im + kern_im * spec_re], axis=1
            )
            top, rest = halves(wave)
            cols = thrice(top, rest, core_ref)
            edge = thrice(top, rest, rim_ref)
            rim_lanes[slot, :, :LANES] += pltpu.roll(edge[:, :LANES], 4 * k, 1)
            rim_lanes[slot, :, LANES:] += pltpu.roll(edge[:, LANES:], 4 * k, 1)
            parts = waves(to_image(cols))
            for part in range(4):
                field[slot, k, part] = parts[part]
            plus, minus = sums[slot]
            plus = plus + weight * (parts[0] * parts[0] + parts[1] * parts[1])
            minus = minus + weight * (parts[2] * parts[2] + parts[3] * parts[3])
            new.append((plus, minus))
        return tuple(new)

    blank = jnp.zeros((half, LANES), F32)
    sums = lax.fori_loop(0, kern_count, forward, ((blank, blank), (blank, blank)))

    def set_scale(k, carry):
        lane_row = lax.broadcasted_iota(jnp.int32, (1, LANES), 1)
        group = lax.rem(lane_row + 2, LANES) // 4
        return jnp.where(group == k, weight_ref[k], carry)

    lane_weight = lax.fori_loop(0, kern_count, set_scale, jnp.zeros((1, LANES), F32))

    norm = 1.0 / (64.0 * GRID_Y * GRID_X)
    square = norm * norm
    lane_half = lax.broadcasted_iota(jnp.int32, (half, LANES), 1)
    row_half = lax.broadcasted_iota(jnp.int32, (half, 2 * LANES), 0)
    lane_wide = lax.broadcasted_iota(jnp.int32, (half, 2 * LANES), 1)
    near = (lane_half < 2) | (lane_half >= LANES - 2)
    inside = lane_wide < LANES

    def blur(plus, minus):
        def one(value, other):
            later = jnp.where(row_half == half - 1, value, pltpu.roll(value, half - 1, 0))
            sooner = jnp.where(row_half == 0, other, pltpu.roll(value, 1, 0))
            sides = pltpu.roll(value, 1, 1) + pltpu.roll(value, 2 * LANES - 1, 1)
            return value + DIFFUSE_RATE * (later + sooner + sides - 4.0 * value)
        return one(plus, minus), one(minus, plus)

    def fold(value):
        def back(amount):
            return pltpu.roll(value, LANES - amount, 1)
        value = value + back(48)
        value = value + back(24)
        value = value + back(12)
        return value + back(4) + back(8)

    def unfold(value):
        value = jnp.where(near, value, 0.0)
        value = value + pltpu.roll(value, 4, 1) + pltpu.roll(value, 8, 1)
        value = value + pltpu.roll(value, 12, 1)
        value = value + pltpu.roll(value, 24, 1)
        return value + pltpu.roll(value, 48, 1)

    error = jnp.float32(0.0)
    for slot in range(2):
        live = (slot < count).astype(F32)
        rim_parts = waves(to_image(rim_lanes[slot]))
        for part in range(4):
            rim_field[part] = rim_parts[part]
        weights = jnp.broadcast_to(lane_weight, (half, LANES))
        rim_plus = weights * (rim_parts[0] * rim_parts[0] + rim_parts[1] * rim_parts[1])
        rim_minus = weights * (rim_parts[2] * rim_parts[2] + rim_parts[3] * rim_parts[3])
        plus = jnp.concatenate([sums[slot][0], jnp.where(near, fold(rim_plus), 0.0)], axis=1) * square
        minus = jnp.concatenate([sums[slot][1], jnp.where(near, fold(rim_minus), 0.0)], axis=1) * square
        plus, minus = blur(*blur(plus, minus))
        target = targets_ref[slots[slot]]
        t_top = target[:half]
        one = t_top.astype(BF16)
        t_top = t_top - one.astype(F32)
        two = t_top.astype(BF16)
        three = (t_top - two.astype(F32)).astype(BF16)
        turned = mm(turn_ref[...], one) + mm(turn_ref[...], two) + mm(turn_ref[...], three)

        def slope_of(value, goal):
            resist = 1.0 / (1.0 + jnp.exp(-RESIST_SLOPE * (value[:, :LANES] - RESIST_LEVEL)))
            misfit = resist - goal
            slope = (2.0 * RESIST_SLOPE) * misfit * resist * (1.0 - resist)
            slope = jnp.concatenate([slope, jnp.zeros_like(slope)], axis=1)
            return slope, jnp.sum(misfit * misfit)

        slope_plus, err_plus = slope_of(plus, target[half:])
        slope_minus, err_minus = slope_of(minus, turned)
        error = error + live * (err_plus + err_minus)
        slope_plus, slope_minus = blur(*blur(slope_plus, slope_minus))
        factor = 2.0 * square
        scale_ref[slot, 0] = slope_plus[:, :LANES] * factor
        scale_ref[slot, 1] = slope_minus[:, :LANES] * factor
        rim_f_plus = unfold(slope_plus[:, LANES:] * factor) * weights
        rim_f_minus = unfold(slope_minus[:, LANES:] * factor) * weights
        rim_slope[slot] = from_image(
            unwaves(
                rim_f_plus * rim_field[0],
                rim_f_plus * rim_field[1],
                rim_f_minus * rim_field[2],
                rim_f_minus * rim_field[3],
            )
        )
    error_ref[0] = error * (1.0 / (GRID_Y * CORE_X))

    slope_acc[...] = jnp.zeros_like(slope_acc)
    rim_lane = (lane < 2) | (lane >= LANES - 2)

    def backward(k, carry):
        kern_re, kern_im = kern_at(k)
        weight = weight_ref[k]
        for slot in range(2):
            plus = scale_ref[slot, 0] * weight
            minus = scale_ref[slot, 1] * weight
            cols = from_image(
                unwaves(
                    plus * field[slot, k, 0],
                    plus * field[slot, k, 1],
                    minus * field[slot, k, 2],
                    minus * field[slot, k, 3],
                )
            )
            top, rest = halves(cols)
            wave = thrice(top, rest, core_t_ref)
            edge = jnp.concatenate(
                [
                    pltpu.roll(rim_slope[slot, :, :LANES], LANES - 4 * k, 1),
                    pltpu.roll(rim_slope[slot, :, LANES:], LANES - 4 * k, 1),
                ],
                axis=1,
            )
            top, rest = halves(edge)
            wave = wave + thrice(top, rest, rim_t_ref)
            wave_re, wave_im = wave[:, :LANES], wave[:, LANES:]
            slope_acc[slot, :freq_y] += wave_re * kern_re + wave_im * kern_im
            slope_acc[slot, freq_y:] += wave_im * kern_re - wave_re * kern_im
        return carry

    lax.fori_loop(0, kern_count, backward, 0)

    for slot in (1, 0):
        top, rest = halves(slope_acc[slot])
        tall = mm(pick_t_ref[...], top) + mm(pick_t_ref[...], rest)
        wide = jnp.concatenate([tall[:ROWS], tall[ROWS:]], axis=1)
        both = mm(pair(wide), lanes_t_ref[...])
        slopes_ref[slots[slot]] = both[:ROWS] + both[ROWS:]


def owner_imaging(me, owner_list, kern_weight, packets, targets, kernels):
    kern_count, freq_y, freq_x = kernels.shape[2:]
    tiles = packets.shape[0]
    core, rim, rows = image_tables(freq_y, freq_x)
    lanes, picks = pick_tables(freq_y, freq_x)

    def tall(table):
        return np.concatenate(halves_np(table), axis=0)

    def three(table):
        top, rest = halves_np(table)
        return np.concatenate([top, top, rest], axis=1)

    tables = [
        tall(core),
        tall(core.T),
        tall(rim),
        tall(rim.T),
        three(rows),
        three(rows.T),
        lanes.astype(BF16),
        lanes.T.astype(BF16),
        picks.astype(BF16),
        picks.T.astype(BF16),
        np.eye(GRID_Y // 2)[::-1].astype(BF16),
    ]
    half = GRID_Y // 2
    smem = pl.BlockSpec(memory_space=pltpu.SMEM)
    vmem = pl.BlockSpec(memory_space=pltpu.VMEM)
    return pl.pallas_call(
        imaging_kernel,
        in_specs=[smem, smem, smem] + [vmem] * (3 + len(tables)),
        out_specs=(vmem, smem),
        out_shape=(
            jax.ShapeDtypeStruct((tiles, ROWS, LANES), F32),
            jax.ShapeDtypeStruct((1,), F32),
        ),
        scratch_shapes=[
            pltpu.VMEM((2, 2 * freq_y, LANES), F32),
            pltpu.VMEM((2, kern_count, 4, half, LANES), F32),
            pltpu.VMEM((4, half, LANES), F32),
            pltpu.VMEM((2, freq_y, 2 * LANES), F32),
            pltpu.VMEM((2, freq_y, 2 * LANES), F32),
            pltpu.VMEM((2, 2 * freq_y, LANES), F32),
            pltpu.VMEM((2, 2, half, LANES), F32),
        ],
        compiler_params=pltpu.CompilerParams(vmem_limit_bytes=40 * 2**20),
        name="owner_imaging",
    )(me, owner_list, kern_weight, packets, targets, kernels, *[jnp.asarray(t) for t in tables])


def on_device(mask_tiles, target_grid, kernels, kern_weight, owner_list):
    tile_px = mask_tiles.shape[1]
    freq_y, freq_x = kernels.shape[3:]
    count = lax.axis_size("tile")
    cols, rows = mask_tables(tile_px, freq_y, freq_x)
    me = lax.axis_index("tile").astype(jnp.int32)
    up = [(i, i + 1) for i in range(count - 1)]
    down = [(i + 1, i) for i in range(count - 1)]

    def spread(packet):
        wide = jnp.broadcast_to(packet[None], (count,) + packet.shape)
        return lax.all_to_all(wide, "tile", 0, 0, tiled=True)

    targets = spread(target_grid.reshape(GRID_Y, CORE_X))
    parts = mask_spectrum(mask_tiles, cols, rows)
    from_next = lax.ppermute(parts[1], "tile", down)
    from_last = lax.ppermute(parts[2], "tile", up)
    packets = spread(parts[0] + from_next + from_last)
    slopes, owner_error = owner_imaging(
        me.reshape(1), owner_list, kern_weight, packets, targets, kernels
    )
    returned = lax.all_to_all(slopes, "tile", 0, 0, tiled=True)
    my_owner = lax.dynamic_index_in_dim(owner_list[:, 0], me, 0, keepdims=False)
    own = lax.dynamic_index_in_dim(returned, my_owner, 0, keepdims=True)
    last = lax.ppermute(own, "tile", up)
    following = lax.ppermute(own, "tile", down)
    current = mask_update(mask_tiles, own, last, following, cols, rows)
    return (current, owner_error)


def solution(mesh):
    placed = (
        P(("stripe", "tile"), None, None),
        P(("stripe", "tile"), None),
        P("tile", None, None, None, None),
        P(),
        P("stripe", None),
    )
    return jax.shard_map(
        on_device,
        mesh=mesh,
        in_specs=placed,
        out_specs=(P(("stripe", "tile"), None, None), P(("stripe", "tile"))),
        check_vma=False,
    )
```

profile of v0, /device:TPU:18, one launch (start us, length us, event | category | flops | bytes accessed | tf_op | source)
XLA Modules:
  0.0 148.6 jit_solution(17894173887139641129)
XLA Ops:
  0.6 0.0 copy-start
  0.6 2.2 %copy-done = f32[1,1024,1024]{2,1,0:T(8,128)S(1)} copy-done((f32[1,1024,1024]{2,1,0:T(8,128)S(1)}, f32[1,1024,1024]{2,1,0:T(8,128)}, u32[]{:S(2)}) %copy-start) | copy-done | bytes 4194328
  2.8 0.0 copy-start.5
  2.8 1.0 copy-done.5
  3.9 0.0 copy-start.7
  3.9 1.0 copy-done.7
  4.8 0.0 copy-start.12
  4.8 0.9 copy-done.12
  5.7 0.0 copy-start.13
  5.7 0.9 copy-done.13
  6.6 0.0 copy-start.22
  6.6 0.0 copy-start.23
  6.7 0.0 copy-start.2
  6.7 0.0 copy-start.8
  6.7 0.0 copy-start.14
  6.7 0.0 copy-start.21
  6.7 3.1 %mask_spectrum.1 = f32[3,72,128]{2,1,0:T(8,128)S(1)} custom-call(f32[1,1024,1024]{2,1,0:T(8,128)S(1)} %copy-done, bf16[1024,256]{1,0:T(8,128)(2,1)S(1)} %copy-done.5, bf16[256,256]{1,0:T(8,128)(2,1)S(1)} %copy-done.13, bf16[256,256]{1,0:T(8,128)(2,1)S(1)} %copy-done.12, bf16[160,1024]{1,0:T(8,128)(2,1)S(1)} %copy-done.7), custom_call_target="tpu_custom_call" | custom-call | tf_op jit(solution)/shard_map/mask_spectrum/pallas_call | solution.py:119
  9.8 2.7 %collective-permute-start = (f32[72,128]{1,0:T(8,128)S(1)}, f32[72,128]{1,0:T(8,128)S(1)}, u32[]{:S(2)}, u32[]{:S(2)}) collective-permute-start(f32[72,128]{1,0:T(8,128)S(1)} %get-tuple-element.6), channel_id=1, source_target_pairs={{1,0},{2,1},{3,2},{4,3},{5,4},{6,5},{7,6},{8,7},{9,8},{10,9},{11,1... | collective-permute-start | bytes 110600 | tf_op jit(solution)/shard_map/ppermute | solution.py:527
  12.6 1.9 %collective-permute-start.1 = (f32[72,128]{1,0:T(8,128)S(1)}, f32[72,128]{1,0:T(8,128)S(1)}, u32[]{:S(2)}, u32[]{:S(2)}) collective-permute-start(f32[72,128]{1,0:T(8,128)S(1)} %get-tuple-element.7), channel_id=1, source_target_pairs={{0,1},{1,2},{2,3},{3,4},{4,5},{5,6},{6,7},{7,8},{8,9},{9,10},{10,1... | collective-permute-start | bytes 110600 | tf_op jit(solution)/shard_map/ppermute | solution.py:528
  14.5 0.0 collective-permute-done
  14.5 4.2 %collective-permute-done.1 = f32[72,128]{1,0:T(8,128)S(1)} collective-permute-done((f32[72,128]{1,0:T(8,128)S(1)}, f32[72,128]{1,0:T(8,128)S(1)}, u32[]{:S(2)}, u32[]{:S(2)}) %collective-permute-start.1) | collective-permute-done | bytes 36896 | tf_op jit(solution)/shard_map/ppermute | solution.py:528
  18.8 20.4 %all_to_all.15.packets_ref = f32[16,72,128]{2,1,0:T(8,128)S(1)} all-to-all(f32[16,72,128]{2,1,0:T(8,128)S(1)} %broadcast_in_dim.6), channel_id=1, replica_groups=mesh['stripe'=2,'tile'=16] {'tile'}, dimensions={0} | all-to-all | bytes 1179648 | tf_op jit(solution)/shard_map/all_to_all | solution.py:523
  39.2 0.0 copy-done.22
  39.2 1.1 broadcast_in_dim.15
  40.2 5.6 %all-to-all-start.1 = ((f32[16,128,128]{2,1,0:T(8,128)}), f32[16,128,128]{2,1,0:T(8,128)S(1)}, u32[]{:S(2)}, u32[]{:S(2)}) async-start(f32[16,128,128]{2,1,0:T(8,128)} %broadcast_in_dim.15), calls=%async_computation.1 | async-start | bytes 2097152 | tf_op jit(solution)/shard_map/all_to_all | solution.py:523
  45.8 0.0 copy-done.23
  45.8 0.1 copy.24.owner_ref
  45.9 25.1 %all-to-all-done.1.targets_ref = f32[16,128,128]{2,1,0:T(8,128)S(1)} async-done(((f32[16,128,128]{2,1,0:T(8,128)}), f32[16,128,128]{2,1,0:T(8,128)S(1)}, u32[]{:S(2)}, u32[]{:S(2)}) %all-to-all-start.1) | async-done | bytes 1048608 | tf_op jit(solution)/shard_map/all_to_all | solution.py:523
  71.0 0.0 copy-done.2
  71.0 0.0 copy-done.8
  71.0 0.0 copy-done.14
  71.0 0.0 copy-done.21
  71.0 0.0 copy-start.9
  71.0 0.9 copy-done.9
  72.0 0.0 copy-start.10
  72.0 0.9 copy-done.10
  72.9 0.0 copy-start.11
  72.9 0.9 copy-done.11
  73.9 0.0 copy-start.15
  73.9 0.8 copy-done.15
  74.7 0.8 copy-done.16
  75.5 0.8 copy-done.17
  76.4 0.8 copy-done.18
  77.2 0.0 copy-start.19
  77.2 0.8 copy-done.19
  77.9 0.0 copy-start.20
  77.9 0.7 copy-done.20
  78.7 32.5 %owner_imaging.1 = (f32[16,72,128]{2,1,0:T(8,128)S(1)}, f32[1]{0:T(128)}) custom-call(s32[1]{0:T(128)} %bitcast.me_ref, s32[16,1]{1,0:T(8,128)S(1)} %copy.24.owner_ref, f32[24]{0:T(128)S(1)} %copy-done.21, f32[16,72,128]{2,1,0:T(8,128)S(1)} %all_to_all.15.packets_ref, f32[16,128,128]{2,1,0:T(8,128)S(1)} %all-to-all-done.1.targets_ref, ...), custom_call_target="tpu_custom_call" | custom-call | tf_op jit(solution)/shard_map/owner_imaging/pallas_call | solution.py:490
  111.2 0.0 copy-start.4
  111.2 0.8 copy-done.4
  112.0 4.6 %all-to-all-start.2 = ((f32[16,72,128]{2,1,0:T(8,128)}), f32[16,72,128]{2,1,0:T(8,128)S(1)}, u32[]{:S(2)}, u32[]{:S(2)}) async-start(f32[16,72,128]{2,1,0:T(8,128)} %copy-done.4), calls=%async_computation.2 | async-start | bytes 1179648 | tf_op jit(solution)/shard_map/all_to_all | solution.py:533
  116.7 0.6 constant_dynamic-slice_fusion.1
  119.2 12.7 %all-to-all-done.2 = f32[16,72,128]{2,1,0:T(8,128)S(1)} async-done(((f32[16,72,128]{2,1,0:T(8,128)}), f32[16,72,128]{2,1,0:T(8,128)S(1)}, u32[]{:S(2)}, u32[]{:S(2)}) %all-to-all-start.2) | async-done | bytes 589856 | tf_op jit(solution)/shard_map/all_to_all | solution.py:533
  132.0 2.8 %collective-permute-start.3 = (f32[1,72,128]{2,1,0:T(8,128)S(1)}, f32[1,72,128]{2,1,0:T(8,128)S(1)}, u32[]{:S(2)}, u32[]{:S(2)}) collective-permute-start(f32[1,72,128]{2,1,0:T(8,128)S(1)} %constant_dynamic-slice_fusion.own_ref), channel_id=1, source_target_pairs={{1,0},{2,1},{3,2},{4,3},{5,4},{6,5},{7,6},{8,7},{9,8},{10,9},{11,1... | collective-permute-start | bytes 110600 | tf_op jit(solution)/shard_map/ppermute | solution.py:537
  134.8 1.9 %collective-permute-start.2 = (f32[1,72,128]{2,1,0:T(8,128)S(1)}, f32[1,72,128]{2,1,0:T(8,128)S(1)}, u32[]{:S(2)}, u32[]{:S(2)}) collective-permute-start(f32[1,72,128]{2,1,0:T(8,128)S(1)} %constant_dynamic-slice_fusion.own_ref), channel_id=1, source_target_pairs={{0,1},{1,2},{2,3},{3,4},{4,5},{5,6},{6,7},{7,8},{8,9},{9,10},{10,1... | collective-permute-start | bytes 110600 | tf_op jit(solution)/shard_map/ppermute | solution.py:536
  136.7 0.0 collective-permute-done.3.high_ref
  136.7 4.2 %collective-permute-done.2.low_ref = f32[1,72,128]{2,1,0:T(8,128)S(1)} collective-permute-done((f32[1,72,128]{2,1,0:T(8,128)S(1)}, f32[1,72,128]{2,1,0:T(8,128)S(1)}, u32[]{:S(2)}, u32[]{:S(2)}) %collective-permute-start.2) | collective-permute-done | bytes 36896 | tf_op jit(solution)/shard_map/ppermute | solution.py:536
  141.0 0.0 copy-start.1
  141.0 2.2 %copy-done.1 = f32[1,1024,1024]{2,1,0:T(8,128)S(1)} copy-done((f32[1,1024,1024]{2,1,0:T(8,128)S(1)}, f32[1,1024,1024]{2,1,0:T(8,128)}, u32[]{:S(2)}) %copy-start.1) | copy-done | bytes 4194328
  143.2 0.0 copy-start.3
  143.2 1.1 copy-done.3
  144.3 0.0 copy-start.6
  144.3 1.0 copy-done.6
  145.3 3.2 %mask_update.1 = f32[1,1024,1024]{2,1,0:T(8,128)} custom-call(s32[1]{0:T(128)} %constant.25.clone.1.tile_ref, f32[1,1024,1024]{2,1,0:T(8,128)S(1)} %copy-done.1, f32[1,72,128]{2,1,0:T(8,128)S(1)} %constant_dynamic-slice_fusion.own_ref, f32[1,72,128]{2,1,0:T(8,128)S(1)} %collective-permute-done.2.low_ref, f32[1,72,128]{2,1,0:T(8,128)S(1)} %collective-permute-done.3.high_ref, ...), custom_call_target="tpu_custom_call" | custom-call | tf_op jit(solution)/shard_map/mask_update/pallas_call | solution.py:170
  (7 shorter events, 0.1 us)
Async XLA Ops:
  0.6 2.2 %copy-start = (f32[1,1024,1024]{2,1,0:T(8,128)S(1)}, f32[1,1024,1024]{2,1,0:T(8,128)}, u32[]{:S(2)}) copy-start(f32[1,1024,1024]{2,1,0:T(8,128)} %mask_ref.3) | copy-start | bytes 12582916
  2.8 1.0 copy-start.5
  3.9 1.0 copy-start.7
  4.8 0.9 copy-start.12
  5.7 0.9 copy-start.13
  6.6 32.5 %copy-start.22 = (f32[1,16384]{1,0:T(1,128)S(1)}, f32[1,16384]{1,0:T(1,128)}, u32[]{:S(2)}) copy-start(f32[1,16384]{1,0:T(1,128)} %param.23) | copy-start | bytes 196612
  6.6 39.2 %copy-start.23 = (s32[16,1]{0,1:T(1,128)S(1)}, s32[16,1]{0,1:T(1,128)}, u32[]{:S(2)}) copy-start(s32[16,1]{0,1:T(1,128)} %param.26) | copy-start | bytes 196
  6.7 64.3 %copy-start.2 = (f32[1,2,24,64,96]{4,3,2,1,0:T(8,128)S(1)}, f32[1,2,24,64,96]{4,3,2,1,0:T(8,128)}, u32[]{:S(2)}) copy-start(f32[1,2,24,64,96]{4,3,2,1,0:T(8,128)} %kern_ref.1) | copy-start | bytes 3538948
  6.7 64.3 %copy-start.8 = (bf16[512,256]{1,0:T(8,128)(2,1)S(1)}, bf16[512,256]{1,0:T(8,128)(2,1)}, u32[]{:S(2)}) copy-start(bf16[512,256]{1,0:T(8,128)(2,1)} %constant.58.clone.rim_t_ref) | copy-start | bytes 786436
  6.7 64.3 %copy-start.14 = (bf16[128,144]{1,0:T(8,128)(2,1)S(1)}, bf16[128,144]{1,0:T(8,128)(2,1)}, u32[]{:S(2)}) copy-start(bf16[128,144]{1,0:T(8,128)(2,1)} %constant.63.clone.pick_ref) | copy-start | bytes 110596
  6.7 64.3 %copy-start.21 = (f32[24]{0:T(128)S(1)}, f32[24]{0:T(128)}, u32[]{:S(2)}) copy-start(f32[24]{0:T(128)} %weight_ref.1) | copy-start | bytes 292
  9.8 4.7 %collective-permute-start = (f32[72,128]{1,0:T(8,128)S(1)}, f32[72,128]{1,0:T(8,128)S(1)}, u32[]{:S(2)}, u32[]{:S(2)}) collective-permute-start(f32[72,128]{1,0:T(8,128)S(1)} %get-tuple-element.6), channel_id=1, source_target_pairs={{1,0},{2,1},{3,2},{4,3},{5,4},{6,5},{7,6},{8,7},{9,8},{10,9},{11,1... | collective-permute-start | bytes 110600 | tf_op jit(solution)/shard_map/ppermute | solution.py:527
  12.6 6.2 %collective-permute-start.1 = (f32[72,128]{1,0:T(8,128)S(1)}, f32[72,128]{1,0:T(8,128)S(1)}, u32[]{:S(2)}, u32[]{:S(2)}) collective-permute-start(f32[72,128]{1,0:T(8,128)S(1)} %get-tuple-element.7), channel_id=1, source_target_pairs={{0,1},{1,2},{2,3},{3,4},{4,5},{5,6},{6,7},{7,8},{8,9},{9,10},{10,1... | collective-permute-start | bytes 110600 | tf_op jit(solution)/shard_map/ppermute | solution.py:528
  40.2 30.7 %all-to-all-start.1 = ((f32[16,128,128]{2,1,0:T(8,128)}), f32[16,128,128]{2,1,0:T(8,128)S(1)}, u32[]{:S(2)}, u32[]{:S(2)}) async-start(f32[16,128,128]{2,1,0:T(8,128)} %broadcast_in_dim.15), calls=%async_computation.1 | async-start | bytes 2097152 | tf_op jit(solution)/shard_map/all_to_all | solution.py:523
  71.0 1.0 copy-start.9
  72.0 0.9 copy-start.10
  72.9 0.9 copy-start.11
  73.9 0.8 copy-start.15
  74.7 0.8 copy-start.16
  75.5 0.8 copy-start.17
  76.4 0.8 copy-start.18
  77.2 0.8 copy-start.19
  77.9 0.7 copy-start.20
  111.2 0.8 copy-start.4
  112.0 19.9 %all-to-all-start.2 = ((f32[16,72,128]{2,1,0:T(8,128)}), f32[16,72,128]{2,1,0:T(8,128)S(1)}, u32[]{:S(2)}, u32[]{:S(2)}) async-start(f32[16,72,128]{2,1,0:T(8,128)} %copy-done.4), calls=%async_computation.2 | async-start | bytes 1179648 | tf_op jit(solution)/shard_map/all_to_all | solution.py:533
  132.0 4.8 %collective-permute-start.3 = (f32[1,72,128]{2,1,0:T(8,128)S(1)}, f32[1,72,128]{2,1,0:T(8,128)S(1)}, u32[]{:S(2)}, u32[]{:S(2)}) collective-permute-start(f32[1,72,128]{2,1,0:T(8,128)S(1)} %constant_dynamic-slice_fusion.own_ref), channel_id=1, source_target_pairs={{1,0},{2,1},{3,2},{4,3},{5,4},{6,5},{7,6},{8,7},{9,8},{10,9},{11,1... | collective-permute-start | bytes 110600 | tf_op jit(solution)/shard_map/ppermute | solution.py:537
  134.8 6.2 %collective-permute-start.2 = (f32[1,72,128]{2,1,0:T(8,128)S(1)}, f32[1,72,128]{2,1,0:T(8,128)S(1)}, u32[]{:S(2)}, u32[]{:S(2)}) collective-permute-start(f32[1,72,128]{2,1,0:T(8,128)S(1)} %constant_dynamic-slice_fusion.own_ref), channel_id=1, source_target_pairs={{0,1},{1,2},{2,3},{3,4},{4,5},{5,6},{6,7},{7,8},{8,9},{9,10},{10,1... | collective-permute-start | bytes 110600 | tf_op jit(solution)/shard_map/ppermute | solution.py:536
  141.0 2.2 %copy-start.1 = (f32[1,1024,1024]{2,1,0:T(8,128)S(1)}, f32[1,1024,1024]{2,1,0:T(8,128)}, u32[]{:S(2)}) copy-start(f32[1,1024,1024]{2,1,0:T(8,128)} %mask_ref.3) | copy-start | bytes 12582916
  143.2 1.1 copy-start.3
  144.3 1.0 copy-start.6
where the time goes:
time: 150 us; the launch traced here: 149 us
  waiting for transfers between devices  46.3 us (31%)
  Pallas kernels  38.9 us (26%)
  local copies, waits for them, and re-layouts  20.7 us (14%)
  blocking collectives  20.4 us (14%)
  starting transfers between devices  19.6 us (13%)
  between operations  2.71 us (2%)
    pallas_call x1, Pallas kernels, owner_imaging(): pl.pallas_call(imaging_kernel, in_specs=[smem, smem, smem] + [vmem] * (3...  32.5 us
    all_to_all x1, waiting for transfers between devices, spread(): return lax.all_to_all(wide, 'tile', 0, 0, tiled=True)  25.1 us
    all_to_all x1, blocking collectives, spread(): return lax.all_to_all(wide, 'tile', 0, 0, tiled=True)  20.4 us
    unnamed x49, local copies, waits for them, and re-layouts  18.9 us
    all_to_all x1, waiting for transfers between devices, on_device(): returned = lax.all_to_all(slopes, 'tile', 0, 0, tiled=True)  12.7 us
    all_to_all x1, starting transfers between devices, spread(): return lax.all_to_all(wide, 'tile', 0, 0, tiled=True)  5.57 us
    all_to_all x1, starting transfers between devices, on_device(): returned = lax.all_to_all(slopes, 'tile', 0, 0, tiled=True)  4.62 us
    ppermute x1, waiting for transfers between devices, on_device(): from_last = lax.ppermute(parts[2], 'tile', up)  4.24 us
  transfers between devices with their start and end apart: 6, of which 4 were waited for; matrix products, arithmetic and copies ran while one was open for 0% of the time, Pallas kernels for 0%

commit v1 on v0

v1 whole, which is shorter than its diff:
```python
import functools

import jax
import jax.numpy as jnp
import numpy as np
from jax import lax
from jax.experimental import pallas as pl
from jax.experimental.pallas import tpu as pltpu
from jax.sharding import PartitionSpec as P

AMBIT = 256
GRID_X = 192
GRID_Y = 128
CORE_X = 128
RESIST_SLOPE = 3.0
RESIST_LEVEL = 1.2
DIFFUSE_RATE = 0.2
STEP_SIZE = 1.0

LANES = 128
MOST = 2
BLOCKS = 4
BATCH = 6
ROWS = 72
ROWS_PAD = 80
F32 = jnp.float32
BF16 = jnp.bfloat16


def halves_np(table):
    table = np.asarray(table, np.float32)
    top = table.astype(BF16)
    rest = (table - top.astype(np.float32)).astype(BF16)
    return top, rest


def halves(value):
    top = value.astype(BF16)
    rest = (value - top.astype(F32)).astype(BF16)
    return top, rest


def mm(left, right):
    return jnp.dot(left, right, preferred_element_type=F32)


def in_hbm(value):
    return pltpu.with_memory_space_constraint(jnp.asarray(value), pltpu.HBM)


def real_waves(places, period, most, width):
    angles = 2.0 * np.pi * np.outer(places, np.arange(most + 1)) / period
    waves = np.concatenate([np.cos(angles), np.sin(angles[:, 1:])], axis=1)
    return np.pad(waves, ((0, 0), (0, width - waves.shape[1])))


def signed_picks(count, width):
    freqs = np.arange(count) - count // 2
    most = count // 2
    even = np.zeros((count, width))
    odd = np.zeros((count, width))
    for at, freq in enumerate(freqs):
        even[at, abs(freq)] = 1.0
        if freq != 0:
            odd[at, most + abs(freq)] = np.sign(freq)
    return even, odd


def mask_tables(tile_px, freq_y, freq_x):
    win = tile_px + 2 * AMBIT
    mid_x = (GRID_X - 1) / 2 * (win // GRID_X)
    mid_y = (GRID_Y - 1) / 2 * (tile_px // GRID_Y)
    cols = real_waves(np.arange(win) - mid_x, win, freq_x // 2, LANES)
    rows = real_waves(np.arange(tile_px) - mid_y, tile_px, freq_y // 2, ROWS_PAD)
    return cols, rows


def rim_marks(packet):
    row = lax.broadcasted_iota(jnp.int32, packet.shape, 0)
    lane = lax.broadcasted_iota(jnp.int32, packet.shape, 1)
    return lane, lax.rem(lane - row + LANES, packet.shape[0]) == 0


def packed(tall, used):
    body, line = tall[:-8], tall[-8:-7]
    rows = body.shape[0]
    lane, marked = rim_marks(body)
    line = jnp.where(marked & (lane < used), jnp.broadcast_to(line, body.shape), 0.0)
    one = jnp.sum(jnp.where(lane < rows, line, 0.0), axis=1, keepdims=True)
    two = jnp.sum(jnp.where(lane >= rows, line, 0.0), axis=1, keepdims=True)
    body = jnp.where(lane < used, body, 0.0)
    return jnp.where(lane == used, one, jnp.where(lane == used + 1, two, body))


def unpacked(packet, used):
    rows = packet.shape[0]
    lane, marked = rim_marks(packet)
    line = jnp.where(lane < rows, packet[:, used : used + 1], packet[:, used + 1 : used + 2])
    line = jnp.sum(jnp.where(marked & (lane < used), line, 0.0), axis=0, keepdims=True)
    body = jnp.where(lane < used, packet, 0.0)
    return jnp.concatenate([body, line, jnp.zeros((7, LANES), F32)], axis=0)


def fetch(pairs, sems):
    copies = [pltpu.make_async_copy(src, dst, sems.at[at]) for at, (src, dst) in enumerate(pairs)]
    for copy in copies:
        copy.start()
    return copies


def spectrum_kernel(used, me_ref, mask_hbm, cols_hbm, rows_hbm, out_ref, mask, cols, rows, total, sems):
    tile_px = mask.shape[0]
    block = tile_px // BLOCKS
    pairs = [(cols_hbm, cols), (rows_hbm, rows)]
    for at in range(BLOCKS):
        place = pl.ds(at * block, block)
        pairs.append((mask_hbm.at[0, place], mask.at[place]))
    copies = fetch(pairs, sems)
    copies[0].wait()
    copies[1].wait()

    def columns(top_part, rest_part, table):
        both = mm(top_part, table)
        return both[:, :LANES] + both[:, LANES:] + mm(rest_part, table[:, :LANES])

    for at in range(BLOCKS):
        copies[2 + at].wait()
        top, rest = halves(mask[at * block : (at + 1) * block])
        row_table = rows[:, at * block : (at + 1) * block]
        parts = (
            columns(top, rest, cols[AMBIT : AMBIT + tile_px]),
            columns(top[:, :AMBIT], rest[:, :AMBIT], cols[AMBIT + tile_px :]),
            columns(top[:, tile_px - AMBIT :], rest[:, tile_px - AMBIT :], cols[:AMBIT]),
        )
        for part, terms in enumerate(parts):
            piece = mm(row_table, jnp.concatenate(halves(terms), axis=1))
            if at == 0:
                total[part] = piece
            else:
                total[part] += piece

    def summed(part):
        whole = total[part]
        return packed(
            whole[:ROWS, :LANES] + whole[:ROWS, LANES:] + whole[ROWS_PAD : ROWS_PAD + ROWS, :LANES], used
        )

    odd = lax.rem(me_ref[0], 2) == 1
    low, high = summed(1), summed(2)
    out_ref[0] = summed(0)
    out_ref[1] = jnp.where(odd, high, low)
    out_ref[2] = jnp.where(odd, low, high)


def mask_spectrum(me, mask_tiles, cols, rows, freq_y, freq_x):
    tile_px = mask_tiles.shape[1]
    col_stack = np.concatenate(halves_np(cols), axis=1)
    row_stack = np.concatenate(halves_np(rows.T), axis=0)
    hbm = pl.BlockSpec(memory_space=pltpu.HBM)
    return pl.pallas_call(
        functools.partial(spectrum_kernel, freq_x + 1),
        in_specs=[pl.BlockSpec(memory_space=pltpu.SMEM), hbm, hbm, hbm],
        out_specs=pl.BlockSpec(memory_space=pltpu.VMEM),
        out_shape=jax.ShapeDtypeStruct((3, freq_y, LANES), F32),
        scratch_shapes=[
            pltpu.VMEM((tile_px, tile_px), F32),
            pltpu.VMEM(col_stack.shape, BF16),
            pltpu.VMEM(row_stack.shape, BF16),
            pltpu.VMEM((3, 2 * ROWS_PAD, 2 * LANES), F32),
            pltpu.SemaphoreType.DMA((2 + BLOCKS,)),
        ],
        compiler_params=pltpu.CompilerParams(vmem_limit_bytes=20 * 2**20),
        name="mask_spectrum",
    )(me, in_hbm(mask_tiles), in_hbm(col_stack), in_hbm(row_stack))


def slot_of(owner_ref, tile):
    owner = owner_ref[tile]

    def count(other, before):
        return before + ((owner_ref[other] == owner) & (other < tile)).astype(jnp.int32)

    return owner, lax.fori_loop(0, owner_ref.shape[0], count, jnp.int32(0))


def tiles_of(owner_ref, owner):
    def find(tile, carry):
        count, first, second = carry
        mine = owner_ref[tile] == owner
        first = jnp.where(mine & (count == 0), tile, first)
        second = jnp.where(mine & (count == 1), tile, second)
        return count + mine.astype(jnp.int32), first, second

    zero = jnp.int32(0)
    return lax.fori_loop(0, owner_ref.shape[0], find, (zero, zero, zero))


def mate_of(me):
    return me + 1 - 2 * lax.rem(me, 2)


def owner_pick_kernel(me_ref, owner_ref, packets_hbm, targets_hbm, out_ref, sems):
    _, first, second = tiles_of(owner_ref, mate_of(me_ref[0]))
    rows = packets_hbm.shape[1]
    pairs = []
    for slot, tile in enumerate((first, second)):
        pairs.append((packets_hbm.at[tile], out_ref.at[slot, pl.ds(0, rows)]))
        pairs.append((targets_hbm.at[tile], out_ref.at[slot, pl.ds(rows, targets_hbm.shape[1])]))
    for copy in fetch(pairs, sems):
        copy.wait()


def owner_pick(me, owner_list, packets, targets):
    smem = pl.BlockSpec(memory_space=pltpu.SMEM)
    vmem = pl.BlockSpec(memory_space=pltpu.VMEM)
    hbm = pl.BlockSpec(memory_space=pltpu.HBM)
    rows = packets.shape[1] + targets.shape[1]
    return pl.pallas_call(
        owner_pick_kernel,
        in_specs=[smem, smem, hbm, hbm],
        out_specs=vmem,
        out_shape=jax.ShapeDtypeStruct((MOST, rows, LANES), F32),
        scratch_shapes=[pltpu.SemaphoreType.DMA((2 * MOST,))],
        compiler_params=pltpu.CompilerParams(vmem_limit_bytes=2**20),
        name="owner_pick",
    )(me, owner_list, in_hbm(packets), in_hbm(targets))


def around(tile, tiles):
    return [
        (tile, None),
        (jnp.maximum(tile - 1, 0), tile > 0),
        (jnp.minimum(tile + 1, tiles - 1), tile < tiles - 1),
    ]


def tile_pick_kernel(me_ref, owner_ref, slopes_hbm, out_ref, sems):
    pairs = []
    for at, (tile, _) in enumerate(around(mate_of(me_ref[0]), owner_ref.shape[0])):
        owner, slot = slot_of(owner_ref, tile)
        pairs.append((slopes_hbm.at[owner, slot], out_ref.at[at]))
    for copy in fetch(pairs, sems):
        copy.wait()


def tile_pick(me, owner_list, slopes):
    smem = pl.BlockSpec(memory_space=pltpu.SMEM)
    vmem = pl.BlockSpec(memory_space=pltpu.VMEM)
    return pl.pallas_call(
        tile_pick_kernel,
        in_specs=[smem, smem, pl.BlockSpec(memory_space=pltpu.HBM)],
        out_specs=vmem,
        out_shape=jax.ShapeDtypeStruct((3,) + slopes.shape[2:], F32),
        scratch_shapes=[pltpu.SemaphoreType.DMA((3,))],
        compiler_params=pltpu.CompilerParams(vmem_limit_bytes=2**20),
        name="tile_pick",
    )(me, owner_list, in_hbm(slopes))


def joined(me, mine, other):
    odd = lax.rem(me, 2) == 1
    return jnp.concatenate([jnp.where(odd, other, mine), jnp.where(odd, mine, other)], axis=0)


def update_kernel(
    used, me_ref, owner_ref, slopes_hbm, other_ref, mask_hbm, cols_hbm, rows_hbm, out_hbm,
    mask, cols, rows, held, slopes, sems, out_sems, slope_sems,
):
    tile_px = mask.shape[0]
    block = tile_px // BLOCKS
    places = [pl.ds(at * block, block) for at in range(BLOCKS)]
    me = me_ref[0]
    near = around(me, owner_ref.shape[0])
    pairs = []
    for at, (tile, _) in enumerate(near):
        owner, slot = slot_of(owner_ref, tile)
        pairs.append((slopes_hbm.at[owner, slot], slopes.at[at]))
    slope_copies = fetch(pairs, slope_sems)
    copies = fetch(
        [(cols_hbm, cols), (rows_hbm, rows)]
        + [(mask_hbm.at[0, place], mask.at[place]) for place in places],
        sems,
    )
    packets = []
    for at, (_, there) in enumerate(near):
        slope_copies[at].wait()
        packet = unpacked(joined(me, slopes[at], other_ref[at]), used)
        packets.append(packet if there is None else jnp.where(there, packet, 0.0))
    copies[0].wait()

    def spread(packet, table):
        top, rest = halves(packet)
        return mm(
            jnp.concatenate([top, rest, top], axis=1),
            jnp.concatenate([table[:LANES], table[:LANES], table[LANES:]], axis=0),
        )

    wide = spread(packets[0], cols[:, AMBIT : AMBIT + tile_px])
    left = spread(packets[1], cols[:, AMBIT + tile_px :])
    right = spread(packets[2], cols[:, :AMBIT])
    wide = jnp.concatenate(
        [
            wide[:, :AMBIT] + left,
            wide[:, AMBIT : tile_px - AMBIT],
            wide[:, tile_px - AMBIT :] + right,
        ],
        axis=1,
    )
    wide = jnp.concatenate([wide, jnp.zeros((ROWS_PAD - ROWS, tile_px), F32)], axis=0)
    top, rest = halves(wide)
    held[:ROWS_PAD] = top
    held[ROWS_PAD : 2 * ROWS_PAD] = rest
    held[2 * ROWS_PAD :] = top
    copies[1].wait()
    sent = []
    for at, place in enumerate(places):
        copies[2 + at].wait()
        here = slice(at * block, (at + 1) * block)
        mask[here] = mask[here] - STEP_SIZE * mm(rows[here], held[...])
        copy = pltpu.make_async_copy(mask.at[place], out_hbm.at[0, place], out_sems.at[at])
        copy.start()
        sent.append(copy)
    for copy in sent:
        copy.wait()


def mask_update(me, owner_list, slopes, other, mask_tiles, cols, rows, freq_x):
    tile_px = mask_tiles.shape[1]
    col_stack = np.concatenate(halves_np(cols.T), axis=0)
    top, rest = halves_np(rows)
    row_stack = np.concatenate([top, top, rest], axis=1)
    smem = pl.BlockSpec(memory_space=pltpu.SMEM)
    vmem = pl.BlockSpec(memory_space=pltpu.VMEM)
    hbm = pl.BlockSpec(memory_space=pltpu.HBM)
    return pl.pallas_call(
        functools.partial(update_kernel, freq_x + 1),
        in_specs=[smem, smem, hbm, vmem, hbm, hbm, hbm],
        out_specs=hbm,
        out_shape=jax.ShapeDtypeStruct(mask_tiles.shape, F32),
        scratch_shapes=[
            pltpu.VMEM((tile_px, tile_px), F32),
            pltpu.VMEM(col_stack.shape, BF16),
            pltpu.VMEM(row_stack.shape, BF16),
            pltpu.VMEM((3 * ROWS_PAD, tile_px), BF16),
            pltpu.VMEM((3,) + slopes.shape[2:], F32),
            pltpu.SemaphoreType.DMA((2 + BLOCKS,)),
            pltpu.SemaphoreType.DMA((BLOCKS,)),
            pltpu.SemaphoreType.DMA((3,)),
        ],
        compiler_params=pltpu.CompilerParams(vmem_limit_bytes=20 * 2**20),
        name="mask_update",
    )(
        me, owner_list, in_hbm(slopes), other, in_hbm(mask_tiles), in_hbm(col_stack), in_hbm(row_stack)
    )


def image_tables(freq_y, freq_x):
    places_v = np.arange(GRID_X) - (GRID_X - 1) / 2
    freqs_b = np.arange(freq_x) - (freq_x - 1) / 2
    beta = 2.0 * np.pi * np.outer(freqs_b, places_v) / GRID_X
    first = (GRID_X - CORE_X) // 2

    def block(lane_of):
        table = np.zeros((2 * LANES, 2 * LANES))
        for place, lane in lane_of:
            table[:freq_x, lane] = np.cos(beta[:, place])
            table[:freq_x, LANES + lane] = np.sin(beta[:, place])
            table[LANES : LANES + freq_x, lane] = -np.sin(beta[:, place])
            table[LANES : LANES + freq_x, LANES + lane] = np.cos(beta[:, place])
        return table

    core = block([(first + lane, lane) for lane in range(CORE_X)])
    last = first + CORE_X
    rim = block(
        [(first - 2, LANES - 2), (first - 1, LANES - 1), (last, 0), (last + 1, 1)]
    )
    places_u = np.arange(GRID_Y // 2) + 0.5
    freqs_a = np.arange(freq_y) - (freq_y - 1) / 2
    alpha = 2.0 * np.pi * np.outer(places_u, freqs_a) / GRID_Y
    rows = np.concatenate([np.cos(alpha), np.sin(alpha)], axis=0)
    return core, rim, rows


def pick_tables(freq_y, freq_x):
    col_even, col_odd = signed_picks(freq_x, LANES)
    row_even, row_odd = signed_picks(freq_y, ROWS)
    lanes = np.zeros((LANES, 2 * LANES))
    lanes[:, :freq_x] = col_even.T
    lanes[:, LANES : LANES + freq_x] = col_odd.T
    rows = np.block([[row_even, -row_odd], [-row_odd, -row_even]])
    return lanes, rows


def imaging_kernel(
    places, used, me_ref, owner_ref, weight_ref, packets_hbm, targets_hbm, other_ref, kern_ref, table_ref,
    slopes_hbm, error_ref,
    spec, field, rim_field, rim_lanes, rim_slope, slope_acc, scale_ref, ready, packets, targets, sems, slot_sems,
):
    me = me_ref[0]
    kern_count, freq_y, freq_x = kern_ref.shape[2:]
    batch = max(size for size in range(1, BATCH + 1) if kern_count % size == 0)
    count, first, second = tiles_of(owner_ref, me)
    slots = (first, second)
    split = packets_hbm.shape[1]
    arrivals = fetch(
        [(packets_hbm.at[slots[slot]], packets.at[slot]) for slot in range(MOST)]
        + [(targets_hbm.at[slots[slot]], targets.at[slot]) for slot in range(MOST)],
        slot_sems,
    )
    for copy in arrivals:
        copy.wait()

    def table(name):
        start, height, width = places[name]
        return table_ref[start : start + height, :width]

    def pair(value):
        top, rest = halves(value)
        return jnp.concatenate([top, rest], axis=0)

    for slot in range(MOST):
        packet = joined(me, packets[slot], other_ref[slot, :split])
        packet = jnp.where(slot < count, unpacked(packet, used), 0.0)
        both = mm(pair(packet), table("lanes"))
        both = both[:ROWS] + both[ROWS:]
        tall = jnp.concatenate([both[:, :LANES], both[:, LANES:]], axis=0)
        top, rest = halves(tall)
        spec[slot] = mm(table("picks"), top) + mm(table("picks"), rest)

    half = GRID_Y // 2
    lane = lax.broadcasted_iota(jnp.int32, (freq_y, LANES), 1)
    live_lane = lane < freq_x

    def kern_at(k):
        def one(part):
            raw = kern_ref[0, part, k]
            wide = jnp.concatenate([raw, jnp.zeros((freq_y, LANES - freq_x), F32)], axis=1)
            return wide
        return one(0), one(1)

    def to_image(stack):
        top, rest = halves(stack)
        return mm(table("rows"), jnp.concatenate([top, rest, top], axis=0))

    def from_image(stack):
        top, rest = halves(stack)
        both = mm(table("rows_t"), jnp.concatenate([top, rest], axis=0))
        return both[:freq_y] + both[freq_y:]

    def thrice(top, rest, name):
        both = table(name)
        height = both.shape[0] // 2
        return mm(
            jnp.concatenate([top, rest, top], axis=1),
            jnp.concatenate([both[:height], both[:height], both[height:]], axis=0),
        )

    def waves(stack):
        even_re, even_im = stack[:half, :LANES], stack[:half, LANES:]
        odd_re, odd_im = stack[half:, :LANES], stack[half:, LANES:]
        return even_re - odd_im, even_im + odd_re, even_re + odd_im, even_im - odd_re

    def unwaves(plus_re, plus_im, minus_re, minus_im):
        above = jnp.concatenate([plus_re + minus_re, plus_im + minus_im], axis=1)
        below = jnp.concatenate([plus_im - minus_im, minus_re - plus_re], axis=1)
        return jnp.concatenate([above, below], axis=0)

    rim_lanes[...] = jnp.zeros_like(rim_lanes)

    def forward(group, sums):
        tops, rests = [], []
        for step in range(batch):
            kern_re, kern_im = kern_at(group * batch + step)
            for slot in range(2):
                spec_re, spec_im = spec[slot, :freq_y], spec[slot, freq_y:]
                wave = jnp.concatenate(
                    [kern_re * spec_re - kern_im * spec_im, kern_re * spec_im + kern_im * spec_re], axis=1
                )
                top, rest = halves(wave)
                tops.append(top)
                rests.append(rest)
        top, rest = jnp.concatenate(tops, axis=0), jnp.concatenate(rests, axis=0)
        cols = thrice(top, rest, "core")
        edges = thrice(top, rest, "rim")
        new = list(sums)
        for step in range(batch):
            k = group * batch + step
            weight = weight_ref[k]
            for slot in range(2):
                at = (2 * step + slot) * freq_y
                edge = edges[at : at + freq_y]
                rim_lanes[slot, :, :LANES] += pltpu.roll(edge[:, :LANES], 4 * k, 1)
                rim_lanes[slot, :, LANES:] += pltpu.roll(edge[:, LANES:], 4 * k, 1)
                parts = waves(to_image(cols[at : at + freq_y]))
                for part in range(4):
                    field[slot, k, part] = parts[part]
                plus, minus = new[slot]
                plus = plus + weight * (parts[0] * parts[0] + parts[1] * parts[1])
                minus = minus + weight * (parts[2] * parts[2] + parts[3] * parts[3])
                new[slot] = (plus, minus)
        return tuple(new)

    blank = jnp.zeros((half, LANES), F32)
    sums = lax.fori_loop(0, kern_count // batch, forward, ((blank, blank), (blank, blank)))

    def set_scale(k, carry):
        lane_row = lax.broadcasted_iota(jnp.int32, (1, LANES), 1)
        group = lax.rem(lane_row + 2, LANES) // 4
        return jnp.where(group == k, weight_ref[k], carry)

    lane_weight = lax.fori_loop(0, kern_count, set_scale, jnp.zeros((1, LANES), F32))

    norm = 1.0 / (64.0 * GRID_Y * GRID_X)
    square = norm * norm
    lane_half = lax.broadcasted_iota(jnp.int32, (half, LANES), 1)
    row_half = lax.broadcasted_iota(jnp.int32, (half, 2 * LANES), 0)
    lane_wide = lax.broadcasted_iota(jnp.int32, (half, 2 * LANES), 1)
    near = (lane_half < 2) | (lane_half >= LANES - 2)
    inside = lane_wide < LANES

    def blur(plus, minus):
        def one(value, other):
            later = jnp.where(row_half == half - 1, value, pltpu.roll(value, half - 1, 0))
            sooner = jnp.where(row_half == 0, other, pltpu.roll(value, 1, 0))
            sides = pltpu.roll(value, 1, 1) + pltpu.roll(value, 2 * LANES - 1, 1)
            return value + DIFFUSE_RATE * (later + sooner + sides - 4.0 * value)
        return one(plus, minus), one(minus, plus)

    def fold(value):
        def back(amount):
            return pltpu.roll(value, LANES - amount, 1)
        value = value + back(48)
        value = value + back(24)
        value = value + back(12)
        return value + back(4) + back(8)

    def unfold(value):
        value = jnp.where(near, value, 0.0)
        value = value + pltpu.roll(value, 4, 1) + pltpu.roll(value, 8, 1)
        value = value + pltpu.roll(value, 12, 1)
        value = value + pltpu.roll(value, 24, 1)
        return value + pltpu.roll(value, 48, 1)

    error = jnp.float32(0.0)
    for slot in range(2):
        live = (slot < count).astype(F32)
        rim_parts = waves(to_image(rim_lanes[slot]))
        for part in range(4):
            rim_field[part] = rim_parts[part]
        weights = jnp.broadcast_to(lane_weight, (half, LANES))
        rim_plus = weights * (rim_parts[0] * rim_parts[0] + rim_parts[1] * rim_parts[1])
        rim_minus = weights * (rim_parts[2] * rim_parts[2] + rim_parts[3] * rim_parts[3])
        plus = jnp.concatenate([sums[slot][0], jnp.where(near, fold(rim_plus), 0.0)], axis=1) * square
        minus = jnp.concatenate([sums[slot][1], jnp.where(near, fold(rim_minus), 0.0)], axis=1) * square
        plus, minus = blur(*blur(plus, minus))
        target = joined(me, targets[slot], other_ref[slot, split:])
        t_top = target[:half]
        one = t_top.astype(BF16)
        t_top = t_top - one.astype(F32)
        two = t_top.astype(BF16)
        three = (t_top - two.astype(F32)).astype(BF16)
        turned = mm(table("turn"), one) + mm(table("turn"), two) + mm(table("turn"), three)

        def slope_of(value, goal):
            resist = 1.0 / (1.0 + jnp.exp(-RESIST_SLOPE * (value[:, :LANES] - RESIST_LEVEL)))
            misfit = resist - goal
            slope = (2.0 * RESIST_SLOPE) * misfit * resist * (1.0 - resist)
            slope = jnp.concatenate([slope, jnp.zeros_like(slope)], axis=1)
            return slope, jnp.sum(misfit * misfit)

        slope_plus, err_plus = slope_of(plus, target[half:])
        slope_minus, err_minus = slope_of(minus, turned)
        error = error + live * (err_plus + err_minus)
        slope_plus, slope_minus = blur(*blur(slope_plus, slope_minus))
        factor = 2.0 * square
        scale_ref[slot, 0] = slope_plus[:, :LANES] * factor
        scale_ref[slot, 1] = slope_minus[:, :LANES] * factor
        rim_f_plus = unfold(slope_plus[:, LANES:] * factor) * weights
        rim_f_minus = unfold(slope_minus[:, LANES:] * factor) * weights
        rim_slope[slot] = from_image(
            unwaves(
                rim_f_plus * rim_field[0],
                rim_f_plus * rim_field[1],
                rim_f_minus * rim_field[2],
                rim_f_minus * rim_field[3],
            )
        )
    error_ref[0] = error * (1.0 / (GRID_Y * CORE_X))

    slope_acc[...] = jnp.zeros_like(slope_acc)
    rim_lane = (lane < 2) | (lane >= LANES - 2)

    def backward(group, carry):
        tops, rests, rim_tops, rim_rests = [], [], [], []
        for step in range(batch):
            k = group * batch + step
            weight = weight_ref[k]
            for slot in range(2):
                plus = scale_ref[slot, 0] * weight
                minus = scale_ref[slot, 1] * weight
                cols = from_image(
                    unwaves(
                        plus * field[slot, k, 0],
                        plus * field[slot, k, 1],
                        minus * field[slot, k, 2],
                        minus * field[slot, k, 3],
                    )
                )
                top, rest = halves(cols)
                tops.append(top)
                rests.append(rest)
                edge = jnp.concatenate(
                    [
                        pltpu.roll(rim_slope[slot, :, :LANES], LANES - 4 * k, 1),
                        pltpu.roll(rim_slope[slot, :, LANES:], LANES - 4 * k, 1),
                    ],
                    axis=1,
                )
                top, rest = halves(edge)
                rim_tops.append(top)
                rim_rests.append(rest)
        def stack(pieces):
            return jnp.concatenate(pieces, axis=0)
        waves_all = thrice(stack(tops), stack(rests), "core_t") + thrice(
            stack(rim_tops), stack(rim_rests), "rim_t"
        )
        sums = [[slope_acc[slot, :freq_y], slope_acc[slot, freq_y:]] for slot in range(2)]
        for step in range(batch):
            kern_re, kern_im = kern_at(group * batch + step)
            for slot in range(2):
                at = (2 * step + slot) * freq_y
                wave_re, wave_im = waves_all[at : at + freq_y, :LANES], waves_all[at : at + freq_y, LANES:]
                sums[slot][0] += wave_re * kern_re + wave_im * kern_im
                sums[slot][1] += wave_im * kern_re - wave_re * kern_im
        for slot in range(2):
            slope_acc[slot, :freq_y] = sums[slot][0]
            slope_acc[slot, freq_y:] = sums[slot][1]
        return carry

    lax.fori_loop(0, kern_count // batch, backward, 0)

    for slot in range(MOST):
        top, rest = halves(slope_acc[slot])
        tall = mm(table("picks_t"), top) + mm(table("picks_t"), rest)
        wide = jnp.concatenate([tall[:ROWS], tall[ROWS:]], axis=1)
        both = mm(pair(wide), table("lanes_t"))
        packet = packed(both[:ROWS] + both[ROWS:], used)
        ready[0, slot] = packet[:split]
        ready[1, slot] = packet[split:]
    tiles = slopes_hbm.shape[0]
    copies = fetch([(ready.at[tile % 2], slopes_hbm.at[tile]) for tile in range(tiles)], sems)
    for copy in copies:
        copy.wait()


def owner_imaging(me, owner_list, kern_weight, packets, targets, other, kernels):
    kern_count, freq_y, freq_x = kernels.shape[2:]
    tiles, split = packets.shape[:2]
    core, rim, rows = image_tables(freq_y, freq_x)
    lanes, picks = pick_tables(freq_y, freq_x)

    def tall(table):
        return np.concatenate(halves_np(table), axis=0)

    def three(table):
        top, rest = halves_np(table)
        return np.concatenate([top, top, rest], axis=1)

    def square_up(table):
        top, rest = halves_np(table)
        return np.block([[top, top], [rest, np.zeros_like(rest)]])

    tables = {
        "core": tall(core),
        "core_t": tall(core.T),
        "rim": tall(rim),
        "rim_t": tall(rim.T),
        "rows": three(rows),
        "rows_t": square_up(rows.T),
        "lanes": lanes.astype(BF16),
        "lanes_t": lanes.T.astype(BF16),
        "picks": picks.astype(BF16),
        "picks_t": picks.T.astype(BF16),
        "turn": np.eye(GRID_Y // 2)[::-1].astype(BF16),
    }
    places, pieces, start = {}, [], 0
    for name, piece in tables.items():
        height, width = piece.shape
        places[name] = (start, height, width)
        pieces.append(np.pad(piece, ((0, 0), (0, 2 * LANES - width))))
        start += height
    half = GRID_Y // 2
    smem = pl.BlockSpec(memory_space=pltpu.SMEM)
    vmem = pl.BlockSpec(memory_space=pltpu.VMEM)
    hbm = pl.BlockSpec(memory_space=pltpu.HBM)
    return pl.pallas_call(
        functools.partial(imaging_kernel, places, freq_x + 1),
        in_specs=[smem, smem, smem, hbm, hbm] + [vmem] * 3,
        out_specs=(hbm, smem),
        out_shape=(
            jax.ShapeDtypeStruct((tiles, MOST, split, LANES), F32),
            jax.ShapeDtypeStruct((1,), F32),
        ),
        scratch_shapes=[
            pltpu.VMEM((MOST, 2 * freq_y, LANES), F32),
            pltpu.VMEM((MOST, kern_count, 4, half, LANES), F32),
            pltpu.VMEM((4, half, LANES), F32),
            pltpu.VMEM((MOST, freq_y, 2 * LANES), F32),
            pltpu.VMEM((MOST, freq_y, 2 * LANES), F32),
            pltpu.VMEM((MOST, 2 * freq_y, LANES), F32),
            pltpu.VMEM((MOST, 2, half, LANES), F32),
            pltpu.VMEM((2, MOST, split, LANES), F32),
            pltpu.VMEM((MOST,) + packets.shape[1:], F32),
            pltpu.VMEM((MOST,) + targets.shape[1:], F32),
            pltpu.SemaphoreType.DMA((tiles,)),
            pltpu.SemaphoreType.DMA((2 * MOST,)),
        ],
        compiler_params=pltpu.CompilerParams(vmem_limit_bytes=20 * 2**20),
        name="owner_imaging",
    )(
        me, owner_list, kern_weight, in_hbm(packets), in_hbm(targets), other, kernels,
        jnp.asarray(np.concatenate(pieces, axis=0)),
    )


def on_device(mask_tiles, target_grid, kernels, kern_weight, owner_list):
    tile_px = mask_tiles.shape[1]
    freq_y, freq_x = kernels.shape[3:]
    count = lax.axis_size("tile")
    cols, rows = mask_tables(tile_px, freq_y, freq_x)
    me = lax.axis_index("tile").astype(jnp.int32).reshape(1)
    mates = [(i, i + 1 - 2 * (i % 2)) for i in range(count)]
    seams = [(i, i - 1 + 2 * (i % 2)) for i in range(1, count - 1)]

    def spread(value):
        value = value.reshape(1, 2, -1, LANES)
        wide = jnp.broadcast_to(value, (count // 2,) + value.shape[1:])
        return lax.all_to_all(wide.reshape(count, -1, LANES), "tile", 0, 0, tiled=True)

    owner_list = owner_list.reshape(-1)
    targets = spread(target_grid)
    parts = mask_spectrum(me, mask_tiles, cols, rows, freq_y, freq_x)
    from_seam = lax.ppermute(parts[1], "tile", seams)
    from_mate = lax.ppermute(parts[2], "tile", mates)
    packet, targets = lax.optimization_barrier((parts[0] + from_seam + from_mate, targets))
    packets = spread(packet)
    other = lax.ppermute(owner_pick(me, owner_list, packets, targets), "tile", mates)
    slopes, owner_error = owner_imaging(me, owner_list, kern_weight, packets, targets, other, kernels)
    slopes = lax.all_to_all(slopes, "tile", 0, 0, tiled=True)
    other = lax.ppermute(tile_pick(me, owner_list, slopes), "tile", mates)
    current = mask_update(me, owner_list, slopes, other, mask_tiles, cols, rows, freq_x)
    return (current, owner_error)


def solution(mesh):
    placed = (
        P(("stripe", "tile"), None, None),
        P(("stripe", "tile"), None),
        P("tile", None, None, None, None),
        P(),
        P("stripe", None),
    )
    return jax.shard_map(
        on_device,
        mesh=mesh,
        in_specs=placed,
        out_specs=(P(("stripe", "tile"), None, None), P(("stripe", "tile"))),
        check_vma=False,
    )
```

time: 150 us -> 84.1 us (0.56)
  the two profiles are of different devices: /device:TPU:18 before, /device:TPU:0 now
where the time goes in v1:
time: 84.1 us; the launch traced here: 83.5 us
  blocking collectives  31.8 us (38%)
  Pallas kernels  29.2 us (35%)
  starting transfers between devices  11.8 us (14%)
  waiting for transfers between devices  8.25 us (10%)
  local copies, waits for them, and re-layouts  1.73 us (2%)
    all_to_all x1, blocking collectives, on_device(): slopes = lax.all_to_all(slopes, 'tile', 0, 0, tiled=True)  17.7 us
    pallas_call x1, Pallas kernels, owner_imaging(): pl.pallas_call(functools.partial(imaging_kernel, places, freq_x + 1), in_...  14.9 us
    all_to_all x1, blocking collectives, spread(): lax.all_to_all(wide.reshape(count, -1, LANES), 'tile', 0, 0, tiled=True)  14.1 us
    all_to_all x1, starting transfers between devices, spread(): lax.all_to_all(wide.reshape(count, -1, LANES), 'tile', 0, 0, tiled=True)  7.7 us
    pallas_call x1, Pallas kernels, mask_update(): pl.pallas_call(functools.partial(update_kernel, freq_x + 1), in_specs=[sm...  6.28 us
    all_to_all x1, waiting for transfers between devices, spread(): lax.all_to_all(wide.reshape(count, -1, LANES), 'tile', 0, 0, tiled=True)  4.93 us
    pallas_call x1, Pallas kernels, mask_spectrum(): pl.pallas_call(functools.partial(spectrum_kernel, freq_x + 1), in_specs=[...  4.74 us
    ppermute x1, starting transfers between devices, on_device(): from_mate = lax.ppermute(parts[2], 'tile', mates)  3.29 us
  transfers between devices with their start and end apart: 5, of which 4 were waited for; matrix products, arithmetic and copies ran while one was open for 0% of the time, Pallas kernels for 6%

profile of v1, /device:TPU:0, one launch (start us, length us, event | category | flops | bytes accessed | tf_op | source)
XLA Modules:
  0.0 83.5 jit_solution(12929190241501075578)
XLA Ops:
  0.6 0.0 copy-start.2
  0.6 1.7 %broadcast_in_dim.15 = f32[8,2,64,128]{3,2,1,0:T(8,128)} broadcast(f32[2,64,128]{2,1,0:T(8,128)} %bitcast.23), dimensions={1,2,3} | broadcast | bytes 589824 | tf_op jit(solution)/shard_map/broadcast_in_dim | solution.py:737
  2.3 0.0 copy-start
  2.3 0.0 copy-start.1
  2.3 0.0 copy-start.3
  2.3 7.7 %all-to-all-start = ((f32[16,64,128]{2,1,0:T(8,128)}), f32[16,64,128]{2,1,0:T(8,128)}, u32[]{:S(2)}, u32[]{:S(2)}) async-start(f32[16,64,128]{2,1,0:T(8,128)} %bitcast.20), calls=%async_computation | async-start | bytes 1048576 | tf_op jit(solution)/shard_map/all_to_all | solution.py:738
  10.0 4.7 %mask_spectrum.1 = f32[3,64,128]{2,1,0:T(8,128)S(1)} custom-call(s32[1]{0:T(128)} %bitcast.me_ref, f32[1,1024,1024]{2,1,0:T(8,128)} %mask_hbm.3, bf16[1536,256]{1,0:T(8,128)(2,1)} %constant.14.clone.cols_hbm, bf16[160,1024]{1,0:T(8,128)(2,1)} %constant.15.clone.rows_hbm), custom_call_target="tpu_custom_call" | custom-call | tf_op jit(solution)/shard_map/mask_spectrum/pallas_call | solution.py:160
  14.8 0.7 collective-permute-start
  15.5 3.3 %collective-permute-start.1 = (f32[64,128]{1,0:T(8,128)S(1)}, f32[64,128]{1,0:T(8,128)S(1)}, u32[]{:S(2)}, u32[]{:S(2)}) collective-permute-start(f32[64,128]{1,0:T(8,128)S(1)} %get-tuple-element.11), channel_id=1, source_target_pairs={{0,1},{1,0},{2,3},{3,2},{4,5},{5,4},{6,7},{7,6},{8,9},{9,8},{10,11... | collective-permute-start | bytes 98312 | tf_op jit(solution)/shard_map/ppermute | solution.py:744
  18.8 0.0 collective-permute-done
  18.8 0.9 %collective-permute-done.1 = f32[64,128]{1,0:T(8,128)S(1)} collective-permute-done((f32[64,128]{1,0:T(8,128)S(1)}, f32[64,128]{1,0:T(8,128)S(1)}, u32[]{:S(2)}, u32[]{:S(2)}) %collective-permute-start.1) | collective-permute-done | bytes 32800 | tf_op jit(solution)/shard_map/ppermute | solution.py:744
  19.6 4.9 %all-to-all-done.targets_hbm = f32[16,64,128]{2,1,0:T(8,128)} async-done(((f32[16,64,128]{2,1,0:T(8,128)}), f32[16,64,128]{2,1,0:T(8,128)}, u32[]{:S(2)}, u32[]{:S(2)}) %all-to-all-start) | async-done | bytes 524320 | tf_op jit(solution)/shard_map/all_to_all | solution.py:738
  24.6 14.1 %all_to_all.15.packets_hbm = f32[16,32,128]{2,1,0:T(8,128)} all-to-all(f32[16,32,128]{2,1,0:T(8,128)S(1)} %bitcast.21), channel_id=1, replica_groups=mesh['stripe'=2,'tile'=16] {'tile'}, dimensions={0} | all-to-all | bytes 524288 | tf_op jit(solution)/shard_map/all_to_all | solution.py:738
  38.6 0.0 copy-done.2
  38.6 1.6 %owner_pick.1 = f32[2,96,128]{2,1,0:T(8,128)S(1)} custom-call(s32[1]{0:T(128)} %bitcast.me_ref, s32[16]{0:T(128)S(1)} %bitcast.16, f32[16,32,128]{2,1,0:T(8,128)} %all_to_all.15.packets_hbm, f32[16,64,128]{2,1,0:T(8,128)} %all-to-all-done.targets_hbm), custom_call_target="tpu_custom_call" | custom-call | tf_op jit(solution)/shard_map/owner_pick/pallas_call | solution.py:218
  40.2 0.1 collective-permute-start.2
  40.3 1.3 %collective-permute-done.2.other_ref = f32[2,96,128]{2,1,0:T(8,128)S(1)} collective-permute-done((f32[2,96,128]{2,1,0:T(8,128)S(1)}, f32[2,96,128]{2,1,0:T(8,128)S(1)}, u32[]{:S(2)}, u32[]{:S(2)}) %collective-permute-start.2) | collective-permute-done | bytes 98336 | tf_op jit(solution)/shard_map/ppermute | solution.py:747
  41.6 0.0 copy-done
  41.6 0.0 copy-done.1
  41.6 0.0 copy-done.3
  41.6 14.9 %owner_imaging.1 = (f32[16,2,32,128]{3,2,1,0:T(8,128)S(1)}, f32[1]{0:T(128)}) custom-call(s32[1]{0:T(128)} %bitcast.me_ref, s32[16]{0:T(128)S(1)} %bitcast.17, f32[24]{0:T(128)S(1)} %copy-done.3, f32[16,32,128]{2,1,0:T(8,128)} %all_to_all.15.packets_hbm, f32[16,64,128]{2,1,0:T(8,128)} %all-to-all-done.targets_hbm, ...), custom_call_target="tpu_custom_call" | custom-call | tf_op jit(solution)/shard_map/owner_imaging/pallas_call | solution.py:696
  56.5 17.7 %all_to_all.16.slopes_hbm = f32[16,2,32,128]{3,2,1,0:T(8,128)} all-to-all(f32[16,2,32,128]{3,2,1,0:T(8,128)S(1)} %get-tuple-element.8), channel_id=1, replica_groups=mesh['stripe'=2,'tile'=16] {'tile'}, dimensions={0} | all-to-all | bytes 1048576 | tf_op jit(solution)/shard_map/all_to_all | solution.py:749
  74.3 1.7 %tile_pick.1 = f32[3,32,128]{2,1,0:T(8,128)S(1)} custom-call(s32[1]{0:T(128)} %bitcast.me_ref, s32[16]{0:T(128)S(1)} %bitcast.18, f32[16,2,32,128]{3,2,1,0:T(8,128)} %all_to_all.16.slopes_hbm), custom_call_target="tpu_custom_call" | custom-call | tf_op jit(solution)/shard_map/tile_pick/pallas_call | solution.py:249
  75.9 0.1 collective-permute-start.3
  76.1 1.2 %collective-permute-done.3.other_ref = f32[3,32,128]{2,1,0:T(8,128)S(1)} collective-permute-done((f32[3,32,128]{2,1,0:T(8,128)S(1)}, f32[3,32,128]{2,1,0:T(8,128)S(1)}, u32[]{:S(2)}, u32[]{:S(2)}) %collective-permute-start.3) | collective-permute-done | bytes 49184 | tf_op jit(solution)/shard_map/ppermute | solution.py:750
  77.2 6.3 %mask_update.1 = f32[1,1024,1024]{2,1,0:T(8,128)} custom-call(s32[1]{0:T(128)} %bitcast.me_ref, s32[16]{0:T(128)S(1)} %bitcast.19, f32[16,2,32,128]{3,2,1,0:T(8,128)} %all_to_all.16.slopes_hbm, f32[3,32,128]{2,1,0:T(8,128)S(1)} %collective-permute-done.3.other_ref, f32[1,1024,1024]{2,1,0:T(8,128)} %mask_hbm.3, bf16[256,1536]{1,0:T(8,128)(2,1)} %constant.17.clone.cols_hbm, ...), custom_call_target="tpu_custom_call" | custom-call | tf_op jit(solution)/shard_map/mask_update/pallas_call | solution.py:335
  (3 shorter events, 0.0 us)
Async XLA Ops:
  0.6 38.0 %copy-start.2 = (s32[16,1]{0,1:T(1,128)S(1)}, s32[16,1]{0,1:T(1,128)}, u32[]{:S(2)}) copy-start(s32[16,1]{0,1:T(1,128)} %param.14) | copy-start | bytes 196
  2.3 39.3 %copy-start = (f32[1,2,24,64,96]{4,3,2,1,0:T(8,128)S(1)}, f32[1,2,24,64,96]{4,3,2,1,0:T(8,128)}, u32[]{:S(2)}) copy-start(f32[1,2,24,64,96]{4,3,2,1,0:T(8,128)} %kern_ref.1) | copy-start | bytes 3538948
  2.3 39.3 %copy-start.1 = (bf16[3024,256]{1,0:T(8,128)(2,1)S(1)}, bf16[3024,256]{1,0:T(8,128)(2,1)}, u32[]{:S(2)}) copy-start(bf16[3024,256]{1,0:T(8,128)(2,1)} %constant.16.clone.table_ref) | copy-start | bytes 4644868
  2.3 39.3 %copy-start.3 = (f32[24]{0:T(128)S(1)}, f32[24]{0:T(128)}, u32[]{:S(2)}) copy-start(f32[24]{0:T(128)} %weight_ref.1) | copy-start | bytes 292
  2.3 22.2 %all-to-all-start = ((f32[16,64,128]{2,1,0:T(8,128)}), f32[16,64,128]{2,1,0:T(8,128)}, u32[]{:S(2)}, u32[]{:S(2)}) async-start(f32[16,64,128]{2,1,0:T(8,128)} %bitcast.20), calls=%async_computation | async-start | bytes 1048576 | tf_op jit(solution)/shard_map/all_to_all | solution.py:738
  14.8 4.0 %collective-permute-start = (f32[64,128]{1,0:T(8,128)S(1)}, f32[64,128]{1,0:T(8,128)S(1)}, u32[]{:S(2)}, u32[]{:S(2)}) collective-permute-start(f32[64,128]{1,0:T(8,128)S(1)} %get-tuple-element.10), channel_id=1, source_target_pairs={{1,2},{2,1},{3,4},{4,3},{5,6},{6,5},{7,8},{8,7},{9,10},{10,9},{11,... | collective-permute-start | bytes 98312 | tf_op jit(solution)/shard_map/ppermute | solution.py:743
  15.5 4.2 %collective-permute-start.1 = (f32[64,128]{1,0:T(8,128)S(1)}, f32[64,128]{1,0:T(8,128)S(1)}, u32[]{:S(2)}, u32[]{:S(2)}) collective-permute-start(f32[64,128]{1,0:T(8,128)S(1)} %get-tuple-element.11), channel_id=1, source_target_pairs={{0,1},{1,0},{2,3},{3,2},{4,5},{5,4},{6,7},{7,6},{8,9},{9,8},{10,11... | collective-permute-start | bytes 98312 | tf_op jit(solution)/shard_map/ppermute | solution.py:744
  40.2 1.4 %collective-permute-start.2 = (f32[2,96,128]{2,1,0:T(8,128)S(1)}, f32[2,96,128]{2,1,0:T(8,128)S(1)}, u32[]{:S(2)}, u32[]{:S(2)}) collective-permute-start(f32[2,96,128]{2,1,0:T(8,128)S(1)} %owner_pick.1), channel_id=1, source_target_pairs={{0,1},{1,0},{2,3},{3,2},{4,5},{5,4},{6,7},{7,6},{8,9},{9,8},{10,11... | collective-permute-start | bytes 294920 | tf_op jit(solution)/shard_map/ppermute | solution.py:747
  75.9 1.3 %collective-permute-start.3 = (f32[3,32,128]{2,1,0:T(8,128)S(1)}, f32[3,32,128]{2,1,0:T(8,128)S(1)}, u32[]{:S(2)}, u32[]{:S(2)}) collective-permute-start(f32[3,32,128]{2,1,0:T(8,128)S(1)} %tile_pick.1), channel_id=1, source_target_pairs={{0,1},{1,0},{2,3},{3,2},{4,5},{5,4},{6,7},{7,6},{8,9},{9,8},{10,11... | collective-permute-start | bytes 147464 | tf_op jit(solution)/shard_map/ppermute | solution.py:750

commit v2 on v1

--- a/solution.py
+++ b/solution.py
@@ -20,6 +20,7 @@
 LANES = 128
 MOST = 2
 BLOCKS = 4
+PIECES = 16
 BATCH = 6
 ROWS = 72
 ROWS_PAD = 80
@@ -46,6 +47,10 @@
 
 def in_hbm(value):
     return pltpu.with_memory_space_constraint(jnp.asarray(value), pltpu.HBM)
+
+
+def in_vmem(value):
+    return pltpu.with_memory_space_constraint(jnp.asarray(value), pltpu.VMEM)
 
 
 def real_waves(places, period, most, width):
@@ -108,7 +113,7 @@
     return copies
 
 
-def spectrum_kernel(used, me_ref, mask_hbm, cols_hbm, rows_hbm, out_ref, mask, cols, rows, total, sems):
+def spectrum_kernel(used, mask_hbm, cols_hbm, rows_hbm, target_hbm, out_ref, mask, cols, rows, total, sems, target_sems):
     tile_px = mask.shape[0]
     block = tile_px // BLOCKS
     pairs = [(cols_hbm, cols), (rows_hbm, rows)]
@@ -116,6 +121,11 @@
         place = pl.ds(at * block, block)
         pairs.append((mask_hbm.at[0, place], mask.at[place]))
     copies = fetch(pairs, sems)
+    size = target_hbm.shape[0] // PIECES
+    goals = fetch(
+        [(target_hbm.at[pl.ds(at * size, size)], out_ref.at[at, pl.ds(16, size)]) for at in range(PIECES)],
+        target_sems,
+    )
     copies[0].wait()
     copies[1].wait()
 
@@ -145,42 +155,49 @@
             whole[:ROWS, :LANES] + whole[:ROWS, LANES:] + whole[ROWS_PAD : ROWS_PAD + ROWS, :LANES], used
         )
 
-    odd = lax.rem(me_ref[0], 2) == 1
-    low, high = summed(1), summed(2)
-    out_ref[0] = summed(0)
-    out_ref[1] = jnp.where(odd, high, low)
-    out_ref[2] = jnp.where(odd, low, high)
-
-
-def mask_spectrum(me, mask_tiles, cols, rows, freq_y, freq_x):
+    for part in range(3):
+        packet = summed(part)
+        for at in range(PIECES):
+            out_ref[at, 4 * part : 4 * part + 4] = packet[4 * at : 4 * at + 4]
+    for copy in goals:
+        copy.wait()
+
+
+def mask_spectrum(mask_tiles, target, cols, rows, freq_x):
     tile_px = mask_tiles.shape[1]
     col_stack = np.concatenate(halves_np(cols), axis=1)
     row_stack = np.concatenate(halves_np(rows.T), axis=0)
     hbm = pl.BlockSpec(memory_space=pltpu.HBM)
     return pl.pallas_call(
         functools.partial(spectrum_kernel, freq_x + 1),
-        in_specs=[pl.BlockSpec(memory_space=pltpu.SMEM), hbm, hbm, hbm],
+        in_specs=[hbm, hbm, hbm, hbm],
         out_specs=pl.BlockSpec(memory_space=pltpu.VMEM),
-        out_shape=jax.ShapeDtypeStruct((3, freq_y, LANES), F32),
+        out_shape=jax.ShapeDtypeStruct((PIECES, 24, LANES), F32),
         scratch_shapes=[
             pltpu.VMEM((tile_px, tile_px), F32),
             pltpu.VMEM(col_stack.shape, BF16),
             pltpu.VMEM(row_stack.shape, BF16),
             pltpu.VMEM((3, 2 * ROWS_PAD, 2 * LANES), F32),
             pltpu.SemaphoreType.DMA((2 + BLOCKS,)),
+            pltpu.SemaphoreType.DMA((PIECES,)),
         ],
         compiler_params=pltpu.CompilerParams(vmem_limit_bytes=20 * 2**20),
         name="mask_spectrum",
-    )(me, in_hbm(mask_tiles), in_hbm(col_stack), in_hbm(row_stack))
-
-
-def slot_of(owner_ref, tile):
-    owner = owner_ref[tile]
+    )(in_hbm(mask_tiles), in_hbm(col_stack), in_hbm(row_stack), in_hbm(target))
+
+
+def slots_of(owner_ref, tiles):
+    owners = [owner_ref[tile] for tile in tiles]
 
     def count(other, before):
-        return before + ((owner_ref[other] == owner) & (other < tile)).astype(jnp.int32)
-
-    return owner, lax.fori_loop(0, owner_ref.shape[0], count, jnp.int32(0))
+        held = owner_ref[other]
+        return tuple(
+            seen + ((held == owner) & (other < tile)).astype(jnp.int32)
+            for seen, owner, tile in zip(before, owners, tiles)
+        )
+
+    ranks = lax.fori_loop(0, owner_ref.shape[0], count, (jnp.int32(0),) * len(tiles))
+    return list(zip(owners, ranks))
 
 
 def tiles_of(owner_ref, owner):
@@ -199,31 +216,65 @@
     return me + 1 - 2 * lax.rem(me, 2)
 
 
-def owner_pick_kernel(me_ref, owner_ref, packets_hbm, targets_hbm, out_ref, sems):
-    _, first, second = tiles_of(owner_ref, mate_of(me_ref[0]))
-    rows = packets_hbm.shape[1]
-    pairs = []
-    for slot, tile in enumerate((first, second)):
-        pairs.append((packets_hbm.at[tile], out_ref.at[slot, pl.ds(0, rows)]))
-        pairs.append((targets_hbm.at[tile], out_ref.at[slot, pl.ds(rows, targets_hbm.shape[1])]))
-    for copy in fetch(pairs, sems):
-        copy.wait()
-
-
-def owner_pick(me, owner_list, packets, targets):
+def route_kernel(me_ref, owner_ref, pieces_ref, *rest):
+    edges_ref = rest[0] if len(rest) == 3 else None
+    out_ref, seen = rest[-2:]
+    tiles = owner_ref.shape[0]
+    base = me_ref[0] // PIECES * PIECES
+
+    def clear(at, carry):
+        seen[at] = 0
+        return carry
+
+    lax.fori_loop(0, tiles, clear, 0)
+
+    def send(tile, carry):
+        owner = owner_ref[tile]
+        slot = seen[owner]
+        seen[owner] = slot + 1
+        at = tile - base
+
+        @pl.when((at >= 0) & (at < PIECES))
+        def _():
+            high = pieces_ref[jnp.maximum(at - 1, 0), 8:12]
+            low = pieces_ref[jnp.minimum(at + 1, PIECES - 1), 4:8]
+            if edges_ref is None:
+                edge_high, edge_low = jnp.zeros_like(high), jnp.zeros_like(low)
+            else:
+                edge_high, edge_low = edges_ref[0, 8:12], edges_ref[1, 4:8]
+            high = jnp.where(at > 0, high, edge_high)
+            low = jnp.where(at < PIECES - 1, low, edge_low)
+            packet = pieces_ref[at, :4] + high + low
+
+            @pl.when(slot == 0)
+            def _():
+                out_ref[owner, :4] = packet
+                out_ref[owner, 8:16] = pieces_ref[at, 16:]
+
+            @pl.when(slot == 1)
+            def _():
+                out_ref[owner, 4:8] = packet
+                out_ref[owner, 16:] = pieces_ref[at, 16:]
+
+        return carry
+
+    lax.fori_loop(0, tiles, send, 0)
+
+
+def route(me, owner_list, pieces, edges):
     smem = pl.BlockSpec(memory_space=pltpu.SMEM)
     vmem = pl.BlockSpec(memory_space=pltpu.VMEM)
-    hbm = pl.BlockSpec(memory_space=pltpu.HBM)
-    rows = packets.shape[1] + targets.shape[1]
+    tiles = owner_list.shape[0]
+    extra = [] if edges is None else [edges]
     return pl.pallas_call(
-        owner_pick_kernel,
-        in_specs=[smem, smem, hbm, hbm],
+        route_kernel,
+        in_specs=[smem, smem, vmem] + [vmem] * len(extra),
         out_specs=vmem,
-        out_shape=jax.ShapeDtypeStruct((MOST, rows, LANES), F32),
-        scratch_shapes=[pltpu.SemaphoreType.DMA((2 * MOST,))],
+        out_shape=jax.ShapeDtypeStruct((tiles, 24, LANES), F32),
+        scratch_shapes=[pltpu.SMEM((tiles,), jnp.int32)],
         compiler_params=pltpu.CompilerParams(vmem_limit_bytes=2**20),
-        name="owner_pick",
-    )(me, owner_list, in_hbm(packets), in_hbm(targets))
+        name="route",
+    )(me, owner_list, in_vmem(pieces), *extra)
 
 
 def around(tile, tiles):
@@ -234,13 +285,10 @@
     ]
 
 
-def tile_pick_kernel(me_ref, owner_ref, slopes_hbm, out_ref, sems):
-    pairs = []
-    for at, (tile, _) in enumerate(around(mate_of(me_ref[0]), owner_ref.shape[0])):
-        owner, slot = slot_of(owner_ref, tile)
-        pairs.append((slopes_hbm.at[owner, slot], out_ref.at[at]))
-    for copy in fetch(pairs, sems):
-        copy.wait()
+def tile_pick_kernel(me_ref, owner_ref, slopes_ref, out_ref):
+    tiles = [tile for tile, _ in around(mate_of(me_ref[0]), owner_ref.shape[0])]
+    for at, (owner, slot) in enumerate(slots_of(owner_ref, tiles)):
+        out_ref[at] = slopes_ref[owner, slot]
 
 
 def tile_pick(me, owner_list, slopes):
@@ -248,13 +296,12 @@
     vmem = pl.BlockSpec(memory_space=pltpu.VMEM)
     return pl.pallas_call(
         tile_pick_kernel,
-        in_specs=[smem, smem, pl.BlockSpec(memory_space=pltpu.HBM)],
+        in_specs=[smem, smem, vmem],
         out_specs=vmem,
         out_shape=jax.ShapeDtypeStruct((3,) + slopes.shape[2:], F32),
-        scratch_shapes=[pltpu.SemaphoreType.DMA((3,))],
         compiler_params=pltpu.CompilerParams(vmem_limit_bytes=2**20),
         name="tile_pick",
-    )(me, owner_list, in_hbm(slopes))
+    )(me, owner_list, in_vmem(slopes))
 
 
 def joined(me, mine, other):
@@ -263,30 +310,17 @@
 
 
 def update_kernel(
-    used, me_ref, owner_ref, slopes_hbm, other_ref, mask_hbm, cols_hbm, rows_hbm, out_hbm,
-    mask, cols, rows, held, slopes, sems, out_sems, slope_sems,
+    used, me_ref, owner_ref, slopes_ref, other_ref, mask_ref, cols, rows, out_hbm, out, held, out_sems
 ):
-    tile_px = mask.shape[0]
+    tile_px = out.shape[0]
     block = tile_px // BLOCKS
-    places = [pl.ds(at * block, block) for at in range(BLOCKS)]
     me = me_ref[0]
     near = around(me, owner_ref.shape[0])
-    pairs = []
-    for at, (tile, _) in enumerate(near):
-        owner, slot = slot_of(owner_ref, tile)
-        pairs.append((slopes_hbm.at[owner, slot], slopes.at[at]))
-    slope_copies = fetch(pairs, slope_sems)
-    copies = fetch(
-        [(cols_hbm, cols), (rows_hbm, rows)]
-        + [(mask_hbm.at[0, place], mask.at[place]) for place in places],
-        sems,
-    )
     packets = []
-    for at, (_, there) in enumerate(near):
-        slope_copies[at].wait()
-        packet = unpacked(joined(me, slopes[at], other_ref[at]), used)
+    for at, (owner, slot) in enumerate(slots_of(owner_ref, [tile for tile, _ in near])):
+        packet = unpacked(joined(me, slopes_ref[owner, slot], other_ref[at]), used)
+        there = near[at][1]
         packets.append(packet if there is None else jnp.where(there, packet, 0.0))
-    copies[0].wait()
 
     def spread(packet, table):
         top, rest = halves(packet)
@@ -311,13 +345,12 @@
     held[:ROWS_PAD] = top
     held[ROWS_PAD : 2 * ROWS_PAD] = rest
     held[2 * ROWS_PAD :] = top
-    copies[1].wait()
     sent = []
-    for at, place in enumerate(places):
-        copies[2 + at].wait()
+    for at in range(BLOCKS):
         here = slice(at * block, (at + 1) * block)
-        mask[here] = mask[here] - STEP_SIZE * mm(rows[here], held[...])
-        copy = pltpu.make_async_copy(mask.at[place], out_hbm.at[0, place], out_sems.at[at])
+        place = pl.ds(at * block, block)
+        out[here] = mask_ref[0, here] - STEP_SIZE * mm(rows[here], held[...])
+        copy = pltpu.make_async_copy(out.at[place], out_hbm.at[0, place], out_sems.at[at])
         copy.start()
         sent.append(copy)
     for copy in sent:
@@ -334,23 +367,18 @@
     hbm = pl.BlockSpec(memory_space=pltpu.HBM)
     return pl.pallas_call(
         functools.partial(update_kernel, freq_x + 1),
-        in_specs=[smem, smem, hbm, vmem, hbm, hbm, hbm],
+        in_specs=[smem, smem] + [vmem] * 5,
         out_specs=hbm,
         out_shape=jax.ShapeDtypeStruct(mask_tiles.shape, F32),
         scratch_shapes=[
             pltpu.VMEM((tile_px, tile_px), F32),
-            pltpu.VMEM(col_stack.shape, BF16),
-            pltpu.VMEM(row_stack.shape, BF16),
             pltpu.VMEM((3 * ROWS_PAD, tile_px), BF16),
-            pltpu.VMEM((3,) + slopes.shape[2:], F32),
-            pltpu.SemaphoreType.DMA((2 + BLOCKS,)),
             pltpu.SemaphoreType.DMA((BLOCKS,)),
-            pltpu.SemaphoreType.DMA((3,)),
         ],
-        compiler_params=pltpu.CompilerParams(vmem_limit_bytes=20 * 2**20),
+        compiler_params=pltpu.CompilerParams(vmem_limit_bytes=16 * 2**20),
         name="mask_update",
     )(
-        me, owner_list, in_hbm(slopes), other, in_hbm(mask_tiles), in_hbm(col_stack), in_hbm(row_stack)
+        me, owner_list, in_vmem(slopes), other, in_vmem(mask_tiles), in_vmem(col_stack), in_vmem(row_stack)
     )
 
 
@@ -392,23 +420,17 @@
 
 
 def imaging_kernel(
-    places, used, me_ref, owner_ref, weight_ref, packets_hbm, targets_hbm, other_ref, kern_ref, table_ref,
+    places, used, me_ref, owner_ref, weight_ref, pieces_ref, kern_ref, table_ref,
     slopes_hbm, error_ref,
-    spec, field, rim_field, rim_lanes, rim_slope, slope_acc, scale_ref, ready, packets, targets, sems, slot_sems,
+    spec, field, rim_field, rim_lanes, rim_slope, slope_acc, scale_ref, ready, sems,
 ):
     me = me_ref[0]
     kern_count, freq_y, freq_x = kern_ref.shape[2:]
     batch = max(size for size in range(1, BATCH + 1) if kern_count % size == 0)
     count, first, second = tiles_of(owner_ref, me)
     slots = (first, second)
-    split = packets_hbm.shape[1]
-    arrivals = fetch(
-        [(packets_hbm.at[slots[slot]], packets.at[slot]) for slot in range(MOST)]
-        + [(targets_hbm.at[slots[slot]], targets.at[slot]) for slot in range(MOST)],
-        slot_sems,
-    )
-    for copy in arrivals:
-        copy.wait()
+    split = freq_y // 2
+    firsts = [slot // PIECES * PIECES for slot in slots]
 
     def table(name):
         start, height, width = places[name]
@@ -419,7 +441,9 @@
         return jnp.concatenate([top, rest], axis=0)
 
     for slot in range(MOST):
-        packet = joined(me, packets[slot], other_ref[slot, :split])
+        packet = jnp.concatenate(
+            [pieces_ref[firsts[slot] + at, 4 * slot : 4 * slot + 4] for at in range(PIECES)], axis=0
+        )
         packet = jnp.where(slot < count, unpacked(packet, used), 0.0)
         both = mm(pair(packet), table("lanes"))
         both = both[:ROWS] + both[ROWS:]
@@ -553,7 +577,10 @@
         plus = jnp.concatenate([sums[slot][0], jnp.where(near, fold(rim_plus), 0.0)], axis=1) * square
         minus = jnp.concatenate([sums[slot][1], jnp.where(near, fold(rim_minus), 0.0)], axis=1) * square
         plus, minus = blur(*blur(plus, minus))
-        target = joined(me, targets[slot], other_ref[slot, split:])
+        target = jnp.concatenate(
+            [pieces_ref[firsts[slot] + at, 8 + 8 * slot : 16 + 8 * slot] for at in range(PIECES)], axis=0
+        )
+        target = jnp.where(slot < count, target, 0.0)
         t_top = target[:half]
         one = t_top.astype(BF16)
         t_top = t_top - one.astype(F32)
@@ -653,9 +680,9 @@
         copy.wait()
 
 
-def owner_imaging(me, owner_list, kern_weight, packets, targets, other, kernels):
+def owner_imaging(me, owner_list, kern_weight, pieces, kernels):
     kern_count, freq_y, freq_x = kernels.shape[2:]
-    tiles, split = packets.shape[:2]
+    tiles, split = owner_list.shape[0], freq_y // 2
     core, rim, rows = image_tables(freq_y, freq_x)
     lanes, picks = pick_tables(freq_y, freq_x)
 
@@ -683,11 +710,11 @@
         "picks_t": picks.T.astype(BF16),
         "turn": np.eye(GRID_Y // 2)[::-1].astype(BF16),
     }
-    places, pieces, start = {}, [], 0
+    places, stacked, start = {}, [], 0
     for name, piece in tables.items():
         height, width = piece.shape
         places[name] = (start, height, width)
-        pieces.append(np.pad(piece, ((0, 0), (0, 2 * LANES - width))))
+        stacked.append(np.pad(piece, ((0, 0), (0, 2 * LANES - width))))
         start += height
     half = GRID_Y // 2
     smem = pl.BlockSpec(memory_space=pltpu.SMEM)
@@ -695,7 +722,7 @@
     hbm = pl.BlockSpec(memory_space=pltpu.HBM)
     return pl.pallas_call(
         functools.partial(imaging_kernel, places, freq_x + 1),
-        in_specs=[smem, smem, smem, hbm, hbm] + [vmem] * 3,
+        in_specs=[smem, smem, smem] + [vmem] * 3,
         out_specs=(hbm, smem),
         out_shape=(
             jax.ShapeDtypeStruct((tiles, MOST, split, LANES), F32),
@@ -710,16 +737,13 @@
             pltpu.VMEM((MOST, 2 * freq_y, LANES), F32),
             pltpu.VMEM((MOST, 2, half, LANES), F32),
             pltpu.VMEM((2, MOST, split, LANES), F32),
-            pltpu.VMEM((MOST,) + packets.shape[1:], F32),
-            pltpu.VMEM((MOST,) + targets.shape[1:], F32),
             pltpu.SemaphoreType.DMA((tiles,)),
-            pltpu.SemaphoreType.DMA((2 * MOST,)),
         ],
         compiler_params=pltpu.CompilerParams(vmem_limit_bytes=20 * 2**20),
         name="owner_imaging",
     )(
-        me, owner_list, kern_weight, in_hbm(packets), in_hbm(targets), other, kernels,
-        jnp.asarray(np.concatenate(pieces, axis=0)),
+        me, owner_list, kern_weight, in_vmem(pieces), in_vmem(kernels),
+        in_vmem(np.concatenate(stacked, axis=0)),
     )
 
 
@@ -729,23 +753,22 @@
     count = lax.axis_size("tile")
     cols, rows = mask_tables(tile_px, freq_y, freq_x)
     me = lax.axis_index("tile").astype(jnp.int32).reshape(1)
+    owner_list = owner_list.reshape(-1)
     mates = [(i, i + 1 - 2 * (i % 2)) for i in range(count)]
-    seams = [(i, i - 1 + 2 * (i % 2)) for i in range(1, count - 1)]
-
-    def spread(value):
-        value = value.reshape(1, 2, -1, LANES)
-        wide = jnp.broadcast_to(value, (count // 2,) + value.shape[1:])
-        return lax.all_to_all(wide.reshape(count, -1, LANES), "tile", 0, 0, tiled=True)
-
-    owner_list = owner_list.reshape(-1)
-    targets = spread(target_grid)
-    parts = mask_spectrum(me, mask_tiles, cols, rows, freq_y, freq_x)
-    from_seam = lax.ppermute(parts[1], "tile", seams)
-    from_mate = lax.ppermute(parts[2], "tile", mates)
-    packet, targets = lax.optimization_barrier((parts[0] + from_seam + from_mate, targets))
-    packets = spread(packet)
-    other = lax.ppermute(owner_pick(me, owner_list, packets, targets), "tile", mates)
-    slopes, owner_error = owner_imaging(me, owner_list, kern_weight, packets, targets, other, kernels)
+
+    pieces = mask_spectrum(mask_tiles, target_grid.reshape(GRID_Y, CORE_X), cols, rows, freq_x)
+    if count == PIECES:
+        pieces, edges = lax.all_to_all(pieces, "tile", 0, 0, tiled=True), None
+    else:
+        groups = [list(range(at, at + PIECES)) for at in range(0, count, PIECES)]
+        pieces = lax.all_to_all(pieces, "tile", 0, 0, axis_index_groups=groups, tiled=True)
+        later = [(i, i + PIECES) for i in range(count - PIECES)]
+        sooner = [(i + PIECES, i) for i in range(count - PIECES)]
+        edges = jnp.stack(
+            [lax.ppermute(pieces[PIECES - 1], "tile", later), lax.ppermute(pieces[0], "tile", sooner)]
+        )
+    pieces = lax.all_to_all(route(me, owner_list, pieces, edges), "tile", 0, 0, tiled=True)
+    slopes, owner_error = owner_imaging(me, owner_list, kern_weight, pieces, kernels)
     slopes = lax.all_to_all(slopes, "tile", 0, 0, tiled=True)
     other = lax.ppermute(tile_pick(me, owner_list, slopes), "tile", mates)
     current = mask_update(me, owner_list, slopes, other, mask_tiles, cols, rows, freq_x)

time: 84.1 us -> 72.5 us (0.86)
  starting transfers between devices: 11.8 us -> 7.46 us
  Pallas kernels: 29.2 us -> 25 us
  blocking collectives: 31.8 us -> 28.8 us
  waiting for transfers between devices: 8.25 us -> 10.2 us
  local copies, waits for them, and re-layouts: 1.73 us -> 0.03 us
    all_to_all x1, waiting for transfers between devices: 4.93 us -> 8.99 us  [on_device(): pieces, edges = (lax.all_to_all(pieces, 'tile', 0, 0, tiled=True), None)]
    ppermute x3 -> x0, starting transfers between devices: 4.02 us -> none  [the longest x1 3.29 us: on_device(): from_mate = lax.ppermute(parts[2], 'tile', mates)]
    pallas_call x1, Pallas kernels: 6.28 us -> 3.49 us  [mask_update(): pl.pallas_call(functools.partial(update_kernel, freq_x + 1), in_specs=[sm...]
    all_to_all x1, blocking collectives: 14.1 us -> 11.7 us  [on_device(): lax.all_to_all(route(me, owner_list, pieces, edges), 'tile', 0, 0, tiled=...]
    ppermute x3 -> x0, waiting for transfers between devices: 2.15 us -> none  [the longest x1 1.29 us: on_device(): lax.ppermute(owner_pick(me, owner_list, packets, targets), 'tile', mates)]
    broadcast_in_dim x2 -> x0, local copies, waits for them, and re-layouts: 1.71 us -> none  [spread(): wide = jnp.broadcast_to(value, (count // 2,) + value.shape[1:])]
    pallas_call x2, Pallas kernels: 3.25 us -> 1.76 us  [the longest x1 1.05 us: route(): pl.pallas_call(route_kernel, in_specs=[smem, smem, vmem] + [vmem] * len(e...]
    pallas_call x1, Pallas kernels: 4.74 us -> 5.82 us  [mask_spectrum(): pl.pallas_call(functools.partial(spectrum_kernel, freq_x + 1), in_specs=[...]
  transfers between devices with their start and end apart: 5 -> 2, of which waited for: 4 -> 2; matrix products, arithmetic and copies ran while one was open for 0% -> 0% of each run, Pallas kernels for 6% -> 0%
where the time goes in v2:
time: 72.5 us; the launch traced here: 72.2 us
  blocking collectives  28.8 us (40%)
  Pallas kernels  25 us (34%)
  waiting for transfers between devices  10.2 us (14%)
  starting transfers between devices  7.46 us (10%)
    all_to_all x1, blocking collectives, on_device(): slopes = lax.all_to_all(slopes, 'tile', 0, 0, tiled=True)  17.1 us
    pallas_call x1, Pallas kernels, owner_imaging(): pl.pallas_call(functools.partial(imaging_kernel, places, freq_x + 1), in_...  13.9 us
    all_to_all x1, blocking collectives, on_device(): lax.all_to_all(route(me, owner_list, pieces, edges), 'tile', 0, 0, tiled=...  11.7 us
    all_to_all x1, waiting for transfers between devices, on_device(): pieces, edges = (lax.all_to_all(pieces, 'tile', 0, 0, tiled=True), None)  8.99 us
    all_to_all x1, starting transfers between devices, on_device(): pieces, edges = (lax.all_to_all(pieces, 'tile', 0, 0, tiled=True), None)  7.38 us
    pallas_call x1, Pallas kernels, mask_spectrum(): pl.pallas_call(functools.partial(spectrum_kernel, freq_x + 1), in_specs=[...  5.82 us
    pallas_call x1, Pallas kernels, mask_update(): pl.pallas_call(functools.partial(update_kernel, freq_x + 1), in_specs=[sm...  3.49 us
  transfers between devices with their start and end apart: 2, of which 2 were waited for; matrix products, arithmetic and copies ran while one was open for 0% of the time, Pallas kernels for 0%

profile of v2, /device:TPU:0, one launch (start us, length us, event | category | flops | bytes accessed | tf_op | source)
XLA Modules:
  0.0 72.2 jit_solution(10216110690820972392)
XLA Ops:
  0.6 0.0 copy-start.2
  0.6 0.0 copy-start.5
  0.7 0.0 copy-start.6
  0.7 0.0 copy-start.1
  0.7 5.8 %mask_spectrum.1 = f32[16,24,128]{2,1,0:T(8,128)} custom-call(f32[1,1024,1024]{2,1,0:T(8,128)} %mask_ref.1, bf16[1536,256]{1,0:T(8,128)(2,1)} %constant.14.clone.cols_hbm, bf16[160,1024]{1,0:T(8,128)(2,1)} %constant.15.clone.rows_hbm, f32[128,128]{1,0:T(8,128)} %bitcast.7), custom_call_target="tpu_custom_call" | custom-call | tf_op jit(solution)/shard_map/mask_spectrum/pallas_call | solution.py:171
  6.5 7.4 %all-to-all-start = ((f32[16,24,128]{2,1,0:T(8,128)}), f32[16,24,128]{2,1,0:T(8,128)S(1)}, u32[]{:S(2)}, u32[]{:S(2)}) async-start(f32[16,24,128]{2,1,0:T(8,128)} %mask_spectrum.1), calls=%async_computation | async-start | bytes 393216 | tf_op jit(solution)/shard_map/all_to_all | solution.py:761
  13.9 9.0 %all-to-all-done.pieces_ref = f32[16,24,128]{2,1,0:T(8,128)S(1)} async-done(((f32[16,24,128]{2,1,0:T(8,128)}), f32[16,24,128]{2,1,0:T(8,128)S(1)}, u32[]{:S(2)}, u32[]{:S(2)}) %all-to-all-start) | async-done | bytes 196640 | tf_op jit(solution)/shard_map/all_to_all | solution.py:761
  22.9 0.0 copy-start
  22.9 0.0 copy-start.3
  22.9 0.0 copy-start.4
  22.9 0.0 copy-done.5
  22.9 1.0 %route.1 = f32[16,24,128]{2,1,0:T(8,128)S(1)} custom-call(s32[1]{0:T(128)} %bitcast.me_ref, s32[16]{0:T(128)S(1)} %bitcast.3, f32[16,24,128]{2,1,0:T(8,128)S(1)} %all-to-all-done.pieces_ref), custom_call_target="tpu_custom_call" | custom-call | tf_op jit(solution)/shard_map/route/pallas_call | solution.py:269
  24.0 11.7 %all_to_all.15.pieces_ref = f32[16,24,128]{2,1,0:T(8,128)S(1)} all-to-all(f32[16,24,128]{2,1,0:T(8,128)S(1)} %route.1), channel_id=1, replica_groups=mesh['stripe'=2,'tile'=16] {'tile'}, dimensions={0} | all-to-all | bytes 393216 | tf_op jit(solution)/shard_map/all_to_all | solution.py:770
  35.7 0.0 copy-done.2
  35.7 0.0 copy-done.6
  35.7 0.0 copy-done.1
  35.7 13.9 %owner_imaging.1 = (f32[16,2,32,128]{3,2,1,0:T(8,128)S(1)}, f32[1]{0:T(128)}) custom-call(s32[1]{0:T(128)} %bitcast.me_ref, s32[16]{0:T(128)S(1)} %bitcast.4, f32[24]{0:T(128)S(1)} %copy-done.6, f32[16,24,128]{2,1,0:T(8,128)S(1)} %all_to_all.15.pieces_ref, f32[1,2,24,64,96]{4,3,2,1,0:T(8,128)S(1)} %copy-done.1, bf16[3024,256]{1,0:T(8,128)(2,1)S(1)} %copy-done.2), custom_call_target="tpu_custom_call" | custom-call | tf_op jit(solution)/shard_map/owner_imaging/pallas_call | solution.py:723
  49.6 17.1 %all_to_all.16.slopes_ref = f32[16,2,32,128]{3,2,1,0:T(8,128)S(1)} all-to-all(f32[16,2,32,128]{3,2,1,0:T(8,128)S(1)} %get-tuple-element.4), channel_id=1, replica_groups=mesh['stripe'=2,'tile'=16] {'tile'}, dimensions={0} | all-to-all | bytes 1048576 | tf_op jit(solution)/shard_map/all_to_all | solution.py:772
  66.7 0.7 tile_pick.1
  67.4 0.1 collective-permute-start
  67.5 1.2 %collective-permute-done.other_ref = f32[3,32,128]{2,1,0:T(8,128)S(1)} collective-permute-done((f32[3,32,128]{2,1,0:T(8,128)S(1)}, f32[3,32,128]{2,1,0:T(8,128)S(1)}, u32[]{:S(2)}, u32[]{:S(2)}) %collective-permute-start) | collective-permute-done | bytes 49184 | tf_op jit(solution)/shard_map/ppermute | solution.py:773
  68.7 0.0 copy-done
  68.7 0.0 copy-done.3
  68.7 0.0 copy-done.4
  68.7 3.5 %mask_update.1 = f32[1,1024,1024]{2,1,0:T(8,128)} custom-call(s32[1]{0:T(128)} %bitcast.me_ref, s32[16]{0:T(128)S(1)} %bitcast.6, f32[16,2,32,128]{3,2,1,0:T(8,128)S(1)} %all_to_all.16.slopes_ref, f32[3,32,128]{2,1,0:T(8,128)S(1)} %collective-permute-done.other_ref, f32[1,1024,1024]{2,1,0:T(8,128)S(1)} %copy-done, bf16[256,1536]{1,0:T(8,128)(2,1)S(1)} %copy-done.3, ...), custom_call_target="tpu_custom_call" | custom-call | tf_op jit(solution)/shard_map/mask_update/pallas_call | solution.py:368
Async XLA Ops:
  0.6 35.0 %copy-start.2 = (bf16[3024,256]{1,0:T(8,128)(2,1)S(1)}, bf16[3024,256]{1,0:T(8,128)(2,1)}, u32[]{:S(2)}) copy-start(bf16[3024,256]{1,0:T(8,128)(2,1)} %constant.16.clone.table_ref) | copy-start | bytes 4644868
  0.6 22.2 %copy-start.5 = (s32[16,1]{0,1:T(1,128)S(1)}, s32[16,1]{0,1:T(1,128)}, u32[]{:S(2)}) copy-start(s32[16,1]{0,1:T(1,128)} %param.14) | copy-start | bytes 196
  0.7 35.0 %copy-start.6 = (f32[24]{0:T(128)S(1)}, f32[24]{0:T(128)}, u32[]{:S(2)}) copy-start(f32[24]{0:T(128)} %weight_ref.1) | copy-start | bytes 292
  0.7 35.0 %copy-start.1 = (f32[1,2,24,64,96]{4,3,2,1,0:T(8,128)S(1)}, f32[1,2,24,64,96]{4,3,2,1,0:T(8,128)}, u32[]{:S(2)}) copy-start(f32[1,2,24,64,96]{4,3,2,1,0:T(8,128)} %kern_ref.1) | copy-start | bytes 3538948
  6.5 16.4 %all-to-all-start = ((f32[16,24,128]{2,1,0:T(8,128)}), f32[16,24,128]{2,1,0:T(8,128)S(1)}, u32[]{:S(2)}, u32[]{:S(2)}) async-start(f32[16,24,128]{2,1,0:T(8,128)} %mask_spectrum.1), calls=%async_computation | async-start | bytes 393216 | tf_op jit(solution)/shard_map/all_to_all | solution.py:761
  22.9 45.8 %copy-start = (f32[1,1024,1024]{2,1,0:T(8,128)S(1)}, f32[1,1024,1024]{2,1,0:T(8,128)}, u32[]{:S(2)}) copy-start(f32[1,1024,1024]{2,1,0:T(8,128)} %mask_ref.1) | copy-start | bytes 12582916
  22.9 45.8 %copy-start.3 = (bf16[256,1536]{1,0:T(8,128)(2,1)S(1)}, bf16[256,1536]{1,0:T(8,128)(2,1)}, u32[]{:S(2)}) copy-start(bf16[256,1536]{1,0:T(8,128)(2,1)} %constant.17.clone.cols) | copy-start | bytes 2359300
  22.9 45.8 %copy-start.4 = (bf16[1024,240]{1,0:T(8,128)(2,1)S(1)}, bf16[1024,240]{1,0:T(8,128)(2,1)}, u32[]{:S(2)}) copy-start(bf16[1024,240]{1,0:T(8,128)(2,1)} %constant.18.clone.rows) | copy-start | bytes 1474564
  67.4 1.3 %collective-permute-start = (f32[3,32,128]{2,1,0:T(8,128)S(1)}, f32[3,32,128]{2,1,0:T(8,128)S(1)}, u32[]{:S(2)}, u32[]{:S(2)}) collective-permute-start(f32[3,32,128]{2,1,0:T(8,128)S(1)} %tile_pick.1), channel_id=1, source_target_pairs={{0,1},{1,0},{2,3},{3,2},{4,5},{5,4},{6,7},{7,6},{8,9},{9,8},{10,11... | collective-permute-start | bytes 147464 | tf_op jit(solution)/shard_map/ppermute | solution.py:773

commit v3 on v2

v3 whole, which is shorter than its diff:
```python
import functools

import jax
import jax.numpy as jnp
import numpy as np
from jax import lax
from jax.experimental import pallas as pl
from jax.experimental.pallas import tpu as pltpu
from jax.sharding import PartitionSpec as P

AMBIT = 256
GRID_X = 192
GRID_Y = 128
CORE_X = 128
RESIST_SLOPE = 3.0
RESIST_LEVEL = 1.2
DIFFUSE_RATE = 0.2
STEP_SIZE = 1.0

LANES = 128
MOST = 2
BLOCKS = 4
PIECES = 16
BATCH = 12
WIDE = 8
RIM_WIDTH = 16
RIM_KERNS = LANES // RIM_WIDTH
ROWS = 72
ROWS_PAD = 80
F32 = jnp.float32
BF16 = jnp.bfloat16


def halves_np(table):
    table = np.asarray(table, np.float32)
    top = table.astype(BF16)
    rest = (table - top.astype(np.float32)).astype(BF16)
    return top, rest


def halves(value):
    top = value.astype(BF16)
    rest = (value - top.astype(F32)).astype(BF16)
    return top, rest


def mm(left, right):
    return jnp.dot(left, right, preferred_element_type=F32)


def in_hbm(value):
    return pltpu.with_memory_space_constraint(jnp.asarray(value), pltpu.HBM)


def in_vmem(value):
    return pltpu.with_memory_space_constraint(jnp.asarray(value), pltpu.VMEM)


def real_waves(places, period, most, width):
    angles = 2.0 * np.pi * np.outer(places, np.arange(most + 1)) / period
    waves = np.concatenate([np.cos(angles), np.sin(angles[:, 1:])], axis=1)
    return np.pad(waves, ((0, 0), (0, width - waves.shape[1])))


def signed_picks(count, width):
    freqs = np.arange(count) - count // 2
    most = count // 2
    even = np.zeros((count, width))
    odd = np.zeros((count, width))
    for at, freq in enumerate(freqs):
        even[at, abs(freq)] = 1.0
        if freq != 0:
            odd[at, most + abs(freq)] = np.sign(freq)
    return even, odd


def mask_tables(tile_px, freq_y, freq_x):
    win = tile_px + 2 * AMBIT
    mid_x = (GRID_X - 1) / 2 * (win // GRID_X)
    mid_y = (GRID_Y - 1) / 2 * (tile_px // GRID_Y)
    most = freq_x // 2
    cols = real_waves(np.arange(AMBIT), win, most, LANES)
    rows = real_waves(np.arange(tile_px) - mid_y, tile_px, freq_y // 2, ROWS_PAD)
    blocks = win // AMBIT
    angles = 2.0 * np.pi * np.outer(AMBIT * np.arange(blocks) - mid_x, np.arange(most + 1)) / win
    turns = np.zeros((2, blocks, LANES))
    turns[0, :, : most + 1] = np.cos(angles)
    turns[0, :, most + 1 : 2 * most + 1] = np.cos(angles[:, 1:])
    turns[1, :, : most + 1] = -np.sin(angles)
    turns[1, :, most + 1 : 2 * most + 1] = np.sin(angles[:, 1:])
    return cols, turns.astype(np.float32).reshape(2 * blocks, 1, LANES), rows


def swapped(value, used):
    lane = lax.broadcasted_iota(jnp.int32, value.shape, 1)
    most = (used - 1) // 2
    return jnp.where(lane <= most, pltpu.roll(value, LANES - most, 1), pltpu.roll(value, most, 1))


def packed(tall, used):
    rows = tall.shape[0] - 8
    body, line = tall[:rows], jnp.broadcast_to(tall[rows : rows + 1], (8, LANES))
    lane = lax.broadcasted_iota(jnp.int32, (8, LANES), 1)
    row = lax.broadcasted_iota(jnp.int32, (8, LANES), 0)
    spare = LANES - used
    first = jnp.where(lane < used, body[:8], 0.0)
    for at in range(-(-used // spare)):
        moved = pltpu.roll(line, (used - spare * at) % LANES, 1)
        first = jnp.where((row == at) & (lane >= used), moved, first)
    return jnp.concatenate([first, body[8:]], axis=0)


def unpacked(packet, used):
    lane = lax.broadcasted_iota(jnp.int32, packet.shape, 1)
    first = packet[:8]
    lane8 = lane[:8]
    row = lax.broadcasted_iota(jnp.int32, (8, LANES), 0)
    spare = LANES - used
    line = jnp.zeros((8, LANES), F32)
    for at in range(-(-used // spare)):
        moved = pltpu.roll(first, (spare * at - used) % LANES, 1)
        here = (row == at) & (lane8 >= spare * at) & (lane8 < min(spare * at + spare, used))
        line = line + jnp.where(here, moved, 0.0)
    line = jnp.where(row == 0, jnp.sum(line, axis=0, keepdims=True), 0.0)
    return jnp.concatenate([jnp.where(lane < used, packet, 0.0), line], axis=0)


def own_place():
    return lax.axis_index("tile").astype(jnp.int32)


def fetch(pairs, sems):
    copies = [pltpu.make_async_copy(src, dst, sems.at[at]) for at, (src, dst) in enumerate(pairs)]
    for copy in copies:
        copy.start()
    return copies


def spectrum_kernel(
    used, mask_hbm, cols_hbm, turns_hbm, rows_hbm, target_hbm, out_ref, mask, cols, turns, rows, sems, target_sems
):
    tile_px = mask.shape[0]
    width = AMBIT
    count = tile_px // width
    pairs = [(rows_hbm, rows)]
    for at in range(count):
        place = pl.ds(at * width, width)
        pairs.append((mask_hbm.at[0, :, place], mask.at[:, place]))
    pairs[2:2] = [(cols_hbm, cols), (turns_hbm, turns)]
    copies = fetch(pairs, sems)
    table_copies = [copies.pop(2), copies.pop(2)]
    size = target_hbm.shape[0] // PIECES
    goals = fetch(
        [(target_hbm.at[pl.ds(at * size, size)], out_ref.at[at, pl.ds(16, size)]) for at in range(PIECES)],
        target_sems,
    )

    def turned(both, block):
        return turns[block] * both[0] + turns[block + turns.shape[0] // 2] * both[1]

    copies[0].wait()
    own = None
    for at in range(count):
        copies[1 + at].wait()
        top, rest = halves(mask[:, at * width : (at + 1) * width])
        both = mm(rows[...], top)
        top, rest = halves(both[:ROWS_PAD] + both[ROWS_PAD:] + mm(rows[:ROWS_PAD], rest))
        if at == 0:
            for copy in table_copies:
                copy.wait()
        waves = mm(
            jnp.concatenate([top, rest, top], axis=1),
            jnp.concatenate([cols[:, :LANES], cols[:, :LANES], cols[:, LANES:]], axis=0),
        )
        both = (waves, swapped(waves, used))
        if at == 0:
            low = turned(both, count + 1)
        if at == count - 1:
            high = turned(both, 0)
        piece = turned(both, at + 1)
        own = piece if own is None else own + piece

    own, low, high = [packed(part[:ROWS], used) for part in (own, low, high)]
    groups = own.shape[0] // 8
    low = pltpu.roll(low.reshape(groups, 8, LANES), 4, 1)
    upper = lax.broadcasted_iota(jnp.int32, (8, LANES), 0) < 4
    for at in range(groups):
        mine, other = own[8 * at : 8 * at + 8], low[at]
        out_ref[2 * at, :8] = jnp.where(upper, mine, other)
        out_ref[2 * at + 1, :8] = jnp.where(upper, other, mine)
        out_ref[2 * at, 8:16] = high[8 * at : 8 * at + 8]
        out_ref[2 * at + 1, 8:16] = high[8 * at : 8 * at + 8]
    for copy in goals:
        copy.wait()


def mask_spectrum(mask_tiles, target, cols, turns, rows, freq_x):
    tile_px = mask_tiles.shape[1]
    col_stack = np.concatenate(halves_np(cols), axis=1)
    row_stack = np.concatenate(halves_np(rows.T), axis=0)
    hbm = pl.BlockSpec(memory_space=pltpu.HBM)
    return pl.pallas_call(
        functools.partial(spectrum_kernel, freq_x + 1),
        in_specs=[hbm] * 5,
        out_specs=pl.BlockSpec(memory_space=pltpu.VMEM),
        out_shape=jax.ShapeDtypeStruct((PIECES, 24, LANES), F32),
        scratch_shapes=[
            pltpu.VMEM((tile_px, tile_px), F32),
            pltpu.VMEM(col_stack.shape, BF16),
            pltpu.VMEM(turns.shape, F32),
            pltpu.VMEM(row_stack.shape, BF16),
            pltpu.SemaphoreType.DMA((3 + tile_px // AMBIT,)),
            pltpu.SemaphoreType.DMA((PIECES,)),
        ],
        compiler_params=pltpu.CompilerParams(vmem_limit_bytes=20 * 2**20),
        name="mask_spectrum",
    )(in_hbm(mask_tiles), in_hbm(col_stack), in_hbm(turns), in_hbm(row_stack), in_hbm(target))


def slot_pair(first, second, used):
    spare = LANES - used
    lane = lax.broadcasted_iota(jnp.int32, (8, LANES), 1)
    groups = [part[at : at + 8] for part in (first, second) for at in range(0, part.shape[0], 8)]
    last = groups.pop()
    for at, host in enumerate((1, 2, 3, 5)):
        groups[host] = jnp.where(lane < used, groups[host], pltpu.roll(last, (used - spare * at) % LANES, 1))
    return jnp.concatenate(groups, axis=0)


def slot_half(pair, slot, used):
    spare = LANES - used
    lane = lax.broadcasted_iota(jnp.int32, (8, LANES), 1)
    last = jnp.zeros((8, LANES), F32)
    for at, host in enumerate((1, 2, 3, 5)):
        moved = pltpu.roll(pair[8 * host : 8 * host + 8], (spare * at - used) % LANES, 1)
        last = jnp.where((lane >= spare * at) & (lane < min(spare * at + spare, used)), moved, last)
    return jnp.where(slot == 0, pair[:32], jnp.concatenate([pair[32:], last], axis=0))


def slots_of(owner_ref, tiles):
    owners = [owner_ref[tile] for tile in tiles]

    def count(other, before):
        held = owner_ref[other]
        return tuple(
            seen + ((held == owner) & (other < tile)).astype(jnp.int32)
            for seen, owner, tile in zip(before, owners, tiles)
        )

    ranks = lax.fori_loop(0, owner_ref.shape[0], count, (jnp.int32(0),) * len(tiles))
    return list(zip(owners, ranks))


def tiles_of(owner_ref, owner):
    def find(tile, carry):
        count, first, second = carry
        mine = owner_ref[tile] == owner
        first = jnp.where(mine & (count == 0), tile, first)
        second = jnp.where(mine & (count == 1), tile, second)
        return count + mine.astype(jnp.int32), first, second

    zero = jnp.int32(0)
    return lax.fori_loop(0, owner_ref.shape[0], find, (zero, zero, zero))


def mate_of(me):
    return me + 1 - 2 * lax.rem(me, 2)


def route_kernel(owner_ref, pieces_ref, *rest):
    edges_ref = rest[0] if len(rest) == 3 else None
    out_ref, seen = rest[-2:]
    tiles = owner_ref.shape[0]
    me = own_place()
    base = me // PIECES * PIECES
    row = lax.broadcasted_iota(jnp.int32, (8, LANES), 0)
    mine = row // 4 == lax.rem(me, 2)

    def clear(at, carry):
        seen[at] = 0
        return carry

    lax.fori_loop(0, tiles, clear, 0)

    def send(tile, carry):
        owner = owner_ref[tile]
        slot = seen[owner]
        seen[owner] = slot + 1
        at = tile - base

        @pl.when((at >= 0) & (at < PIECES))
        def _():
            high = pieces_ref[jnp.maximum(at - 1, 0), 8:16]
            low = pieces_ref[jnp.minimum(at + 1, PIECES - 1), :8]
            if edges_ref is None:
                edge_high, edge_low = jnp.zeros_like(high), jnp.zeros_like(low)
            else:
                edge_high, edge_low = edges_ref[0, 8:16], edges_ref[1, :8]
            high = jnp.where(at > 0, high, edge_high)
            low = jnp.where(at < PIECES - 1, low, edge_low)
            packet = pieces_ref[at, :8] + high + pltpu.roll(low, 4, 0)
            beside = jnp.where(mine, out_ref[owner, :8], pltpu.roll(packet, 4, 0))
            out_ref[owner, :8] = jnp.where(slot == 0, packet, beside)
            out_ref[owner, pl.ds(pl.multiple_of(8 + 8 * slot, 8), 8)] = pieces_ref[at, 16:]

        return carry

    lax.fori_loop(0, tiles, send, 0)


def route(owner_list, pieces, edges):
    smem = pl.BlockSpec(memory_space=pltpu.SMEM)
    vmem = pl.BlockSpec(memory_space=pltpu.VMEM)
    tiles = owner_list.shape[0]
    extra = [] if edges is None else [edges]
    return pl.pallas_call(
        route_kernel,
        in_specs=[smem, vmem] + [vmem] * len(extra),
        out_specs=vmem,
        out_shape=jax.ShapeDtypeStruct((tiles, 24, LANES), F32),
        scratch_shapes=[pltpu.SMEM((tiles,), jnp.int32)],
        compiler_params=pltpu.CompilerParams(vmem_limit_bytes=2**20),
        name="route",
    )(owner_list, in_vmem(pieces), *extra)


def around(tile, tiles):
    return [
        (tile, None),
        (jnp.maximum(tile - 1, 0), tile > 0),
        (jnp.minimum(tile + 1, tiles - 1), tile < tiles - 1),
    ]


def tile_pick_kernel(used, owner_ref, slopes_ref, out_ref):
    tiles = [tile for tile, _ in around(mate_of(own_place()), owner_ref.shape[0])]
    for at, (owner, slot) in enumerate(slots_of(owner_ref, tiles)):
        out_ref[at] = slot_half(slopes_ref[owner], slot, used)


def tile_pick(owner_list, slopes, freq_x):
    smem = pl.BlockSpec(memory_space=pltpu.SMEM)
    vmem = pl.BlockSpec(memory_space=pltpu.VMEM)
    return pl.pallas_call(
        functools.partial(tile_pick_kernel, freq_x + 1),
        in_specs=[smem, vmem],
        out_specs=vmem,
        out_shape=jax.ShapeDtypeStruct((3, 32, LANES), F32),
        compiler_params=pltpu.CompilerParams(vmem_limit_bytes=2**20),
        name="tile_pick",
    )(owner_list, in_vmem(slopes))


def joined(me, mine, other):
    odd = lax.rem(me, 2) == 1
    return jnp.concatenate([jnp.where(odd, other, mine), jnp.where(odd, mine, other)], axis=0)


def update_kernel(
    used, owner_ref, slopes_ref, other_ref, mask_ref, cols, turns, rows, out_hbm, out, held, out_sems
):
    tile_px = out.shape[0]
    block = tile_px // BLOCKS
    me = own_place()
    near = around(me, owner_ref.shape[0])
    packets = []
    for at, (owner, slot) in enumerate(slots_of(owner_ref, [tile for tile, _ in near])):
        packet = unpacked(joined(me, slot_half(slopes_ref[owner], slot, used), other_ref[at]), used)
        there = near[at][1]
        packets.append(packet if there is None else jnp.where(there, packet, 0.0))

    own, last, following = [(packet, swapped(packet, used)) for packet in packets]

    def turned_back(both, block):
        return turns[block] * both[0] - turns[block + turns.shape[0] // 2] * both[1]

    count = tile_px // AMBIT
    waves = [turned_back(own, at + 1) for at in range(count)]
    waves[0] = waves[0] + turned_back(last, count + 1)
    waves[-1] = waves[-1] + turned_back(following, 0)
    blank = jnp.zeros((ROWS_PAD - ROWS, LANES), F32)
    top, rest = halves(jnp.concatenate([part for wave in waves for part in (wave, blank)], axis=0))
    wide = mm(
        jnp.concatenate([top, rest, top], axis=1),
        jnp.concatenate([cols[:LANES], cols[:LANES], cols[LANES:]], axis=0),
    )
    for at in range(count):
        top, rest = halves(wide[at * ROWS_PAD : (at + 1) * ROWS_PAD])
        held[:, at * AMBIT : (at + 1) * AMBIT] = jnp.concatenate([top, rest, top], axis=0)
    sent = []
    for at in range(BLOCKS):
        here = slice(at * block, (at + 1) * block)
        place = pl.ds(at * block, block)
        out[here] = mask_ref[0, here] - STEP_SIZE * mm(rows[here], held[...])
        copy = pltpu.make_async_copy(out.at[place], out_hbm.at[0, place], out_sems.at[at])
        copy.start()
        sent.append(copy)
    for copy in sent:
        copy.wait()


def update_tables(cols, turns, rows):
    top, rest = halves_np(rows)
    return (
        np.concatenate(halves_np(cols.T), axis=0),
        turns,
        np.concatenate([top, top, rest], axis=1),
    )


def mask_update(owner_list, slopes, other, mask_tiles, cols, turns, rows, freq_x):
    tile_px = mask_tiles.shape[1]
    smem = pl.BlockSpec(memory_space=pltpu.SMEM)
    vmem = pl.BlockSpec(memory_space=pltpu.VMEM)
    hbm = pl.BlockSpec(memory_space=pltpu.HBM)
    return pl.pallas_call(
        functools.partial(update_kernel, freq_x + 1),
        in_specs=[smem] + [vmem] * 6,
        out_specs=hbm,
        out_shape=jax.ShapeDtypeStruct(mask_tiles.shape, F32),
        scratch_shapes=[
            pltpu.VMEM((tile_px, tile_px), F32),
            pltpu.VMEM((3 * ROWS_PAD, tile_px), BF16),
            pltpu.SemaphoreType.DMA((BLOCKS,)),
        ],
        compiler_params=pltpu.CompilerParams(vmem_limit_bytes=16 * 2**20),
        name="mask_update",
    )(
        owner_list, in_vmem(slopes), other, in_vmem(mask_tiles),
        in_vmem(cols), in_vmem(turns), in_vmem(rows),
    )


def half_order():
    return np.arange(GRID_Y // 2).reshape(8, -1).T.reshape(-1)


def image_tables(freq_y, freq_x):
    places_v = np.arange(GRID_X) - (GRID_X - 1) / 2
    freqs_b = np.arange(freq_x) - (freq_x - 1) / 2
    beta = 2.0 * np.pi * np.outer(freqs_b, places_v) / GRID_X
    first = (GRID_X - CORE_X) // 2

    def block(lane_of):
        table = np.zeros((2 * LANES, 2 * LANES))
        for place, lane in lane_of:
            table[:freq_x, lane] = np.cos(beta[:, place])
            table[:freq_x, LANES + lane] = np.sin(beta[:, place])
            table[LANES : LANES + freq_x, lane] = -np.sin(beta[:, place])
            table[LANES : LANES + freq_x, LANES + lane] = np.cos(beta[:, place])
        return table

    core = block([(first + lane, lane) for lane in range(CORE_X)])
    last = first + CORE_X
    rim = block(
        [(first - 2, LANES - 2), (first - 1, LANES - 1), (last, 0), (last + 1, 1)]
    )
    places_u = half_order() + 0.5
    freqs_a = np.arange(freq_y) - (freq_y - 1) / 2
    alpha = 2.0 * np.pi * np.outer(places_u, freqs_a) / GRID_Y
    rows = np.concatenate([np.cos(alpha), np.sin(alpha)], axis=0)
    return core, rim, rows


def rim_tables(rim, kern_count):
    seats = [(LANES - 2 + at) % LANES for at in range(4)]
    seats = seats + [LANES + seat for seat in seats]
    top, rest = halves_np(rim.T[seats])
    blank = np.zeros((LANES - 8, 2 * LANES), BF16)
    rim_out = np.concatenate([top, top, blank[8:], rest, blank], axis=0)
    width = -(-kern_count * RIM_WIDTH // LANES) * LANES
    scatter = np.zeros((4 * LANES, width))
    for kern in range(kern_count):
        for at in range(8):
            lane = (4 * kern - 2 + at % 4) % LANES + at // 4 * LANES
            scatter[lane, kern * RIM_WIDTH + at] = 1.0
            scatter[2 * LANES + lane, kern * RIM_WIDTH + 8 + at] = 1.0
    return rim_out, scatter.astype(BF16)


def pick_tables(freq_y, freq_x):
    col_even, col_odd = signed_picks(freq_x, LANES)
    row_even, row_odd = signed_picks(freq_y, ROWS)
    lanes = np.zeros((LANES, 2 * LANES))
    lanes[:, :freq_x] = col_even.T
    lanes[:, LANES : LANES + freq_x] = col_odd.T
    rows = np.block([[row_even, -row_odd], [-row_odd, -row_even]])
    return lanes, rows


def imaging_kernel(places, used, extra, *refs):
    owner_ref, weight_ref, pieces_ref, kern_ref, table_ref = refs[:5]
    later_hbm, refs = refs[5 : 5 + extra], refs[5 + extra :]
    slopes_ref, error_ref, later_ref, refs = refs[0], refs[1], refs[2 : 2 + extra], refs[2 + extra :]
    spec, field, rim_field, rim_lanes, rim_slope, slope_acc, scale_ref, ready, goal_ref, sems = refs
    kern_count, freq_y, freq_x = kern_ref.shape[2:]
    later = fetch(list(zip(later_hbm, later_ref)), sems)
    batch = max(size for size in range(1, BATCH + 1) if kern_count % size == 0)
    count, first, second = tiles_of(owner_ref, own_place())
    slots = (first, second)
    split = freq_y // 2
    firsts = [slot // PIECES * PIECES for slot in slots]

    def table(name):
        start, height, width = places[name]
        return table_ref[start : start + height, :width]

    def pair(value):
        top, rest = halves(value)
        return jnp.concatenate([top, rest], axis=0)

    upper = lax.broadcasted_iota(jnp.int32, (8, LANES), 0) < 4
    for slot in range(MOST):
        target = jnp.concatenate(
            [pieces_ref[firsts[slot] + at, 8 + 8 * slot : 16 + 8 * slot] for at in range(PIECES)], axis=0
        )
        target = jnp.where(slot < count, target, 0.0)
        one = target.astype(BF16)
        target = target - one.astype(F32)
        two = target.astype(BF16)
        three = (target - two.astype(F32)).astype(BF16)
        goal_ref[slot] = mm(table("turn"), one) + mm(table("turn"), two) + mm(table("turn"), three)
        pieces = []
        for at in range(0, PIECES, 2):
            even, odd = pieces_ref[firsts[slot] + at, :8], pieces_ref[firsts[slot] + at + 1, :8]
            if slot == 0:
                pieces.append(jnp.where(upper, even, odd))
            else:
                pieces.append(pltpu.roll(jnp.where(upper, odd, even), 4, 0))
        packet = jnp.concatenate(pieces, axis=0)
        packet = jnp.where(slot < count, unpacked(packet, used), 0.0)
        both = mm(pair(packet), table("lanes"))
        both = both[:ROWS] + both[ROWS:]
        tall = jnp.concatenate([both[:, :LANES], both[:, LANES:]], axis=0)
        top, rest = halves(tall)
        spec[slot] = mm(table("picks"), top) + mm(table("picks"), rest)

    half = GRID_Y // 2
    lane = lax.broadcasted_iota(jnp.int32, (freq_y, LANES), 1)
    live_lane = lane < freq_x

    def kern_at(k):
        def one(part):
            raw = kern_ref[0, part, k]
            wide = jnp.concatenate([raw, jnp.zeros((freq_y, LANES - freq_x), F32)], axis=1)
            return wide
        return one(0), one(1)

    def side_by_side(pieces):
        return pieces[0] if len(pieces) == 1 else jnp.concatenate(pieces, axis=1)

    def apart(wide):
        size = 2 * LANES
        return [wide[:, at : at + size] for at in range(0, wide.shape[1], size)]

    def to_image(stacks):
        pieces = []
        for stack in stacks:
            top, rest = halves(stack)
            pieces.append(jnp.concatenate([top, rest, top], axis=0))
        return apart(mm(table("rows"), side_by_side(pieces)))

    def from_image(stacks):
        pieces = [jnp.concatenate(halves(stack), axis=0) for stack in stacks]
        both = mm(table("rows_t"), side_by_side(pieces))
        return apart(both[:freq_y] + both[freq_y:])

    def thrice(top, rest, name):
        both = table(name)
        height = both.shape[0] // 2
        return mm(
            jnp.concatenate([top, rest, top], axis=1),
            jnp.concatenate([both[:height], both[:height], both[height:]], axis=0),
        )

    def waves(stack):
        even_re, even_im = stack[:half, :LANES], stack[:half, LANES:]
        odd_re, odd_im = stack[half:, :LANES], stack[half:, LANES:]
        return even_re - odd_im, even_im + odd_re, even_re + odd_im, even_im - odd_re

    def unwaves(plus_re, plus_im, minus_re, minus_im):
        above = jnp.concatenate([plus_re + minus_re, plus_im + minus_im], axis=1)
        below = jnp.concatenate([plus_im - minus_im, minus_re - plus_re], axis=1)
        return jnp.concatenate([above, below], axis=0)

    rim_lanes[...] = jnp.zeros_like(rim_lanes)

    def forward(group, sums):
        tops, rests = [], []
        for step in range(batch):
            kern_re, kern_im = kern_at(group * batch + step)
            for slot in range(2):
                spec_re, spec_im = spec[slot, :freq_y], spec[slot, freq_y:]
                wave = jnp.concatenate(
                    [kern_re * spec_re - kern_im * spec_im, kern_re * spec_im + kern_im * spec_re], axis=1
                )
                top, rest = halves(wave)
                tops.append(top)
                rests.append(rest)
        top, rest = jnp.concatenate(tops, axis=0), jnp.concatenate(rests, axis=0)
        cols = thrice(top, rest, "core")
        edges = thrice(top, rest, "rim")
        new = list(sums)
        for step in range(batch):
            k = group * batch + step
            weight = weight_ref[k]
            new[2] = jnp.where(group_of == k, weight, new[2])
            for slot in range(2):
                at = (2 * step + slot) * freq_y
                edge = edges[at : at + freq_y]
                rim_lanes[slot, :, :LANES] += pltpu.roll(edge[:, :LANES], 4 * k, 1)
                rim_lanes[slot, :, LANES:] += pltpu.roll(edge[:, LANES:], 4 * k, 1)
                if at // freq_y % WIDE == 0:
                    images = to_image([cols[at + near * freq_y : at + (near + 1) * freq_y] for near in range(WIDE)])
                parts = waves(images[at // freq_y % WIDE])
                for part in range(4):
                    field[slot, k, part] = parts[part]
                plus, minus = new[slot]
                plus = plus + weight * (parts[0] * parts[0] + parts[1] * parts[1])
                minus = minus + weight * (parts[2] * parts[2] + parts[3] * parts[3])
                new[slot] = (plus, minus)
        return tuple(new)

    blank = jnp.zeros((half, LANES), F32)
    group_of = lax.rem(lax.broadcasted_iota(jnp.int32, (8, LANES), 1) + 2, LANES) // 4
    *sums, lane_weight = lax.fori_loop(
        0, kern_count // batch, forward, ((blank, blank), (blank, blank), jnp.zeros((8, LANES), F32))
    )

    norm = 1.0 / (64.0 * GRID_Y * GRID_X)
    square = norm * norm
    lane_half = lax.broadcasted_iota(jnp.int32, (half, LANES), 1)
    near = (lane_half < 2) | (lane_half >= LANES - 2)
    row_8 = lax.broadcasted_iota(jnp.int32, (8, LANES), 0)

    def rows_beside(value, other):
        first, last = value[:8], value[half - 8 :]
        later = jnp.where(row_8 == 7, last, pltpu.roll(first, 7, 0))
        sooner = jnp.where(row_8 == 0, other[:8], pltpu.roll(last, 1, 0))
        return jnp.concatenate([value[8:], later], axis=0) + jnp.concatenate([sooner, value[:-8]], axis=0)

    at_first, at_last = lane_half == 0, lane_half == LANES - 1

    def spread_out(value, rows, left, right):
        return value + DIFFUSE_RATE * (rows + left + right - 4.0 * value)

    def sides(value):
        return pltpu.roll(value, 1, 1), pltpu.roll(value, LANES - 1, 1)

    def beside(core, rim):
        return jnp.where(at_first, rim[0], core[0]), jnp.where(at_last, rim[1], core[1])

    def blur(core, rim):
        core_sides = [sides(value) for value in core]
        rim_sides = [sides(value) for value in rim]
        rim_one = [
            spread_out(rim[at], rows_beside(rim[at], rim[1 - at]), *beside(rim_sides[at], core_sides[at]))
            for at in range(2)
        ]
        core_one = [
            spread_out(core[at], rows_beside(core[at], core[1 - at]), *beside(core_sides[at], rim_sides[at]))
            for at in range(2)
        ]
        return [
            spread_out(
                core_one[at],
                rows_beside(core_one[at], core_one[1 - at]),
                *beside(sides(core_one[at]), sides(rim_one[at])),
            )
            for at in range(2)
        ]

    def blur_back(core):
        core_sides = [sides(value) for value in core]
        none = jnp.zeros((half, LANES), F32)
        rim_one = [DIFFUSE_RATE * sum(beside((none, none), core_sides[at])) for at in range(2)]
        core_one = [
            spread_out(core[at], rows_beside(core[at], core[1 - at]), *beside(core_sides[at], (none, none)))
            for at in range(2)
        ]
        core_sides = [sides(value) for value in core_one]
        rim_sides = [sides(value) for value in rim_one]
        rim_two = [
            spread_out(rim_one[at], rows_beside(rim_one[at], rim_one[1 - at]), *beside(rim_sides[at], core_sides[at]))
            for at in range(2)
        ]
        core_two = [
            spread_out(core_one[at], rows_beside(core_one[at], core_one[1 - at]), *beside(core_sides[at], rim_sides[at]))
            for at in range(2)
        ]
        return core_two, rim_two

    def fold(value):
        def back(amount):
            return pltpu.roll(value, LANES - amount, 1)
        value = value + back(48)
        value = value + back(24)
        value = value + back(12)
        return value + back(4) + back(8)

    def unfold(value):
        value = jnp.where(near, value, 0.0)
        value = value + pltpu.roll(value, 4, 1) + pltpu.roll(value, 8, 1)
        value = value + pltpu.roll(value, 12, 1)
        value = value + pltpu.roll(value, 24, 1)
        return value + pltpu.roll(value, 48, 1)

    error = jnp.float32(0.0)
    rim_halves = []
    for slot in range(2):
        live = (slot < count).astype(F32)
        rim_parts = waves(to_image([rim_lanes[slot]])[0])
        for part in range(4):
            rim_field[part] = rim_parts[part]
        weights = jnp.concatenate([lane_weight] * (half // 8), axis=0)
        rim_plus = weights * (rim_parts[0] * rim_parts[0] + rim_parts[1] * rim_parts[1])
        rim_minus = weights * (rim_parts[2] * rim_parts[2] + rim_parts[3] * rim_parts[3])
        core = [part * square for part in sums[slot]]
        rim = [jnp.where(near, fold(part), 0.0) * square for part in (rim_plus, rim_minus)]
        core = blur(core, rim)

        def slope_of(value, goal):
            resist = 1.0 / (1.0 + jnp.exp(-RESIST_SLOPE * (value - RESIST_LEVEL)))
            misfit = resist - goal
            return (2.0 * RESIST_SLOPE) * misfit * resist * (1.0 - resist), jnp.sum(misfit * misfit)

        slope_plus, err_plus = slope_of(core[0], goal_ref[slot, :half])
        slope_minus, err_minus = slope_of(core[1], goal_ref[slot, half:])
        error = error + live * (err_plus + err_minus)
        core, rim = blur_back([slope_plus, slope_minus])
        factor = 2.0 * square
        for at in range(2):
            scale_ref[slot, at] = core[at] * factor
        rim_f_plus = unfold(rim[0] * factor) * weights
        rim_f_minus = unfold(rim[1] * factor) * weights
        edge = from_image(
            [
                unwaves(
                    rim_f_plus * rim_field[0],
                    rim_f_plus * rim_field[1],
                    rim_f_minus * rim_field[2],
                    rim_f_minus * rim_field[3],
                )
            ]
        )[0]
        rim_halves.append(jnp.concatenate(halves(edge), axis=1))
    rim_stack = jnp.concatenate(rim_halves, axis=0)
    for part in range(0, rim_slope.shape[2], 2 * LANES):
        moved = mm(rim_stack, table(f"scatter{part}"))
        for slot in range(MOST):
            rim_slope[slot, :, part : part + moved.shape[1]] = moved[slot * freq_y : (slot + 1) * freq_y]
    error_ref[0] = error * (1.0 / (GRID_Y * CORE_X))

    slope_acc[...] = jnp.zeros_like(slope_acc)

    def backward(group, carry):
        tops, rests, edges, images = [], [], [], []
        for step in range(batch):
            k = group * batch + step
            weight = weight_ref[k]
            for slot in range(2):
                plus = scale_ref[slot, 0] * weight
                minus = scale_ref[slot, 1] * weight
                images.append(
                    unwaves(
                        plus * field[slot, k, 0],
                        plus * field[slot, k, 1],
                        minus * field[slot, k, 2],
                        minus * field[slot, k, 3],
                    )
                )
                if len(images) == WIDE:
                    for cols in from_image(images):
                        top, rest = halves(cols)
                        tops.append(top)
                        rests.append(rest)
                    images = []
                edge = rim_slope[slot, :, pl.ds(pl.multiple_of(k // RIM_KERNS * LANES, LANES), LANES)]
                edge = pltpu.roll(edge, LANES - k % RIM_KERNS * RIM_WIDTH, 1).astype(BF16)
                edges.append(jnp.concatenate([edge, edge], axis=1))

        def stack(pieces):
            return jnp.concatenate(pieces, axis=0)
        waves_all = thrice(stack(tops), stack(rests), "core_t") + mm(stack(edges), table("rim_t"))
        sums = [[slope_acc[slot, :freq_y], slope_acc[slot, freq_y:]] for slot in range(2)]
        for step in range(batch):
            kern_re, kern_im = kern_at(group * batch + step)
            for slot in range(2):
                at = (2 * step + slot) * freq_y
                wave_re, wave_im = waves_all[at : at + freq_y, :LANES], waves_all[at : at + freq_y, LANES:]
                sums[slot][0] += wave_re * kern_re + wave_im * kern_im
                sums[slot][1] += wave_im * kern_re - wave_re * kern_im
        for slot in range(2):
            slope_acc[slot, :freq_y] = sums[slot][0]
            slope_acc[slot, freq_y:] = sums[slot][1]
        return carry

    lax.fori_loop(0, kern_count // batch, backward, 0)

    packets = []
    for slot in range(MOST):
        top, rest = halves(slope_acc[slot])
        tall = mm(table("picks_t"), top) + mm(table("picks_t"), rest)
        wide = jnp.concatenate([tall[:ROWS], tall[ROWS:]], axis=1)
        both = mm(pair(wide), table("lanes_t"))
        packets.append(packed(both[:ROWS] + both[ROWS:], used))
    for at in range(2):
        here = slice(at * split, (at + 1) * split)
        ready[at] = slot_pair(packets[0][here], packets[1][here], used)

    def give(pair_at, carry):
        slopes_ref[2 * pair_at] = ready[0]
        slopes_ref[2 * pair_at + 1] = ready[1]
        return carry

    lax.fori_loop(0, slopes_ref.shape[0] // 2, give, 0)
    for copy in later:
        copy.wait()


def imaging_table(kern_count, freq_y, freq_x):
    core, rim, rows = image_tables(freq_y, freq_x)
    lanes, picks = pick_tables(freq_y, freq_x)

    def tall(table):
        return np.concatenate(halves_np(table), axis=0)

    def three(table):
        top, rest = halves_np(table)
        return np.concatenate([top, top, rest], axis=1)

    def square_up(table):
        top, rest = halves_np(table)
        return np.block([[top, top], [rest, np.zeros_like(rest)]])

    rim_out, scatter = rim_tables(rim, kern_count)
    tables = {
        "core": tall(core),
        "core_t": tall(core.T),
        "rim": tall(rim),
        "rim_t": rim_out,
        "rows": three(rows),
        "rows_t": square_up(rows.T),
        "lanes": lanes.astype(BF16),
        "lanes_t": lanes.T.astype(BF16),
        "picks": picks.astype(BF16),
        "picks_t": picks.T.astype(BF16),
        "turn": np.eye(GRID_Y)[
            np.concatenate([GRID_Y // 2 + half_order(), GRID_Y // 2 - 1 - half_order()])
        ].astype(BF16),
    }
    for part in range(0, scatter.shape[1], 2 * LANES):
        tables[f"scatter{part}"] = scatter[:, part : part + 2 * LANES]
    places, stacked, start = {}, [], 0
    for name, piece in tables.items():
        height, width = piece.shape
        places[name] = (start, height, width)
        stacked.append(np.pad(piece, ((0, 0), (0, 2 * LANES - width))))
        start += height
    return places, np.concatenate(stacked, axis=0)


def owner_imaging(owner_list, kern_weight, pieces, kernels, places, table, later):
    kern_count, freq_y, freq_x = kernels.shape[2:]
    tiles, split = owner_list.shape[0], freq_y // 2
    half = GRID_Y // 2
    smem = pl.BlockSpec(memory_space=pltpu.SMEM)
    vmem = pl.BlockSpec(memory_space=pltpu.VMEM)
    hbm = pl.BlockSpec(memory_space=pltpu.HBM)
    return pl.pallas_call(
        functools.partial(imaging_kernel, places, freq_x + 1, len(later)),
        in_specs=[smem, smem, vmem, vmem, vmem] + [hbm] * len(later),
        out_specs=(vmem, smem) + (vmem,) * len(later),
        out_shape=(
            jax.ShapeDtypeStruct((tiles, 2 * split - 8, LANES), F32),
            jax.ShapeDtypeStruct((1,), F32),
        )
        + tuple(jax.ShapeDtypeStruct(part.shape, part.dtype) for part in later),
        scratch_shapes=[
            pltpu.VMEM((MOST, 2 * freq_y, LANES), F32),
            pltpu.VMEM((MOST, kern_count, 4, half, LANES), F32),
            pltpu.VMEM((4, half, LANES), F32),
            pltpu.VMEM((MOST, freq_y, 2 * LANES), F32),
            pltpu.VMEM((MOST, freq_y, -(-kern_count * RIM_WIDTH // LANES) * LANES), F32),
            pltpu.VMEM((MOST, 2 * freq_y, LANES), F32),
            pltpu.VMEM((MOST, 2, half, LANES), F32),
            pltpu.VMEM((2, 2 * split - 8, LANES), F32),
            pltpu.VMEM((MOST, 2 * half, LANES), F32),
            pltpu.SemaphoreType.DMA((len(later),)),
        ],
        compiler_params=pltpu.CompilerParams(vmem_limit_bytes=20 * 2**20),
        name="owner_imaging",
    )(
        owner_list, kern_weight, in_vmem(pieces), in_vmem(kernels),
        in_vmem(table), *[in_hbm(part) for part in later],
    )


def on_device(mask_tiles, target_grid, kernels, kern_weight, owner_list):
    tile_px = mask_tiles.shape[1]
    freq_y, freq_x = kernels.shape[3:]
    count = lax.axis_size("tile")
    cols, turns, rows = mask_tables(tile_px, freq_y, freq_x)
    owner_list = owner_list.reshape(-1)
    mates = [(i, i + 1 - 2 * (i % 2)) for i in range(count)]

    pieces = mask_spectrum(mask_tiles, target_grid.reshape(GRID_Y, CORE_X), cols, turns, rows, freq_x)
    places, table = imaging_table(kernels.shape[2], freq_y, freq_x)
    pieces, table = lax.optimization_barrier((pieces, jnp.asarray(table)))
    if count == PIECES:
        pieces, edges = lax.all_to_all(pieces, "tile", 0, 0, tiled=True), None
    else:
        groups = [list(range(at, at + PIECES)) for at in range(0, count, PIECES)]
        pieces = lax.all_to_all(pieces, "tile", 0, 0, axis_index_groups=groups, tiled=True)
        later = [(i, i + PIECES) for i in range(count - PIECES)]
        sooner = [(i + PIECES, i) for i in range(count - PIECES)]
        edges = jnp.stack(
            [lax.ppermute(pieces[PIECES - 1], "tile", later), lax.ppermute(pieces[0], "tile", sooner)]
        )
    pieces = lax.all_to_all(route(owner_list, pieces, edges), "tile", 0, 0, tiled=True)
    slopes, owner_error, *held = owner_imaging(
        owner_list, kern_weight, pieces, kernels, places, table,
        (mask_tiles,) + update_tables(cols, turns, rows),
    )
    slopes = lax.all_to_all(slopes, "tile", 0, 0, tiled=True)
    other = lax.ppermute(tile_pick(owner_list, slopes, freq_x), "tile", mates)
    current = mask_update(owner_list, slopes, other, *held, freq_x)
    return (current, owner_error)


def solution(mesh):
    placed = (
        P(("stripe", "tile"), None, None),
        P(("stripe", "tile"), None),
        P("tile", None, None, None, None),
        P(),
        P("stripe", None),
    )
    return jax.shard_map(
        on_device,
        mesh=mesh,
        in_specs=placed,
        out_specs=(P(("stripe", "tile"), None, None), P(("stripe", "tile"))),
        check_vma=False,
    )
```

time: 72.5 us -> 67.9 us (0.937)
  blocking collectives: 28.8 us -> 43.6 us
  waiting for transfers between devices: 10.2 us -> 1.12 us
  starting transfers between devices: 7.46 us -> 0.18 us
  Pallas kernels: 25 us -> 22 us
    all_to_all x1 -> x2, blocking collectives: 11.7 us -> 27.8 us  [the longest x1 16.2 us: on_device(): pieces, edges = (lax.all_to_all(pieces, 'tile', 0, 0, tiled=True), None)]
    all_to_all x1 -> x0, waiting for transfers between devices: 8.99 us -> none  [on_device(): pieces, edges = (lax.all_to_all(pieces, 'tile', 0, 0, tiled=True), None)]
    all_to_all x1 -> x0, starting transfers between devices: 7.38 us -> none  [on_device(): pieces, edges = (lax.all_to_all(pieces, 'tile', 0, 0, tiled=True), None)]
    pallas_call x3, Pallas kernels: 15.7 us -> 13.9 us  [the longest x1 12 us: owner_imaging(): pl.pallas_call(functools.partial(imaging_kernel, places, freq_x + 1, len(...]
    all_to_all x1, blocking collectives: 17.1 us -> 15.9 us  [on_device(): slopes = lax.all_to_all(slopes, 'tile', 0, 0, tiled=True)]
    pallas_call x1, Pallas kernels: 5.82 us -> 4.61 us  [mask_spectrum(): pl.pallas_call(functools.partial(spectrum_kernel, freq_x + 1), in_specs=[...]
  transfers between devices with their start and end apart: 2 -> 1, of which waited for: 2 -> 1; matrix products, arithmetic and copies ran while one was open for 0% -> 0% of each run, Pallas kernels for 0% -> 0%
where the time goes in v3:
time: 67.9 us; the launch traced here: 67.6 us
  blocking collectives  43.6 us (64%)
  Pallas kernels  22 us (32%)
  waiting for transfers between devices  1.12 us (2%)
  between operations  0.7 us (1%)
    all_to_all x1, blocking collectives, on_device(): pieces, edges = (lax.all_to_all(pieces, 'tile', 0, 0, tiled=True), None)  16.2 us
    all_to_all x1, blocking collectives, on_device(): slopes = lax.all_to_all(slopes, 'tile', 0, 0, tiled=True)  15.9 us
    pallas_call x1, Pallas kernels, owner_imaging(): pl.pallas_call(functools.partial(imaging_kernel, places, freq_x + 1, len(...  12 us
    all_to_all x1, blocking collectives, on_device(): lax.all_to_all(route(owner_list, pieces, edges), 'tile', 0, 0, tiled=True)  11.6 us
    pallas_call x1, Pallas kernels, mask_spectrum(): pl.pallas_call(functools.partial(spectrum_kernel, freq_x + 1), in_specs=[...  4.61 us
    pallas_call x1, Pallas kernels, mask_update(): pl.pallas_call(functools.partial(update_kernel, freq_x + 1), in_specs=[sm...  3.52 us
  transfers between devices with their start and end apart: 1, of which 1 were waited for; matrix products, arithmetic and copies ran while one was open for 0% of the time, Pallas kernels for 0%

profile of v3, /device:TPU:0, one launch (start us, length us, event | category | flops | bytes accessed | tf_op | source)
XLA Modules:
  0.0 67.6 jit_solution(10317392148317046241)
XLA Ops:
  0.6 0.0 copy-start
  0.6 0.0 copy-start.2
  0.7 0.0 copy-start.3
  0.7 0.0 copy-start.1
  0.7 4.6 %mask_spectrum.1 = f32[16,24,128]{2,1,0:T(8,128)S(1)} custom-call(f32[1,1024,1024]{2,1,0:T(8,128)} %refs_5_.1, bf16[256,256]{1,0:T(8,128)(2,1)} %constant.12.clone.cols_hbm, f32[12,1,128]{2,1,0:T(1,128)} %constant.13.clone.turns_hbm.refs_7_, bf16[160,1024]{1,0:T(8,128)(2,1)} %constant.14.clone.rows_hbm, f32[128,128]{1,0:T(8,128)} %bitcast.6), custom_call_target="tpu_custom_call" | custom-call | tf_op jit(solution)/shard_map/mask_spectrum/pallas_call | solution.py:202
  5.3 16.2 %all_to_all.15.pieces_ref = f32[16,24,128]{2,1,0:T(8,128)S(1)} all-to-all(f32[16,24,128]{2,1,0:T(8,128)S(1)} %mask_spectrum.1), channel_id=1, replica_groups=mesh['stripe'=2,'tile'=16] {'tile'}, dimensions={0} | all-to-all | bytes 393216 | tf_op jit(solution)/shard_map/all_to_all | solution.py:911
  21.5 0.0 copy-done.2
  21.5 1.0 %route.1 = f32[16,24,128]{2,1,0:T(8,128)S(1)} custom-call(s32[16]{0:T(128)S(1)} %bitcast.2, f32[16,24,128]{2,1,0:T(8,128)S(1)} %all_to_all.15.pieces_ref), custom_call_target="tpu_custom_call" | custom-call | tf_op jit(solution)/shard_map/route/pallas_call | solution.py:316
  22.5 11.6 %all_to_all.16.refs_2_ = f32[16,24,128]{2,1,0:T(8,128)S(1)} all-to-all(f32[16,24,128]{2,1,0:T(8,128)S(1)} %route.1), channel_id=1, replica_groups=mesh['stripe'=2,'tile'=16] {'tile'}, dimensions={0} | all-to-all | bytes 393216 | tf_op jit(solution)/shard_map/all_to_all | solution.py:920
  34.1 0.0 copy-done
  34.1 0.0 copy-done.3
  34.1 0.0 copy-done.1
  34.1 12.0 %owner_imaging.1 = (f32[16,56,128]{2,1,0:T(8,128)S(1)}, f32[1]{0:T(128)}, f32[1,1024,1024]{2,1,0:T(8,128)S(1)}, bf16[256,256]{1,0:T(8,128)(2,1)S(1)}, f32[12,1,1...) custom-call(s32[16]{0:T(128)S(1)} %bitcast.3, f32[24]{0:T(128)S(1)} %copy-done.3, f32[16,24,128]{2,1,0:T(8,128)S(1)} %all_to_all.16.refs_2_, ...), custom_call_target="tpu_custom_call" | custom-call | tf_op jit(solution)/shard_map/owner_imaging/pallas_call | solution.py:870
  46.1 15.9 %all_to_all.17.slopes_ref = f32[16,56,128]{2,1,0:T(8,128)S(1)} all-to-all(f32[16,56,128]{2,1,0:T(8,128)S(1)} %get-tuple-element.12), channel_id=1, replica_groups=mesh['stripe'=2,'tile'=16] {'tile'}, dimensions={0} | all-to-all | bytes 917504 | tf_op jit(solution)/shard_map/all_to_all | solution.py:925
  62.0 0.8 %tile_pick.1 = f32[3,32,128]{2,1,0:T(8,128)S(1)} custom-call(s32[16]{0:T(128)S(1)} %bitcast.4, f32[16,56,128]{2,1,0:T(8,128)S(1)} %all_to_all.17.slopes_ref), custom_call_target="tpu_custom_call" | custom-call | tf_op jit(solution)/shard_map/tile_pick/pallas_call | solution.py:344
  62.8 0.2 collective-permute-start
  63.0 1.1 %collective-permute-done.other_ref = f32[3,32,128]{2,1,0:T(8,128)S(1)} collective-permute-done((f32[3,32,128]{2,1,0:T(8,128)S(1)}, f32[3,32,128]{2,1,0:T(8,128)S(1)}, u32[]{:S(2)}, u32[]{:S(2)}) %collective-permute-start) | collective-permute-done | bytes 49184 | tf_op jit(solution)/shard_map/ppermute | solution.py:926
  64.1 3.5 %mask_update.1 = f32[1,1024,1024]{2,1,0:T(8,128)} custom-call(s32[16]{0:T(128)S(1)} %bitcast.5, f32[16,56,128]{2,1,0:T(8,128)S(1)} %all_to_all.17.slopes_ref, f32[3,32,128]{2,1,0:T(8,128)S(1)} %collective-permute-done.other_ref, f32[1,1024,1024]{2,1,0:T(8,128)S(1)} %get-tuple-element.13.mask_ref, bf16[256,256]{1,0:T(8,128)(2,1)S(1)} %get-tuple-element.14.cols, ...), custom_call_target="tpu_custom_call" | custom-call | tf_op jit(solution)/shard_map/mask_update/pallas_call | solution.py:416
Async XLA Ops:
  0.6 33.4 %copy-start = (bf16[3856,256]{1,0:T(8,128)(2,1)S(1)}, bf16[3856,256]{1,0:T(8,128)(2,1)}, u32[]{:S(2)}) copy-start(bf16[3856,256]{1,0:T(8,128)(2,1)} %constant.15.clone.refs_4_) | copy-start | bytes 5922820
  0.6 20.8 %copy-start.2 = (s32[16,1]{0,1:T(1,128)S(1)}, s32[16,1]{0,1:T(1,128)}, u32[]{:S(2)}) copy-start(s32[16,1]{0,1:T(1,128)} %param.15) | copy-start | bytes 196
  0.7 33.4 %copy-start.3 = (f32[24]{0:T(128)S(1)}, f32[24]{0:T(128)}, u32[]{:S(2)}) copy-start(f32[24]{0:T(128)} %refs_1_.1) | copy-start | bytes 292
  0.7 33.4 %copy-start.1 = (f32[1,2,24,64,96]{4,3,2,1,0:T(8,128)S(1)}, f32[1,2,24,64,96]{4,3,2,1,0:T(8,128)}, u32[]{:S(2)}) copy-start(f32[1,2,24,64,96]{4,3,2,1,0:T(8,128)} %refs_3_.1) | copy-start | bytes 3538948
  62.8 1.3 %collective-permute-start = (f32[3,32,128]{2,1,0:T(8,128)S(1)}, f32[3,32,128]{2,1,0:T(8,128)S(1)}, u32[]{:S(2)}, u32[]{:S(2)}) collective-permute-start(f32[3,32,128]{2,1,0:T(8,128)S(1)} %tile_pick.1), channel_id=1, source_target_pairs={{0,1},{1,0},{2,3},{3,2},{4,5},{5,4},{6,7},{7,6},{8,9},{9,8},{10,11... | collective-permute-start | bytes 147464 | tf_op jit(solution)/shard_map/ppermute | solution.py:926

commit v4 on v3

--- a/solution.py
+++ b/solution.py
@@ -21,8 +21,7 @@
 MOST = 2
 BLOCKS = 4
 PIECES = 16
-BATCH = 12
-WIDE = 8
+CHUNK = 6
 RIM_WIDTH = 16
 RIM_KERNS = LANES // RIM_WIDTH
 ROWS = 72
@@ -492,10 +491,10 @@
     owner_ref, weight_ref, pieces_ref, kern_ref, table_ref = refs[:5]
     later_hbm, refs = refs[5 : 5 + extra], refs[5 + extra :]
     slopes_ref, error_ref, later_ref, refs = refs[0], refs[1], refs[2 : 2 + extra], refs[2 + extra :]
-    spec, field, rim_field, rim_lanes, rim_slope, slope_acc, scale_ref, ready, goal_ref, sems = refs
+    spec, field, rim_field, rim_lanes, rim_slope, scale_ref, ready, goal_ref, sems = refs
     kern_count, freq_y, freq_x = kern_ref.shape[2:]
     later = fetch(list(zip(later_hbm, later_ref)), sems)
-    batch = max(size for size in range(1, BATCH + 1) if kern_count % size == 0)
+    chunk = max(size for size in range(1, CHUNK + 1) if kern_count % size == 0)
     count, first, second = tiles_of(owner_ref, own_place())
     slots = (first, second)
     split = freq_y // 2
@@ -583,13 +582,12 @@
         below = jnp.concatenate([plus_im - minus_im, minus_re - plus_re], axis=1)
         return jnp.concatenate([above, below], axis=0)
 
-    rim_lanes[...] = jnp.zeros_like(rim_lanes)
-
-    def forward(group, sums):
+
+    def forward_chunk(start, new):
         tops, rests = [], []
-        for step in range(batch):
-            kern_re, kern_im = kern_at(group * batch + step)
-            for slot in range(2):
+        for step in range(chunk):
+            kern_re, kern_im = kern_at(start + step)
+            for slot in range(MOST):
                 spec_re, spec_im = spec[slot, :freq_y], spec[slot, freq_y:]
                 wave = jnp.concatenate(
                     [kern_re * spec_re - kern_im * spec_im, kern_re * spec_im + kern_im * spec_re], axis=1
@@ -600,32 +598,33 @@
         top, rest = jnp.concatenate(tops, axis=0), jnp.concatenate(rests, axis=0)
         cols = thrice(top, rest, "core")
         edges = thrice(top, rest, "rim")
-        new = list(sums)
-        for step in range(batch):
-            k = group * batch + step
+        places = [(step, slot) for step in range(chunk) for slot in range(MOST)]
+        images = to_image([cols[at * freq_y : (at + 1) * freq_y] for at in range(len(places))])
+        for at, (step, slot) in enumerate(places):
+            k = start + step
             weight = weight_ref[k]
             new[2] = jnp.where(group_of == k, weight, new[2])
-            for slot in range(2):
-                at = (2 * step + slot) * freq_y
-                edge = edges[at : at + freq_y]
-                rim_lanes[slot, :, :LANES] += pltpu.roll(edge[:, :LANES], 4 * k, 1)
-                rim_lanes[slot, :, LANES:] += pltpu.roll(edge[:, LANES:], 4 * k, 1)
-                if at // freq_y % WIDE == 0:
-                    images = to_image([cols[at + near * freq_y : at + (near + 1) * freq_y] for near in range(WIDE)])
-                parts = waves(images[at // freq_y % WIDE])
-                for part in range(4):
-                    field[slot, k, part] = parts[part]
-                plus, minus = new[slot]
-                plus = plus + weight * (parts[0] * parts[0] + parts[1] * parts[1])
-                minus = minus + weight * (parts[2] * parts[2] + parts[3] * parts[3])
-                new[slot] = (plus, minus)
-        return tuple(new)
+            edge = edges[at * freq_y : (at + 1) * freq_y]
+            for part in range(2):
+                here = slice(part * LANES, (part + 1) * LANES)
+                if k == 0:
+                    rim_lanes[slot, :, here] = edge[:, here]
+                else:
+                    rim_lanes[slot, :, here] += pltpu.roll(edge[:, here], 4 * k, 1)
+            parts = waves(images[at])
+            for part in range(4):
+                field[slot, k, part] = parts[part]
+            plus, minus = new[slot]
+            plus = plus + weight * (parts[0] * parts[0] + parts[1] * parts[1])
+            minus = minus + weight * (parts[2] * parts[2] + parts[3] * parts[3])
+            new[slot] = (plus, minus)
 
     blank = jnp.zeros((half, LANES), F32)
     group_of = lax.rem(lax.broadcasted_iota(jnp.int32, (8, LANES), 1) + 2, LANES) // 4
-    *sums, lane_weight = lax.fori_loop(
-        0, kern_count // batch, forward, ((blank, blank), (blank, blank), jnp.zeros((8, LANES), F32))
-    )
+    sums = [(blank, blank), (blank, blank), jnp.zeros((8, LANES), F32)]
+    for start in range(0, kern_count, chunk):
+        forward_chunk(start, sums)
+    lane_weight = sums.pop()
 
     norm = 1.0 / (64.0 * GRID_Y * GRID_X)
     square = norm * norm
@@ -711,7 +710,7 @@
         live = (slot < count).astype(F32)
         rim_parts = waves(to_image([rim_lanes[slot]])[0])
         for part in range(4):
-            rim_field[part] = rim_parts[part]
+            rim_field[slot, part] = rim_parts[part]
         weights = jnp.concatenate([lane_weight] * (half // 8), axis=0)
         rim_plus = weights * (rim_parts[0] * rim_parts[0] + rim_parts[1] * rim_parts[1])
         rim_minus = weights * (rim_parts[2] * rim_parts[2] + rim_parts[3] * rim_parts[3])
@@ -736,10 +735,10 @@
         edge = from_image(
             [
                 unwaves(
-                    rim_f_plus * rim_field[0],
-                    rim_f_plus * rim_field[1],
-                    rim_f_minus * rim_field[2],
-                    rim_f_minus * rim_field[3],
+                    rim_f_plus * rim_field[slot, 0],
+                    rim_f_plus * rim_field[slot, 1],
+                    rim_f_minus * rim_field[slot, 2],
+                    rim_f_minus * rim_field[slot, 3],
                 )
             ]
         )[0]
@@ -751,14 +750,13 @@
             rim_slope[slot, :, part : part + moved.shape[1]] = moved[slot * freq_y : (slot + 1) * freq_y]
     error_ref[0] = error * (1.0 / (GRID_Y * CORE_X))
 
-    slope_acc[...] = jnp.zeros_like(slope_acc)
-
-    def backward(group, carry):
-        tops, rests, edges, images = [], [], [], []
-        for step in range(batch):
-            k = group * batch + step
+
+    def backward_chunk(start, sums):
+        images, edges = [], []
+        for step in range(chunk):
+            k = start + step
             weight = weight_ref[k]
-            for slot in range(2):
+            for slot in range(MOST):
                 plus = scale_ref[slot, 0] * weight
                 minus = scale_ref[slot, 1] * weight
                 images.append(
@@ -769,37 +767,30 @@
                         minus * field[slot, k, 3],
                     )
                 )
-                if len(images) == WIDE:
-                    for cols in from_image(images):
-                        top, rest = halves(cols)
-                        tops.append(top)
-                        rests.append(rest)
-                    images = []
-                edge = rim_slope[slot, :, pl.ds(pl.multiple_of(k // RIM_KERNS * LANES, LANES), LANES)]
-                edge = pltpu.roll(edge, LANES - k % RIM_KERNS * RIM_WIDTH, 1).astype(BF16)
+                column = k // RIM_KERNS * LANES
+                edge = rim_slope[slot, :, column : column + LANES]
+                if k % RIM_KERNS != 0:
+                    edge = pltpu.roll(edge, LANES - k % RIM_KERNS * RIM_WIDTH, 1)
+                edge = edge.astype(BF16)
                 edges.append(jnp.concatenate([edge, edge], axis=1))
-
-        def stack(pieces):
-            return jnp.concatenate(pieces, axis=0)
-        waves_all = thrice(stack(tops), stack(rests), "core_t") + mm(stack(edges), table("rim_t"))
-        sums = [[slope_acc[slot, :freq_y], slope_acc[slot, freq_y:]] for slot in range(2)]
-        for step in range(batch):
-            kern_re, kern_im = kern_at(group * batch + step)
-            for slot in range(2):
-                at = (2 * step + slot) * freq_y
+        pairs = [halves(cols) for cols in from_image(images)]
+        top, rest = [jnp.concatenate(part, axis=0) for part in zip(*pairs)]
+        waves_all = thrice(top, rest, "core_t") + mm(jnp.concatenate(edges, axis=0), table("rim_t"))
+        for step in range(chunk):
+            kern_re, kern_im = kern_at(start + step)
+            for slot in range(MOST):
+                at = (MOST * step + slot) * freq_y
                 wave_re, wave_im = waves_all[at : at + freq_y, :LANES], waves_all[at : at + freq_y, LANES:]
                 sums[slot][0] += wave_re * kern_re + wave_im * kern_im
                 sums[slot][1] += wave_im * kern_re - wave_re * kern_im
-        for slot in range(2):
-            slope_acc[slot, :freq_y] = sums[slot][0]
-            slope_acc[slot, freq_y:] = sums[slot][1]
-        return carry
-
-    lax.fori_loop(0, kern_count // batch, backward, 0)
+
+    slopes = [[jnp.zeros((freq_y, LANES), F32)] * 2 for _ in range(MOST)]
+    for start in range(0, kern_count, chunk):
+        backward_chunk(start, slopes)
 
     packets = []
     for slot in range(MOST):
-        top, rest = halves(slope_acc[slot])
+        top, rest = halves(jnp.concatenate(slopes[slot], axis=0))
         tall = mm(table("picks_t"), top) + mm(table("picks_t"), rest)
         wide = jnp.concatenate([tall[:ROWS], tall[ROWS:]], axis=1)
         both = mm(pair(wide), table("lanes_t"))
@@ -879,10 +870,9 @@
         scratch_shapes=[
             pltpu.VMEM((MOST, 2 * freq_y, LANES), F32),
             pltpu.VMEM((MOST, kern_count, 4, half, LANES), F32),
-            pltpu.VMEM((4, half, LANES), F32),
+            pltpu.VMEM((MOST, 4, half, LANES), F32),
             pltpu.VMEM((MOST, freq_y, 2 * LANES), F32),
             pltpu.VMEM((MOST, freq_y, -(-kern_count * RIM_WIDTH // LANES) * LANES), F32),
-            pltpu.VMEM((MOST, 2 * freq_y, LANES), F32),
             pltpu.VMEM((MOST, 2, half, LANES), F32),
             pltpu.VMEM((2, 2 * split - 8, LANES), F32),
             pltpu.VMEM((MOST, 2 * half, LANES), F32),

time: 67.9 us -> 66.9 us (0.985)
  Pallas kernels: 22 us -> 21 us
    pallas_call x1, Pallas kernels: 12 us -> 11.1 us  [owner_imaging(): pl.pallas_call(functools.partial(imaging_kernel, places, freq_x + 1, len(...]
where the time goes in v4:
time: 66.9 us; the launch traced here: 66.6 us
  blocking collectives  43.6 us (65%)
  Pallas kernels  21 us (31%)
  waiting for transfers between devices  1.12 us (2%)
  between operations  0.7 us (1%)
    all_to_all x1, blocking collectives, on_device(): pieces, edges = (lax.all_to_all(pieces, 'tile', 0, 0, tiled=True), None)  16.2 us
    all_to_all x1, blocking collectives, on_device(): slopes = lax.all_to_all(slopes, 'tile', 0, 0, tiled=True)  15.9 us
    all_to_all x1, blocking collectives, on_device(): lax.all_to_all(route(owner_list, pieces, edges), 'tile', 0, 0, tiled=True)  11.6 us
    pallas_call x1, Pallas kernels, owner_imaging(): pl.pallas_call(functools.partial(imaging_kernel, places, freq_x + 1, len(...  11.1 us
    pallas_call x1, Pallas kernels, mask_spectrum(): pl.pallas_call(functools.partial(spectrum_kernel, freq_x + 1), in_specs=[...  4.61 us
    pallas_call x1, Pallas kernels, mask_update(): pl.pallas_call(functools.partial(update_kernel, freq_x + 1), in_specs=[sm...  3.52 us
  transfers between devices with their start and end apart: 1, of which 1 were waited for; matrix products, arithmetic and copies ran while one was open for 0% of the time, Pallas kernels for 0%

profile of v4, /device:TPU:0, one launch (start us, length us, event | category | flops | bytes accessed | tf_op | source)
XLA Modules:
  0.0 66.6 jit_solution(12877272087482824230)
XLA Ops:
  0.6 0.0 copy-start
  0.6 0.0 copy-start.2
  0.7 0.0 copy-start.3
  0.7 0.0 copy-start.1
  0.7 4.6 %mask_spectrum.1 = f32[16,24,128]{2,1,0:T(8,128)S(1)} custom-call(f32[1,1024,1024]{2,1,0:T(8,128)} %refs_5_.1, bf16[256,256]{1,0:T(8,128)(2,1)} %constant.12.clone.cols_hbm, f32[12,1,128]{2,1,0:T(1,128)} %constant.13.clone.turns_hbm.refs_7_, bf16[160,1024]{1,0:T(8,128)(2,1)} %constant.14.clone.rows_hbm, f32[128,128]{1,0:T(8,128)} %bitcast.6), custom_call_target="tpu_custom_call" | custom-call | tf_op jit(solution)/shard_map/mask_spectrum/pallas_call | solution.py:201
  5.3 16.2 %all_to_all.15.pieces_ref = f32[16,24,128]{2,1,0:T(8,128)S(1)} all-to-all(f32[16,24,128]{2,1,0:T(8,128)S(1)} %mask_spectrum.1), channel_id=1, replica_groups=mesh['stripe'=2,'tile'=16] {'tile'}, dimensions={0} | all-to-all | bytes 393216 | tf_op jit(solution)/shard_map/all_to_all | solution.py:901
  21.5 0.0 copy-done.2
  21.5 1.0 %route.1 = f32[16,24,128]{2,1,0:T(8,128)S(1)} custom-call(s32[16]{0:T(128)S(1)} %bitcast.2, f32[16,24,128]{2,1,0:T(8,128)S(1)} %all_to_all.15.pieces_ref), custom_call_target="tpu_custom_call" | custom-call | tf_op jit(solution)/shard_map/route/pallas_call | solution.py:315
  22.5 11.6 %all_to_all.16.refs_2_ = f32[16,24,128]{2,1,0:T(8,128)S(1)} all-to-all(f32[16,24,128]{2,1,0:T(8,128)S(1)} %route.1), channel_id=1, replica_groups=mesh['stripe'=2,'tile'=16] {'tile'}, dimensions={0} | all-to-all | bytes 393216 | tf_op jit(solution)/shard_map/all_to_all | solution.py:910
  34.1 0.0 copy-done
  34.1 0.0 copy-done.3
  34.1 0.0 copy-done.1
  34.1 11.1 %owner_imaging.1 = (f32[16,56,128]{2,1,0:T(8,128)S(1)}, f32[1]{0:T(128)}, f32[1,1024,1024]{2,1,0:T(8,128)S(1)}, bf16[256,256]{1,0:T(8,128)(2,1)S(1)}, f32[12,1,1...) custom-call(s32[16]{0:T(128)S(1)} %bitcast.3, f32[24]{0:T(128)S(1)} %copy-done.3, f32[16,24,128]{2,1,0:T(8,128)S(1)} %all_to_all.16.refs_2_, ...), custom_call_target="tpu_custom_call" | custom-call | tf_op jit(solution)/shard_map/owner_imaging/pallas_call | solution.py:861
  45.1 15.9 %all_to_all.17.slopes_ref = f32[16,56,128]{2,1,0:T(8,128)S(1)} all-to-all(f32[16,56,128]{2,1,0:T(8,128)S(1)} %get-tuple-element.12), channel_id=1, replica_groups=mesh['stripe'=2,'tile'=16] {'tile'}, dimensions={0} | all-to-all | bytes 917504 | tf_op jit(solution)/shard_map/all_to_all | solution.py:915
  61.0 0.8 %tile_pick.1 = f32[3,32,128]{2,1,0:T(8,128)S(1)} custom-call(s32[16]{0:T(128)S(1)} %bitcast.4, f32[16,56,128]{2,1,0:T(8,128)S(1)} %all_to_all.17.slopes_ref), custom_call_target="tpu_custom_call" | custom-call | tf_op jit(solution)/shard_map/tile_pick/pallas_call | solution.py:343
  61.8 0.2 collective-permute-start
  62.0 1.1 %collective-permute-done.other_ref = f32[3,32,128]{2,1,0:T(8,128)S(1)} collective-permute-done((f32[3,32,128]{2,1,0:T(8,128)S(1)}, f32[3,32,128]{2,1,0:T(8,128)S(1)}, u32[]{:S(2)}, u32[]{:S(2)}) %collective-permute-start) | collective-permute-done | bytes 49184 | tf_op jit(solution)/shard_map/ppermute | solution.py:916
  63.1 3.5 %mask_update.1 = f32[1,1024,1024]{2,1,0:T(8,128)} custom-call(s32[16]{0:T(128)S(1)} %bitcast.5, f32[16,56,128]{2,1,0:T(8,128)S(1)} %all_to_all.17.slopes_ref, f32[3,32,128]{2,1,0:T(8,128)S(1)} %collective-permute-done.other_ref, f32[1,1024,1024]{2,1,0:T(8,128)S(1)} %get-tuple-element.13.mask_ref, bf16[256,256]{1,0:T(8,128)(2,1)S(1)} %get-tuple-element.14.cols, ...), custom_call_target="tpu_custom_call" | custom-call | tf_op jit(solution)/shard_map/mask_update/pallas_call | solution.py:415
Async XLA Ops:
  0.6 33.4 %copy-start = (bf16[3856,256]{1,0:T(8,128)(2,1)S(1)}, bf16[3856,256]{1,0:T(8,128)(2,1)}, u32[]{:S(2)}) copy-start(bf16[3856,256]{1,0:T(8,128)(2,1)} %constant.15.clone.refs_4_) | copy-start | bytes 5922820
  0.6 20.8 %copy-start.2 = (s32[16,1]{0,1:T(1,128)S(1)}, s32[16,1]{0,1:T(1,128)}, u32[]{:S(2)}) copy-start(s32[16,1]{0,1:T(1,128)} %param.15) | copy-start | bytes 196
  0.7 33.4 %copy-start.3 = (f32[24]{0:T(128)S(1)}, f32[24]{0:T(128)}, u32[]{:S(2)}) copy-start(f32[24]{0:T(128)} %refs_1_.1) | copy-start | bytes 292
  0.7 33.4 %copy-start.1 = (f32[1,2,24,64,96]{4,3,2,1,0:T(8,128)S(1)}, f32[1,2,24,64,96]{4,3,2,1,0:T(8,128)}, u32[]{:S(2)}) copy-start(f32[1,2,24,64,96]{4,3,2,1,0:T(8,128)} %refs_3_.1) | copy-start | bytes 3538948
  61.8 1.3 %collective-permute-start = (f32[3,32,128]{2,1,0:T(8,128)S(1)}, f32[3,32,128]{2,1,0:T(8,128)S(1)}, u32[]{:S(2)}, u32[]{:S(2)}) collective-permute-start(f32[3,32,128]{2,1,0:T(8,128)S(1)} %tile_pick.1), channel_id=1, source_target_pairs={{0,1},{1,0},{2,3},{3,2},{4,5},{5,4},{6,7},{7,6},{8,9},{9,8},{10,11... | collective-permute-start | bytes 147464 | tf_op jit(solution)/shard_map/ppermute | solution.py:916

commit v5 on v4

--- a/solution.py
+++ b/solution.py
@@ -158,26 +158,24 @@
         return turns[block] * both[0] + turns[block + turns.shape[0] // 2] * both[1]
 
     copies[0].wait()
-    own = None
+    terms = []
     for at in range(count):
         copies[1 + at].wait()
         top, rest = halves(mask[:, at * width : (at + 1) * width])
         both = mm(rows[...], top)
         top, rest = halves(both[:ROWS_PAD] + both[ROWS_PAD:] + mm(rows[:ROWS_PAD], rest))
-        if at == 0:
-            for copy in table_copies:
-                copy.wait()
-        waves = mm(
-            jnp.concatenate([top, rest, top], axis=1),
-            jnp.concatenate([cols[:, :LANES], cols[:, :LANES], cols[:, LANES:]], axis=0),
-        )
-        both = (waves, swapped(waves, used))
-        if at == 0:
-            low = turned(both, count + 1)
-        if at == count - 1:
-            high = turned(both, 0)
-        piece = turned(both, at + 1)
-        own = piece if own is None else own + piece
+        terms.append(jnp.concatenate([top, rest, top], axis=1))
+
+    for copy in table_copies:
+        copy.wait()
+    table = jnp.concatenate([cols[:, :LANES], cols[:, :LANES], cols[:, LANES:]], axis=0)
+    waves = []
+    for some in (terms,):
+        wave = mm(jnp.concatenate(some, axis=0), table)
+        waves += [wave[at * ROWS_PAD : (at + 1) * ROWS_PAD] for at in range(len(some))]
+    waves = [(wave, swapped(wave, used)) for wave in waves]
+    own = sum(turned(wave, at + 1) for at, wave in enumerate(waves))
+    low, high = turned(waves[0], count + 1), turned(waves[-1], 0)
 
     own, low, high = [packed(part[:ROWS], used) for part in (own, low, high)]
     groups = own.shape[0] // 8
@@ -236,6 +234,14 @@
     return jnp.where(slot == 0, pair[:32], jnp.concatenate([pair[32:], last], axis=0))
 
 
+def each(count, body, carry):
+    if count > PIECES:
+        return lax.fori_loop(0, count, body, carry)
+    for at in range(count):
+        carry = body(jnp.int32(at), carry)
+    return carry
+
+
 def slots_of(owner_ref, tiles):
     owners = [owner_ref[tile] for tile in tiles]
 
@@ -246,7 +252,7 @@
             for seen, owner, tile in zip(before, owners, tiles)
         )
 
-    ranks = lax.fori_loop(0, owner_ref.shape[0], count, (jnp.int32(0),) * len(tiles))
+    ranks = each(owner_ref.shape[0], count, (jnp.int32(0),) * len(tiles))
     return list(zip(owners, ranks))
 
 
@@ -271,7 +277,7 @@
     out_ref, seen = rest[-2:]
     tiles = owner_ref.shape[0]
     me = own_place()
-    base = me // PIECES * PIECES
+    base = me // PIECES * PIECES if tiles > PIECES else 0
     row = lax.broadcasted_iota(jnp.int32, (8, LANES), 0)
     mine = row // 4 == lax.rem(me, 2)
 
@@ -279,7 +285,7 @@
         seen[at] = 0
         return carry
 
-    lax.fori_loop(0, tiles, clear, 0)
+    each(tiles, clear, 0)
 
     def send(tile, carry):
         owner = owner_ref[tile]
@@ -287,8 +293,7 @@
         seen[owner] = slot + 1
         at = tile - base
 
-        @pl.when((at >= 0) & (at < PIECES))
-        def _():
+        def forward():
             high = pieces_ref[jnp.maximum(at - 1, 0), 8:16]
             low = pieces_ref[jnp.minimum(at + 1, PIECES - 1), :8]
             if edges_ref is None:
@@ -302,9 +307,13 @@
             out_ref[owner, :8] = jnp.where(slot == 0, packet, beside)
             out_ref[owner, pl.ds(pl.multiple_of(8 + 8 * slot, 8), 8)] = pieces_ref[at, 16:]
 
+        if tiles > PIECES:
+            pl.when((at >= 0) & (at < PIECES))(forward)
+        else:
+            forward()
         return carry
 
-    lax.fori_loop(0, tiles, send, 0)
+    each(tiles, send, 0)
 
 
 def route(owner_list, pieces, edges):
@@ -504,10 +513,6 @@
         start, height, width = places[name]
         return table_ref[start : start + height, :width]
 
-    def pair(value):
-        top, rest = halves(value)
-        return jnp.concatenate([top, rest], axis=0)
-
     upper = lax.broadcasted_iota(jnp.int32, (8, LANES), 0) < 4
     for slot in range(MOST):
         target = jnp.concatenate(
@@ -528,8 +533,8 @@
                 pieces.append(pltpu.roll(jnp.where(upper, odd, even), 4, 0))
         packet = jnp.concatenate(pieces, axis=0)
         packet = jnp.where(slot < count, unpacked(packet, used), 0.0)
-        both = mm(pair(packet), table("lanes"))
-        both = both[:ROWS] + both[ROWS:]
+        top, rest = halves(packet)
+        both = mm(top, table("lanes")) + mm(rest, table("lanes"))
         tall = jnp.concatenate([both[:, :LANES], both[:, LANES:]], axis=0)
         top, rest = halves(tall)
         spec[slot] = mm(table("picks"), top) + mm(table("picks"), rest)
@@ -793,8 +798,8 @@
         top, rest = halves(jnp.concatenate(slopes[slot], axis=0))
         tall = mm(table("picks_t"), top) + mm(table("picks_t"), rest)
         wide = jnp.concatenate([tall[:ROWS], tall[ROWS:]], axis=1)
-        both = mm(pair(wide), table("lanes_t"))
-        packets.append(packed(both[:ROWS] + both[ROWS:], used))
+        top, rest = halves(wide)
+        packets.append(packed(mm(top, table("lanes_t")) + mm(rest, table("lanes_t")), used))
     for at in range(2):
         here = slice(at * split, (at + 1) * split)
         ready[at] = slot_pair(packets[0][here], packets[1][here], used)

time: 66.9 us -> 65.7 us (0.982)
  Pallas kernels: 21 us -> 19.8 us
where the time goes in v5:
time: 65.7 us; the launch traced here: 65.4 us
  blocking collectives  43.6 us (66%)
  Pallas kernels  19.8 us (30%)
  waiting for transfers between devices  1.12 us (2%)
  between operations  0.69 us (1%)
    all_to_all x1, blocking collectives, on_device(): pieces, edges = (lax.all_to_all(pieces, 'tile', 0, 0, tiled=True), None)  16.2 us
    all_to_all x1, blocking collectives, on_device(): slopes = lax.all_to_all(slopes, 'tile', 0, 0, tiled=True)  15.9 us
    all_to_all x1, blocking collectives, on_device(): lax.all_to_all(route(owner_list, pieces, edges), 'tile', 0, 0, tiled=True)  11.6 us
    pallas_call x1, Pallas kernels, owner_imaging(): pl.pallas_call(functools.partial(imaging_kernel, places, freq_x + 1, len(...  11.1 us
    pallas_call x1, Pallas kernels, mask_spectrum(): pl.pallas_call(functools.partial(spectrum_kernel, freq_x + 1), in_specs=[...  4.01 us
    pallas_call x1, Pallas kernels, mask_update(): pl.pallas_call(functools.partial(update_kernel, freq_x + 1), in_specs=[sm...  3.39 us
  transfers between devices with their start and end apart: 1, of which 1 were waited for; matrix products, arithmetic and copies ran while one was open for 0% of the time, Pallas kernels for 0%

profile of v5, /device:TPU:0, one launch (start us, length us, event | category | flops | bytes accessed | tf_op | source)
XLA Modules:
  0.0 65.4 jit_solution(7708892659239908003)
XLA Ops:
  0.6 0.0 copy-start
  0.6 0.0 copy-start.2
  0.7 0.0 copy-start.3
  0.7 0.0 copy-start.1
  0.7 4.0 %mask_spectrum.1 = f32[16,24,128]{2,1,0:T(8,128)S(1)} custom-call(f32[1,1024,1024]{2,1,0:T(8,128)} %refs_5_.1, bf16[256,256]{1,0:T(8,128)(2,1)} %constant.12.clone.cols_hbm, f32[12,1,128]{2,1,0:T(1,128)} %constant.13.clone.turns_hbm.refs_7_, bf16[160,1024]{1,0:T(8,128)(2,1)} %constant.14.clone.rows_hbm, f32[128,128]{1,0:T(8,128)} %bitcast.6), custom_call_target="tpu_custom_call" | custom-call | tf_op jit(solution)/shard_map/mask_spectrum/pallas_call | solution.py:199
  4.7 16.2 %all_to_all.15.pieces_ref = f32[16,24,128]{2,1,0:T(8,128)S(1)} all-to-all(f32[16,24,128]{2,1,0:T(8,128)S(1)} %mask_spectrum.1), channel_id=1, replica_groups=mesh['stripe'=2,'tile'=16] {'tile'}, dimensions={0} | all-to-all | bytes 393216 | tf_op jit(solution)/shard_map/all_to_all | solution.py:906
  20.9 0.0 copy-done.2
  20.9 0.6 route.1
  21.5 11.6 %all_to_all.16.refs_2_ = f32[16,24,128]{2,1,0:T(8,128)S(1)} all-to-all(f32[16,24,128]{2,1,0:T(8,128)S(1)} %route.1), channel_id=1, replica_groups=mesh['stripe'=2,'tile'=16] {'tile'}, dimensions={0} | all-to-all | bytes 393216 | tf_op jit(solution)/shard_map/all_to_all | solution.py:915
  33.1 0.0 copy-done
  33.1 0.0 copy-done.3
  33.1 0.0 copy-done.1
  33.1 11.1 %owner_imaging.1 = (f32[16,56,128]{2,1,0:T(8,128)S(1)}, f32[1]{0:T(128)}, f32[1,1024,1024]{2,1,0:T(8,128)S(1)}, bf16[256,256]{1,0:T(8,128)(2,1)S(1)}, f32[12,1,1...) custom-call(s32[16]{0:T(128)S(1)} %bitcast.3, f32[24]{0:T(128)S(1)} %copy-done.3, f32[16,24,128]{2,1,0:T(8,128)S(1)} %all_to_all.16.refs_2_, ...), custom_call_target="tpu_custom_call" | custom-call | tf_op jit(solution)/shard_map/owner_imaging/pallas_call | solution.py:866
  44.2 15.9 %all_to_all.17.slopes_ref = f32[16,56,128]{2,1,0:T(8,128)S(1)} all-to-all(f32[16,56,128]{2,1,0:T(8,128)S(1)} %get-tuple-element.12), channel_id=1, replica_groups=mesh['stripe'=2,'tile'=16] {'tile'}, dimensions={0} | all-to-all | bytes 917504 | tf_op jit(solution)/shard_map/all_to_all | solution.py:920
  60.1 0.7 %tile_pick.1 = f32[3,32,128]{2,1,0:T(8,128)S(1)} custom-call(s32[16]{0:T(128)S(1)} %bitcast.4, f32[16,56,128]{2,1,0:T(8,128)S(1)} %all_to_all.17.slopes_ref), custom_call_target="tpu_custom_call" | custom-call | tf_op jit(solution)/shard_map/tile_pick/pallas_call | solution.py:352
  60.7 0.2 collective-permute-start
  60.9 1.1 %collective-permute-done.other_ref = f32[3,32,128]{2,1,0:T(8,128)S(1)} collective-permute-done((f32[3,32,128]{2,1,0:T(8,128)S(1)}, f32[3,32,128]{2,1,0:T(8,128)S(1)}, u32[]{:S(2)}, u32[]{:S(2)}) %collective-permute-start) | collective-permute-done | bytes 49184 | tf_op jit(solution)/shard_map/ppermute | solution.py:921
  62.0 3.4 %mask_update.1 = f32[1,1024,1024]{2,1,0:T(8,128)} custom-call(s32[16]{0:T(128)S(1)} %bitcast.5, f32[16,56,128]{2,1,0:T(8,128)S(1)} %all_to_all.17.slopes_ref, f32[3,32,128]{2,1,0:T(8,128)S(1)} %collective-permute-done.other_ref, f32[1,1024,1024]{2,1,0:T(8,128)S(1)} %get-tuple-element.13.mask_ref, bf16[256,256]{1,0:T(8,128)(2,1)S(1)} %get-tuple-element.14.cols, ...), custom_call_target="tpu_custom_call" | custom-call | tf_op jit(solution)/shard_map/mask_update/pallas_call | solution.py:424
Async XLA Ops:
  0.6 32.5 %copy-start = (bf16[3856,256]{1,0:T(8,128)(2,1)S(1)}, bf16[3856,256]{1,0:T(8,128)(2,1)}, u32[]{:S(2)}) copy-start(bf16[3856,256]{1,0:T(8,128)(2,1)} %constant.15.clone.refs_4_) | copy-start | bytes 5922820
  0.6 20.2 %copy-start.2 = (s32[16,1]{0,1:T(1,128)S(1)}, s32[16,1]{0,1:T(1,128)}, u32[]{:S(2)}) copy-start(s32[16,1]{0,1:T(1,128)} %param.15) | copy-start | bytes 196
  0.7 32.5 %copy-start.3 = (f32[24]{0:T(128)S(1)}, f32[24]{0:T(128)}, u32[]{:S(2)}) copy-start(f32[24]{0:T(128)} %refs_1_.1) | copy-start | bytes 292
  0.7 32.5 %copy-start.1 = (f32[1,2,24,64,96]{4,3,2,1,0:T(8,128)S(1)}, f32[1,2,24,64,96]{4,3,2,1,0:T(8,128)}, u32[]{:S(2)}) copy-start(f32[1,2,24,64,96]{4,3,2,1,0:T(8,128)} %refs_3_.1) | copy-start | bytes 3538948
  60.7 1.3 %collective-permute-start = (f32[3,32,128]{2,1,0:T(8,128)S(1)}, f32[3,32,128]{2,1,0:T(8,128)S(1)}, u32[]{:S(2)}, u32[]{:S(2)}) collective-permute-start(f32[3,32,128]{2,1,0:T(8,128)S(1)} %tile_pick.1), channel_id=1, source_target_pairs={{0,1},{1,0},{2,3},{3,2},{4,5},{5,4},{6,7},{7,6},{8,9},{9,8},{10,11... | collective-permute-start | bytes 147464 | tf_op jit(solution)/shard_map/ppermute | solution.py:921

commit v6 on v5

--- a/solution.py
+++ b/solution.py
@@ -22,6 +22,7 @@
 BLOCKS = 4
 PIECES = 16
 CHUNK = 6
+QUARTER = 32
 RIM_WIDTH = 16
 RIM_KERNS = LANES // RIM_WIDTH
 ROWS = 72
@@ -472,6 +473,14 @@
 
 def rim_tables(rim, kern_count):
     seats = [(LANES - 2 + at) % LANES for at in range(4)]
+    top, rest = halves_np(rim)
+    rim_in = np.zeros((4 * LANES, LANES), BF16)
+    for seat in seats:
+        for quarter, source in enumerate((seat, LANES + seat)):
+            place = (seat + quarter * QUARTER) % LANES
+            rim_in[: 2 * LANES, place] = top[:, source]
+            rim_in[2 * LANES :, place] = top[:, source]
+            rim_in[: 2 * LANES, (place + 2 * QUARTER) % LANES] = rest[:, source]
     seats = seats + [LANES + seat for seat in seats]
     top, rest = halves_np(rim.T[seats])
     blank = np.zeros((LANES - 8, 2 * LANES), BF16)
@@ -483,12 +492,12 @@
             lane = (4 * kern - 2 + at % 4) % LANES + at // 4 * LANES
             scatter[lane, kern * RIM_WIDTH + at] = 1.0
             scatter[2 * LANES + lane, kern * RIM_WIDTH + 8 + at] = 1.0
-    return rim_out, scatter.astype(BF16)
+    return rim_in, rim_out, scatter.astype(BF16)
 
 
 def pick_tables(freq_y, freq_x):
     col_even, col_odd = signed_picks(freq_x, LANES)
-    row_even, row_odd = signed_picks(freq_y, ROWS)
+    row_even, row_odd = signed_picks(freq_y, ROWS_PAD)
     lanes = np.zeros((LANES, 2 * LANES))
     lanes[:, :freq_x] = col_even.T
     lanes[:, LANES : LANES + freq_x] = col_odd.T
@@ -514,16 +523,13 @@
         return table_ref[start : start + height, :width]
 
     upper = lax.broadcasted_iota(jnp.int32, (8, LANES), 0) < 4
+    blank = jnp.zeros((ROWS_PAD - ROWS, LANES), F32)
+    targets, packets = [], []
     for slot in range(MOST):
         target = jnp.concatenate(
             [pieces_ref[firsts[slot] + at, 8 + 8 * slot : 16 + 8 * slot] for at in range(PIECES)], axis=0
         )
-        target = jnp.where(slot < count, target, 0.0)
-        one = target.astype(BF16)
-        target = target - one.astype(F32)
-        two = target.astype(BF16)
-        three = (target - two.astype(F32)).astype(BF16)
-        goal_ref[slot] = mm(table("turn"), one) + mm(table("turn"), two) + mm(table("turn"), three)
+        targets.append(jnp.where(slot < count, target, 0.0))
         pieces = []
         for at in range(0, PIECES, 2):
             even, odd = pieces_ref[firsts[slot] + at, :8], pieces_ref[firsts[slot] + at + 1, :8]
@@ -532,12 +538,29 @@
             else:
                 pieces.append(pltpu.roll(jnp.where(upper, odd, even), 4, 0))
         packet = jnp.concatenate(pieces, axis=0)
-        packet = jnp.where(slot < count, unpacked(packet, used), 0.0)
-        top, rest = halves(packet)
-        both = mm(top, table("lanes")) + mm(rest, table("lanes"))
-        tall = jnp.concatenate([both[:, :LANES], both[:, LANES:]], axis=0)
-        top, rest = halves(tall)
-        spec[slot] = mm(table("picks"), top) + mm(table("picks"), rest)
+        packets += [jnp.where(slot < count, unpacked(packet, used), 0.0), blank]
+
+    top, rest = halves(jnp.concatenate(packets, axis=0))
+    both = mm(
+        jnp.concatenate([top, rest], axis=1), jnp.concatenate([table("lanes"), table("lanes")], axis=0)
+    )
+    tall = [
+        jnp.concatenate([both[at : at + ROWS_PAD, :LANES], both[at : at + ROWS_PAD, LANES:]], axis=0)
+        for at in range(0, MOST * ROWS_PAD, ROWS_PAD)
+    ]
+    top, rest = halves(jnp.concatenate(tall, axis=1))
+    both = mm(table("picks"), top) + mm(table("picks"), rest)
+    for slot in range(MOST):
+        spec[slot] = both[:, slot * LANES : (slot + 1) * LANES]
+
+    target = jnp.concatenate(targets, axis=1)
+    one = target.astype(BF16)
+    target = target - one.astype(F32)
+    two = target.astype(BF16)
+    three = (target - two.astype(F32)).astype(BF16)
+    both = mm(table("turn"), one) + mm(table("turn"), two) + mm(table("turn"), three)
+    for slot in range(MOST):
+        goal_ref[slot] = both[:, slot * LANES : (slot + 1) * LANES]
 
     half = GRID_Y // 2
     lane = lax.broadcasted_iota(jnp.int32, (freq_y, LANES), 1)
@@ -602,7 +625,7 @@
                 rests.append(rest)
         top, rest = jnp.concatenate(tops, axis=0), jnp.concatenate(rests, axis=0)
         cols = thrice(top, rest, "core")
-        edges = thrice(top, rest, "rim")
+        edges = mm(jnp.concatenate([top, rest], axis=1), table("rim"))
         places = [(step, slot) for step in range(chunk) for slot in range(MOST)]
         images = to_image([cols[at * freq_y : (at + 1) * freq_y] for at in range(len(places))])
         for at, (step, slot) in enumerate(places):
@@ -610,12 +633,12 @@
             weight = weight_ref[k]
             new[2] = jnp.where(group_of == k, weight, new[2])
             edge = edges[at * freq_y : (at + 1) * freq_y]
-            for part in range(2):
-                here = slice(part * LANES, (part + 1) * LANES)
-                if k == 0:
-                    rim_lanes[slot, :, here] = edge[:, here]
-                else:
-                    rim_lanes[slot, :, here] += pltpu.roll(edge[:, here], 4 * k, 1)
+            column, place = divmod(k, QUARTER // 4)
+            here = slice(column * LANES, (column + 1) * LANES)
+            if place == 0:
+                rim_lanes[slot, :, here] = edge
+            else:
+                rim_lanes[slot, :, here] += pltpu.roll(edge, 4 * place, 1)
             parts = waves(images[at])
             for part in range(4):
                 field[slot, k, part] = parts[part]
@@ -709,11 +732,23 @@
         value = value + pltpu.roll(value, 24, 1)
         return value + pltpu.roll(value, 48, 1)
 
+    def rim_columns(slot):
+        quarter = lax.rem(lane + 2, LANES) // QUARTER
+        real = imag = jnp.zeros((freq_y, LANES), F32)
+        for column in range(rim_lanes.shape[2] // LANES):
+            both = rim_lanes[slot, :, column * LANES : (column + 1) * LANES]
+            both = both + pltpu.roll(both, 2 * QUARTER, 1)
+            for_real = both if column == 0 else pltpu.roll(both, column * QUARTER, 1)
+            for_imag = both if column == 1 else pltpu.roll(both, (column - 1) * QUARTER % LANES, 1)
+            real = jnp.where(quarter == column, for_real, real)
+            imag = jnp.where(quarter == column, for_imag, imag)
+        return jnp.concatenate([real, imag], axis=1)
+
     error = jnp.float32(0.0)
     rim_halves = []
     for slot in range(2):
         live = (slot < count).astype(F32)
-        rim_parts = waves(to_image([rim_lanes[slot]])[0])
+        rim_parts = waves(to_image([rim_columns(slot)])[0])
         for part in range(4):
             rim_field[slot, part] = rim_parts[part]
         weights = jnp.concatenate([lane_weight] * (half // 8), axis=0)
@@ -793,13 +828,17 @@
     for start in range(0, kern_count, chunk):
         backward_chunk(start, slopes)
 
-    packets = []
-    for slot in range(MOST):
-        top, rest = halves(jnp.concatenate(slopes[slot], axis=0))
-        tall = mm(table("picks_t"), top) + mm(table("picks_t"), rest)
-        wide = jnp.concatenate([tall[:ROWS], tall[ROWS:]], axis=1)
-        top, rest = halves(wide)
-        packets.append(packed(mm(top, table("lanes_t")) + mm(rest, table("lanes_t")), used))
+    tall = jnp.concatenate([jnp.concatenate(slopes[slot], axis=0) for slot in range(MOST)], axis=1)
+    both = mm(table("picks_t"), jnp.concatenate(halves(tall), axis=0))
+    wide = [
+        jnp.concatenate([both[:ROWS_PAD, at : at + LANES], both[ROWS_PAD:, at : at + LANES]], axis=1)
+        for at in range(0, MOST * LANES, LANES)
+    ]
+    top, rest = halves(jnp.concatenate(wide, axis=0))
+    both = mm(
+        jnp.concatenate([top, rest], axis=1), jnp.concatenate([table("lanes_t"), table("lanes_t")], axis=0)
+    )
+    packets = [packed(both[at : at + ROWS], used) for at in range(0, MOST * ROWS_PAD, ROWS_PAD)]
     for at in range(2):
         here = slice(at * split, (at + 1) * split)
         ready[at] = slot_pair(packets[0][here], packets[1][here], used)
@@ -829,18 +868,18 @@
         top, rest = halves_np(table)
         return np.block([[top, top], [rest, np.zeros_like(rest)]])
 
-    rim_out, scatter = rim_tables(rim, kern_count)
+    rim_in, rim_out, scatter = rim_tables(rim, kern_count)
     tables = {
         "core": tall(core),
         "core_t": tall(core.T),
-        "rim": tall(rim),
+        "rim": rim_in,
         "rim_t": rim_out,
         "rows": three(rows),
         "rows_t": square_up(rows.T),
         "lanes": lanes.astype(BF16),
         "lanes_t": lanes.T.astype(BF16),
         "picks": picks.astype(BF16),
-        "picks_t": picks.T.astype(BF16),
+        "picks_t": np.concatenate([picks.T, picks.T], axis=1).astype(BF16),
         "turn": np.eye(GRID_Y)[
             np.concatenate([GRID_Y // 2 + half_order(), GRID_Y // 2 - 1 - half_order()])
         ].astype(BF16),
@@ -876,7 +915,7 @@
             pltpu.VMEM((MOST, 2 * freq_y, LANES), F32),
             pltpu.VMEM((MOST, kern_count, 4, half, LANES), F32),
             pltpu.VMEM((MOST, 4, half, LANES), F32),
-            pltpu.VMEM((MOST, freq_y, 2 * LANES), F32),
+            pltpu.VMEM((MOST, freq_y, -(-kern_count * 4 // QUARTER) * LANES), F32),
             pltpu.VMEM((MOST, freq_y, -(-kern_count * RIM_WIDTH // LANES) * LANES), F32),
             pltpu.VMEM((MOST, 2, half, LANES), F32),
             pltpu.VMEM((2, 2 * split - 8, LANES), F32),

time: 65.7 us -> 65.2 us (level)
  no operation moved by 1% of the time
where the time goes in v6:
time: 65.2 us; the launch traced here: 65 us
  blocking collectives  43.6 us (67%)
  Pallas kernels  19.3 us (30%)
  waiting for transfers between devices  1.12 us (2%)
  between operations  0.69 us (1%)
    all_to_all x1, blocking collectives, on_device(): pieces, edges = (lax.all_to_all(pieces, 'tile', 0, 0, tiled=True), None)  16.2 us
    all_to_all x1, blocking collectives, on_device(): slopes = lax.all_to_all(slopes, 'tile', 0, 0, tiled=True)  15.9 us
    all_to_all x1, blocking collectives, on_device(): lax.all_to_all(route(owner_list, pieces, edges), 'tile', 0, 0, tiled=True)  11.6 us
    pallas_call x1, Pallas kernels, owner_imaging(): pl.pallas_call(functools.partial(imaging_kernel, places, freq_x + 1, len(...  10.6 us
    pallas_call x1, Pallas kernels, mask_spectrum(): pl.pallas_call(functools.partial(spectrum_kernel, freq_x + 1), in_specs=[...  4.01 us
    pallas_call x1, Pallas kernels, mask_update(): pl.pallas_call(functools.partial(update_kernel, freq_x + 1), in_specs=[sm...  3.4 us
  transfers between devices with their start and end apart: 1, of which 1 were waited for; matrix products, arithmetic and copies ran while one was open for 0% of the time, Pallas kernels for 0%

profile of v6, /device:TPU:0, one launch (start us, length us, event | category | flops | bytes accessed | tf_op | source)
XLA Modules:
  0.0 65.0 jit_solution(10962519561936074642)
XLA Ops:
  0.6 0.0 copy-start
  0.6 0.0 copy-start.2
  0.7 0.0 copy-start.3
  0.7 0.0 copy-start.1
  0.7 4.0 %mask_spectrum.1 = f32[16,24,128]{2,1,0:T(8,128)S(1)} custom-call(f32[1,1024,1024]{2,1,0:T(8,128)} %refs_5_.1, bf16[256,256]{1,0:T(8,128)(2,1)} %constant.12.clone.cols_hbm, f32[12,1,128]{2,1,0:T(1,128)} %constant.13.clone.turns_hbm.refs_7_, bf16[160,1024]{1,0:T(8,128)(2,1)} %constant.14.clone.rows_hbm, f32[128,128]{1,0:T(8,128)} %bitcast.6), custom_call_target="tpu_custom_call" | custom-call | tf_op jit(solution)/shard_map/mask_spectrum/pallas_call | solution.py:200
  4.7 16.2 %all_to_all.15.pieces_ref = f32[16,24,128]{2,1,0:T(8,128)S(1)} all-to-all(f32[16,24,128]{2,1,0:T(8,128)S(1)} %mask_spectrum.1), channel_id=1, replica_groups=mesh['stripe'=2,'tile'=16] {'tile'}, dimensions={0} | all-to-all | bytes 393216 | tf_op jit(solution)/shard_map/all_to_all | solution.py:945
  20.9 0.0 copy-done.2
  20.9 0.6 route.1
  21.5 11.6 %all_to_all.16.refs_2_ = f32[16,24,128]{2,1,0:T(8,128)S(1)} all-to-all(f32[16,24,128]{2,1,0:T(8,128)S(1)} %route.1), channel_id=1, replica_groups=mesh['stripe'=2,'tile'=16] {'tile'}, dimensions={0} | all-to-all | bytes 393216 | tf_op jit(solution)/shard_map/all_to_all | solution.py:954
  33.1 0.0 copy-done
  33.1 0.0 copy-done.3
  33.1 0.0 copy-done.1
  33.1 10.6 %owner_imaging.1 = (f32[16,56,128]{2,1,0:T(8,128)S(1)}, f32[1]{0:T(128)}, f32[1,1024,1024]{2,1,0:T(8,128)S(1)}, bf16[256,256]{1,0:T(8,128)(2,1)S(1)}, f32[12,1,1...) custom-call(s32[16]{0:T(128)S(1)} %bitcast.3, f32[24]{0:T(128)S(1)} %copy-done.3, f32[16,24,128]{2,1,0:T(8,128)S(1)} %all_to_all.16.refs_2_, ...), custom_call_target="tpu_custom_call" | custom-call | tf_op jit(solution)/shard_map/owner_imaging/pallas_call | solution.py:905
  43.8 15.9 %all_to_all.17.slopes_ref = f32[16,56,128]{2,1,0:T(8,128)S(1)} all-to-all(f32[16,56,128]{2,1,0:T(8,128)S(1)} %get-tuple-element.12), channel_id=1, replica_groups=mesh['stripe'=2,'tile'=16] {'tile'}, dimensions={0} | all-to-all | bytes 917504 | tf_op jit(solution)/shard_map/all_to_all | solution.py:959
  59.6 0.7 %tile_pick.1 = f32[3,32,128]{2,1,0:T(8,128)S(1)} custom-call(s32[16]{0:T(128)S(1)} %bitcast.4, f32[16,56,128]{2,1,0:T(8,128)S(1)} %all_to_all.17.slopes_ref), custom_call_target="tpu_custom_call" | custom-call | tf_op jit(solution)/shard_map/tile_pick/pallas_call | solution.py:353
  60.3 0.2 collective-permute-start
  60.5 1.1 %collective-permute-done.other_ref = f32[3,32,128]{2,1,0:T(8,128)S(1)} collective-permute-done((f32[3,32,128]{2,1,0:T(8,128)S(1)}, f32[3,32,128]{2,1,0:T(8,128)S(1)}, u32[]{:S(2)}, u32[]{:S(2)}) %collective-permute-start) | collective-permute-done | bytes 49184 | tf_op jit(solution)/shard_map/ppermute | solution.py:960
  61.6 3.4 %mask_update.1 = f32[1,1024,1024]{2,1,0:T(8,128)} custom-call(s32[16]{0:T(128)S(1)} %bitcast.5, f32[16,56,128]{2,1,0:T(8,128)S(1)} %all_to_all.17.slopes_ref, f32[3,32,128]{2,1,0:T(8,128)S(1)} %collective-permute-done.other_ref, f32[1,1024,1024]{2,1,0:T(8,128)S(1)} %get-tuple-element.13.mask_ref, bf16[256,256]{1,0:T(8,128)(2,1)S(1)} %get-tuple-element.14.cols, ...), custom_call_target="tpu_custom_call" | custom-call | tf_op jit(solution)/shard_map/mask_update/pallas_call | solution.py:425
Async XLA Ops:
  0.6 32.5 %copy-start = (bf16[3872,256]{1,0:T(8,128)(2,1)S(1)}, bf16[3872,256]{1,0:T(8,128)(2,1)}, u32[]{:S(2)}) copy-start(bf16[3872,256]{1,0:T(8,128)(2,1)} %constant.15.clone.refs_4_) | copy-start | bytes 5947396
  0.6 20.2 %copy-start.2 = (s32[16,1]{0,1:T(1,128)S(1)}, s32[16,1]{0,1:T(1,128)}, u32[]{:S(2)}) copy-start(s32[16,1]{0,1:T(1,128)} %param.15) | copy-start | bytes 196
  0.7 32.5 %copy-start.3 = (f32[24]{0:T(128)S(1)}, f32[24]{0:T(128)}, u32[]{:S(2)}) copy-start(f32[24]{0:T(128)} %refs_1_.1) | copy-start | bytes 292
  0.7 32.5 %copy-start.1 = (f32[1,2,24,64,96]{4,3,2,1,0:T(8,128)S(1)}, f32[1,2,24,64,96]{4,3,2,1,0:T(8,128)}, u32[]{:S(2)}) copy-start(f32[1,2,24,64,96]{4,3,2,1,0:T(8,128)} %refs_3_.1) | copy-start | bytes 3538948
  60.3 1.3 %collective-permute-start = (f32[3,32,128]{2,1,0:T(8,128)S(1)}, f32[3,32,128]{2,1,0:T(8,128)S(1)}, u32[]{:S(2)}, u32[]{:S(2)}) collective-permute-start(f32[3,32,128]{2,1,0:T(8,128)S(1)} %tile_pick.1), channel_id=1, source_target_pairs={{0,1},{1,0},{2,3},{3,2},{4,5},{5,4},{6,7},{7,6},{8,9},{9,8},{10,11... | collective-permute-start | bytes 147464 | tf_op jit(solution)/shard_map/ppermute | solution.py:960

commit v7 on v6

--- a/solution.py
+++ b/solution.py
@@ -235,38 +235,28 @@
     return jnp.where(slot == 0, pair[:32], jnp.concatenate([pair[32:], last], axis=0))
 
 
-def each(count, body, carry):
-    if count > PIECES:
-        return lax.fori_loop(0, count, body, carry)
-    for at in range(count):
-        carry = body(jnp.int32(at), carry)
-    return carry
-
-
 def slots_of(owner_ref, tiles):
-    owners = [owner_ref[tile] for tile in tiles]
-
-    def count(other, before):
-        held = owner_ref[other]
-        return tuple(
-            seen + ((held == owner) & (other < tile)).astype(jnp.int32)
-            for seen, owner, tile in zip(before, owners, tiles)
-        )
-
-    ranks = each(owner_ref.shape[0], count, (jnp.int32(0),) * len(tiles))
-    return list(zip(owners, ranks))
+    owners = owner_ref[...].astype(F32)
+    lane = lax.broadcasted_iota(jnp.int32, owners.shape, 1)
+    found = []
+    for tile in tiles:
+        owner = jnp.sum(jnp.where(lane == tile, owners, 0.0), axis=1, keepdims=True)
+        before = jnp.where((owners == owner) & (lane < tile), 1.0, 0.0)
+        found.append((jnp.sum(owner).astype(jnp.int32), jnp.sum(before).astype(jnp.int32)))
+    return found
 
 
 def tiles_of(owner_ref, owner):
-    def find(tile, carry):
-        count, first, second = carry
-        mine = owner_ref[tile] == owner
-        first = jnp.where(mine & (count == 0), tile, first)
-        second = jnp.where(mine & (count == 1), tile, second)
-        return count + mine.astype(jnp.int32), first, second
-
-    zero = jnp.int32(0)
-    return lax.fori_loop(0, owner_ref.shape[0], find, (zero, zero, zero))
+    owners = owner_ref[...].astype(F32)
+    lane = lax.broadcasted_iota(jnp.int32, owners.shape, 1).astype(F32)
+    mine = owners == owner.astype(F32)
+    tiles = owners.shape[1]
+    count = jnp.sum(jnp.where(mine, 1.0, 0.0))
+    if tiles == PIECES:
+        return count, jnp.int32(0), jnp.int32(0)
+    first = jnp.min(jnp.where(mine, lane, tiles - 1.0)).astype(jnp.int32)
+    last = jnp.max(jnp.where(mine, lane, 0.0)).astype(jnp.int32)
+    return count, first, last
 
 
 def mate_of(me):
@@ -276,45 +266,45 @@
 def route_kernel(owner_ref, pieces_ref, *rest):
     edges_ref = rest[0] if len(rest) == 3 else None
     out_ref, seen = rest[-2:]
-    tiles = owner_ref.shape[0]
+    tiles = owner_ref.shape[1]
     me = own_place()
     base = me // PIECES * PIECES if tiles > PIECES else 0
     row = lax.broadcasted_iota(jnp.int32, (8, LANES), 0)
     mine = row // 4 == lax.rem(me, 2)
 
+    def send(tile, owner, slot):
+        at = tile - base
+        high = pieces_ref[jnp.maximum(at - 1, 0), 8:16]
+        low = pieces_ref[jnp.minimum(at + 1, PIECES - 1), :8]
+        if edges_ref is None:
+            edge_high, edge_low = jnp.zeros_like(high), jnp.zeros_like(low)
+        else:
+            edge_high, edge_low = edges_ref[0, 8:16], edges_ref[1, :8]
+        high = jnp.where(at > 0, high, edge_high)
+        low = jnp.where(at < PIECES - 1, low, edge_low)
+        packet = pieces_ref[at, :8] + high + pltpu.roll(low, 4, 0)
+        beside = jnp.where(mine, out_ref[owner, :8], pltpu.roll(packet, 4, 0))
+        out_ref[owner, :8] = jnp.where(slot == 0, packet, beside)
+        out_ref[owner, pl.ds(pl.multiple_of(8 + 8 * slot, 8), 8)] = pieces_ref[at, 16:]
+
+    if tiles == PIECES:
+        for tile, (owner, slot) in enumerate(slots_of(owner_ref, list(range(tiles)))):
+            send(jnp.int32(tile), owner, slot)
+        return
+
     def clear(at, carry):
         seen[at] = 0
         return carry
 
-    each(tiles, clear, 0)
-
-    def send(tile, carry):
-        owner = owner_ref[tile]
+    def count(tile, carry):
+        owner = owner_ref[0, tile]
         slot = seen[owner]
         seen[owner] = slot + 1
-        at = tile - base
-
-        def forward():
-            high = pieces_ref[jnp.maximum(at - 1, 0), 8:16]
-            low = pieces_ref[jnp.minimum(at + 1, PIECES - 1), :8]
-            if edges_ref is None:
-                edge_high, edge_low = jnp.zeros_like(high), jnp.zeros_like(low)
-            else:
-                edge_high, edge_low = edges_ref[0, 8:16], edges_ref[1, :8]
-            high = jnp.where(at > 0, high, edge_high)
-            low = jnp.where(at < PIECES - 1, low, edge_low)
-            packet = pieces_ref[at, :8] + high + pltpu.roll(low, 4, 0)
-            beside = jnp.where(mine, out_ref[owner, :8], pltpu.roll(packet, 4, 0))
-            out_ref[owner, :8] = jnp.where(slot == 0, packet, beside)
-            out_ref[owner, pl.ds(pl.multiple_of(8 + 8 * slot, 8), 8)] = pieces_ref[at, 16:]
-
-        if tiles > PIECES:
-            pl.when((at >= 0) & (at < PIECES))(forward)
-        else:
-            forward()
+        pl.when((tile >= base) & (tile < base + PIECES))(lambda: send(tile, owner, slot))
         return carry
 
-    each(tiles, send, 0)
+    lax.fori_loop(0, tiles, clear, 0)
+    lax.fori_loop(0, tiles, count, 0)
 
 
 def route(owner_list, pieces, edges):
@@ -324,13 +314,13 @@
     extra = [] if edges is None else [edges]
     return pl.pallas_call(
         route_kernel,
-        in_specs=[smem, vmem] + [vmem] * len(extra),
+        in_specs=[vmem if tiles == PIECES else smem, vmem] + [vmem] * len(extra),
         out_specs=vmem,
         out_shape=jax.ShapeDtypeStruct((tiles, 24, LANES), F32),
         scratch_shapes=[pltpu.SMEM((tiles,), jnp.int32)],
         compiler_params=pltpu.CompilerParams(vmem_limit_bytes=2**20),
         name="route",
-    )(owner_list, in_vmem(pieces), *extra)
+    )(owner_list.reshape(1, -1), in_vmem(pieces), *extra)
 
 
 def around(tile, tiles):
@@ -342,7 +332,7 @@
 
 
 def tile_pick_kernel(used, owner_ref, slopes_ref, out_ref):
-    tiles = [tile for tile, _ in around(mate_of(own_place()), owner_ref.shape[0])]
+    tiles = [tile for tile, _ in around(mate_of(own_place()), owner_ref.shape[1])]
     for at, (owner, slot) in enumerate(slots_of(owner_ref, tiles)):
         out_ref[at] = slot_half(slopes_ref[owner], slot, used)
 
@@ -352,12 +342,12 @@
     vmem = pl.BlockSpec(memory_space=pltpu.VMEM)
     return pl.pallas_call(
         functools.partial(tile_pick_kernel, freq_x + 1),
-        in_specs=[smem, vmem],
+        in_specs=[vmem, vmem],
         out_specs=vmem,
         out_shape=jax.ShapeDtypeStruct((3, 32, LANES), F32),
         compiler_params=pltpu.CompilerParams(vmem_limit_bytes=2**20),
         name="tile_pick",
-    )(owner_list, in_vmem(slopes))
+    )(owner_list.reshape(1, -1), in_vmem(slopes))
 
 
 def joined(me, mine, other):
@@ -371,7 +361,7 @@
     tile_px = out.shape[0]
     block = tile_px // BLOCKS
     me = own_place()
-    near = around(me, owner_ref.shape[0])
+    near = around(me, owner_ref.shape[1])
     packets = []
     for at, (owner, slot) in enumerate(slots_of(owner_ref, [tile for tile, _ in near])):
         packet = unpacked(joined(me, slot_half(slopes_ref[owner], slot, used), other_ref[at]), used)
@@ -424,7 +414,7 @@
     hbm = pl.BlockSpec(memory_space=pltpu.HBM)
     return pl.pallas_call(
         functools.partial(update_kernel, freq_x + 1),
-        in_specs=[smem] + [vmem] * 6,
+        in_specs=[vmem] * 7,
         out_specs=hbm,
         out_shape=jax.ShapeDtypeStruct(mask_tiles.shape, F32),
         scratch_shapes=[
@@ -435,7 +425,7 @@
         compiler_params=pltpu.CompilerParams(vmem_limit_bytes=16 * 2**20),
         name="mask_update",
     )(
-        owner_list, in_vmem(slopes), other, in_vmem(mask_tiles),
+        owner_list.reshape(1, -1), in_vmem(slopes), other, in_vmem(mask_tiles),
         in_vmem(cols), in_vmem(turns), in_vmem(rows),
     )
 
@@ -529,7 +519,7 @@
         target = jnp.concatenate(
             [pieces_ref[firsts[slot] + at, 8 + 8 * slot : 16 + 8 * slot] for at in range(PIECES)], axis=0
         )
-        targets.append(jnp.where(slot < count, target, 0.0))
+        targets.append(jnp.where(count > slot, target, 0.0))
         pieces = []
         for at in range(0, PIECES, 2):
             even, odd = pieces_ref[firsts[slot] + at, :8], pieces_ref[firsts[slot] + at + 1, :8]
@@ -538,7 +528,7 @@
             else:
                 pieces.append(pltpu.roll(jnp.where(upper, odd, even), 4, 0))
         packet = jnp.concatenate(pieces, axis=0)
-        packets += [jnp.where(slot < count, unpacked(packet, used), 0.0), blank]
+        packets += [jnp.where(count > slot, unpacked(packet, used), 0.0), blank]
 
     top, rest = halves(jnp.concatenate(packets, axis=0))
     both = mm(
@@ -630,8 +620,8 @@
         images = to_image([cols[at * freq_y : (at + 1) * freq_y] for at in range(len(places))])
         for at, (step, slot) in enumerate(places):
             k = start + step
-            weight = weight_ref[k]
-            new[2] = jnp.where(group_of == k, weight, new[2])
+            weight = weight_ref[:, k : k + 1]
+            new[2] = jnp.where(group_of == k, jnp.broadcast_to(weight, (8, LANES)), new[2])
             edge = edges[at * freq_y : (at + 1) * freq_y]
             column, place = divmod(k, QUARTER // 4)
             here = slice(column * LANES, (column + 1) * LANES)
@@ -747,7 +737,7 @@
     error = jnp.float32(0.0)
     rim_halves = []
     for slot in range(2):
-        live = (slot < count).astype(F32)
+        live = (count > slot).astype(F32)
         rim_parts = waves(to_image([rim_columns(slot)])[0])
         for part in range(4):
             rim_field[slot, part] = rim_parts[part]
@@ -795,7 +785,7 @@
         images, edges = [], []
         for step in range(chunk):
             k = start + step
-            weight = weight_ref[k]
+            weight = weight_ref[:, k : k + 1]
             for slot in range(MOST):
                 plus = scale_ref[slot, 0] * weight
                 minus = scale_ref[slot, 1] * weight
@@ -904,7 +894,7 @@
     hbm = pl.BlockSpec(memory_space=pltpu.HBM)
     return pl.pallas_call(
         functools.partial(imaging_kernel, places, freq_x + 1, len(later)),
-        in_specs=[smem, smem, vmem, vmem, vmem] + [hbm] * len(later),
+        in_specs=[vmem] * 5 + [hbm] * len(later),
         out_specs=(vmem, smem) + (vmem,) * len(later),
         out_shape=(
             jax.ShapeDtypeStruct((tiles, 2 * split - 8, LANES), F32),
@@ -925,7 +915,7 @@
         compiler_params=pltpu.CompilerParams(vmem_limit_bytes=20 * 2**20),
         name="owner_imaging",
     )(
-        owner_list, kern_weight, in_vmem(pieces), in_vmem(kernels),
+        owner_list.reshape(1, -1), kern_weight.reshape(1, -1), in_vmem(pieces), in_vmem(kernels),
         in_vmem(table), *[in_hbm(part) for part in later],
     )
 

time: 65.2 us -> 63.5 us (0.974)
  Pallas kernels: 19.3 us -> 17.6 us
    pallas_call x2, Pallas kernels: 4.03 us -> 3.33 us  [the longest x1 3.01 us: mask_update(): pl.pallas_call(functools.partial(update_kernel, freq_x + 1), in_specs=[vm...]
where the time goes in v7:
time: 63.5 us; the launch traced here: 63.2 us
  blocking collectives  43.6 us (69%)
  Pallas kernels  17.6 us (28%)
  waiting for transfers between devices  1.12 us (2%)
  between operations  0.69 us (1%)
    all_to_all x1, blocking collectives, on_device(): pieces, edges = (lax.all_to_all(pieces, 'tile', 0, 0, tiled=True), None)  16.2 us
    all_to_all x1, blocking collectives, on_device(): slopes = lax.all_to_all(slopes, 'tile', 0, 0, tiled=True)  15.9 us
    all_to_all x1, blocking collectives, on_device(): lax.all_to_all(route(owner_list, pieces, edges), 'tile', 0, 0, tiled=True)  11.6 us
    pallas_call x1, Pallas kernels, owner_imaging(): pl.pallas_call(functools.partial(imaging_kernel, places, freq_x + 1, len(...  9.99 us
    pallas_call x1, Pallas kernels, mask_spectrum(): pl.pallas_call(functools.partial(spectrum_kernel, freq_x + 1), in_specs=[...  4.01 us
    pallas_call x1, Pallas kernels, mask_update(): pl.pallas_call(functools.partial(update_kernel, freq_x + 1), in_specs=[vm...  3.01 us
  transfers between devices with their start and end apart: 1, of which 1 were waited for; matrix products, arithmetic and copies ran while one was open for 0% of the time, Pallas kernels for 0%

profile of v7, /device:TPU:0, one launch (start us, length us, event | category | flops | bytes accessed | tf_op | source)
XLA Modules:
  0.0 63.2 jit_solution(10767708175113833292)
XLA Ops:
  0.6 0.0 copy-start
  0.6 0.0 copy-start.2
  0.7 0.0 copy-start.3
  0.7 0.0 copy-start.1
  0.7 4.0 %mask_spectrum.1 = f32[16,24,128]{2,1,0:T(8,128)S(1)} custom-call(f32[1,1024,1024]{2,1,0:T(8,128)} %refs_5_.1, bf16[256,256]{1,0:T(8,128)(2,1)} %constant.12.clone.cols_hbm, f32[12,1,128]{2,1,0:T(1,128)} %constant.13.clone.turns_hbm.refs_7_, bf16[160,1024]{1,0:T(8,128)(2,1)} %constant.14.clone.rows_hbm, f32[128,128]{1,0:T(8,128)} %bitcast.8), custom_call_target="tpu_custom_call" | custom-call | tf_op jit(solution)/shard_map/mask_spectrum/pallas_call | solution.py:200
  4.7 16.2 %all_to_all.15.pieces_ref = f32[16,24,128]{2,1,0:T(8,128)S(1)} all-to-all(f32[16,24,128]{2,1,0:T(8,128)S(1)} %mask_spectrum.1), channel_id=1, replica_groups=mesh['stripe'=2,'tile'=16] {'tile'}, dimensions={0} | all-to-all | bytes 393216 | tf_op jit(solution)/shard_map/all_to_all | solution.py:935
  20.9 0.0 copy-done.2
  20.9 0.3 route.1
  21.2 11.6 %all_to_all.16.refs_2_ = f32[16,24,128]{2,1,0:T(8,128)S(1)} all-to-all(f32[16,24,128]{2,1,0:T(8,128)S(1)} %route.1), channel_id=1, replica_groups=mesh['stripe'=2,'tile'=16] {'tile'}, dimensions={0} | all-to-all | bytes 393216 | tf_op jit(solution)/shard_map/all_to_all | solution.py:944
  32.8 0.0 copy-done
  32.8 0.0 copy-done.3
  32.8 0.0 copy-done.1
  32.8 10.0 %owner_imaging.1 = (f32[16,56,128]{2,1,0:T(8,128)S(1)}, f32[1]{0:T(128)}, f32[1,1024,1024]{2,1,0:T(8,128)S(1)}, bf16[256,256]{1,0:T(8,128)(2,1)S(1)}, f32[12,1,1...) custom-call(s32[1,16]{1,0:T(1,128)S(1)} %bitcast.4, f32[1,24]{1,0:T(1,128)S(1)} %bitcast.7, ...), custom_call_target="tpu_custom_call" | custom-call | tf_op jit(solution)/shard_map/owner_imaging/pallas_call | solution.py:895
  42.8 15.9 %all_to_all.17.slopes_ref = f32[16,56,128]{2,1,0:T(8,128)S(1)} all-to-all(f32[16,56,128]{2,1,0:T(8,128)S(1)} %get-tuple-element.12), channel_id=1, replica_groups=mesh['stripe'=2,'tile'=16] {'tile'}, dimensions={0} | all-to-all | bytes 917504 | tf_op jit(solution)/shard_map/all_to_all | solution.py:949
  58.7 0.3 tile_pick.1
  59.0 0.1 collective-permute-start
  59.1 1.1 %collective-permute-done.other_ref = f32[3,32,128]{2,1,0:T(8,128)S(1)} collective-permute-done((f32[3,32,128]{2,1,0:T(8,128)S(1)}, f32[3,32,128]{2,1,0:T(8,128)S(1)}, u32[]{:S(2)}, u32[]{:S(2)}) %collective-permute-start) | collective-permute-done | bytes 49184 | tf_op jit(solution)/shard_map/ppermute | solution.py:950
  60.2 3.0 %mask_update.1 = f32[1,1024,1024]{2,1,0:T(8,128)} custom-call(s32[1,16]{1,0:T(1,128)S(1)} %bitcast.6, f32[16,56,128]{2,1,0:T(8,128)S(1)} %all_to_all.17.slopes_ref, f32[3,32,128]{2,1,0:T(8,128)S(1)} %collective-permute-done.other_ref, f32[1,1024,1024]{2,1,0:T(8,128)S(1)} %get-tuple-element.13.mask_ref, bf16[256,256]{1,0:T(8,128)(2,1)S(1)} %get-tuple-element.14.cols, ...), custom_call_target="tpu_custom_call" | custom-call | tf_op jit(solution)/shard_map/mask_update/pallas_call | solution.py:415
Async XLA Ops:
  0.6 32.2 %copy-start = (bf16[3872,256]{1,0:T(8,128)(2,1)S(1)}, bf16[3872,256]{1,0:T(8,128)(2,1)}, u32[]{:S(2)}) copy-start(bf16[3872,256]{1,0:T(8,128)(2,1)} %constant.15.clone.refs_4_) | copy-start | bytes 5947396
  0.6 20.2 %copy-start.2 = (s32[16,1]{0,1:T(1,128)S(1)}, s32[16,1]{0,1:T(1,128)}, u32[]{:S(2)}) copy-start(s32[16,1]{0,1:T(1,128)} %param.15) | copy-start | bytes 196
  0.7 32.2 %copy-start.3 = (f32[24]{0:T(128)S(1)}, f32[24]{0:T(128)}, u32[]{:S(2)}) copy-start(f32[24]{0:T(128)} %param.14) | copy-start | bytes 292
  0.7 32.1 %copy-start.1 = (f32[1,2,24,64,96]{4,3,2,1,0:T(8,128)S(1)}, f32[1,2,24,64,96]{4,3,2,1,0:T(8,128)}, u32[]{:S(2)}) copy-start(f32[1,2,24,64,96]{4,3,2,1,0:T(8,128)} %refs_3_.1) | copy-start | bytes 3538948
  59.0 1.3 %collective-permute-start = (f32[3,32,128]{2,1,0:T(8,128)S(1)}, f32[3,32,128]{2,1,0:T(8,128)S(1)}, u32[]{:S(2)}, u32[]{:S(2)}) collective-permute-start(f32[3,32,128]{2,1,0:T(8,128)S(1)} %tile_pick.1), channel_id=1, source_target_pairs={{0,1},{1,0},{2,3},{3,2},{4,5},{5,4},{6,7},{7,6},{8,9},{9,8},{10,11... | collective-permute-start | bytes 147464 | tf_op jit(solution)/shard_map/ppermute | solution.py:950

commit v8 on v7

--- a/solution.py
+++ b/solution.py
@@ -499,7 +499,7 @@
     owner_ref, weight_ref, pieces_ref, kern_ref, table_ref = refs[:5]
     later_hbm, refs = refs[5 : 5 + extra], refs[5 + extra :]
     slopes_ref, error_ref, later_ref, refs = refs[0], refs[1], refs[2 : 2 + extra], refs[2 + extra :]
-    spec, field, rim_field, rim_lanes, rim_slope, scale_ref, ready, goal_ref, sems = refs
+    spec, field, rim_field, rim_slope, scale_ref, ready, goal_ref, sems = refs
     kern_count, freq_y, freq_x = kern_ref.shape[2:]
     later = fetch(list(zip(later_hbm, later_ref)), sems)
     chunk = max(size for size in range(1, CHUNK + 1) if kern_count % size == 0)
@@ -600,6 +600,8 @@
         below = jnp.concatenate([plus_im - minus_im, minus_re - plus_re], axis=1)
         return jnp.concatenate([above, below], axis=0)
 
+
+    rim_sums = [[] for _ in range(MOST)]
 
     def forward_chunk(start, new):
         tops, rests = [], []
@@ -624,11 +626,10 @@
             new[2] = jnp.where(group_of == k, jnp.broadcast_to(weight, (8, LANES)), new[2])
             edge = edges[at * freq_y : (at + 1) * freq_y]
             column, place = divmod(k, QUARTER // 4)
-            here = slice(column * LANES, (column + 1) * LANES)
             if place == 0:
-                rim_lanes[slot, :, here] = edge
+                rim_sums[slot].append(edge)
             else:
-                rim_lanes[slot, :, here] += pltpu.roll(edge, 4 * place, 1)
+                rim_sums[slot][column] = rim_sums[slot][column] + pltpu.roll(edge, 4 * place, 1)
             parts = waves(images[at])
             for part in range(4):
                 field[slot, k, part] = parts[part]
@@ -725,8 +726,7 @@
     def rim_columns(slot):
         quarter = lax.rem(lane + 2, LANES) // QUARTER
         real = imag = jnp.zeros((freq_y, LANES), F32)
-        for column in range(rim_lanes.shape[2] // LANES):
-            both = rim_lanes[slot, :, column * LANES : (column + 1) * LANES]
+        for column, both in enumerate(rim_sums[slot]):
             both = both + pltpu.roll(both, 2 * QUARTER, 1)
             for_real = both if column == 0 else pltpu.roll(both, column * QUARTER, 1)
             for_imag = both if column == 1 else pltpu.roll(both, (column - 1) * QUARTER % LANES, 1)
@@ -905,7 +905,6 @@
             pltpu.VMEM((MOST, 2 * freq_y, LANES), F32),
             pltpu.VMEM((MOST, kern_count, 4, half, LANES), F32),
             pltpu.VMEM((MOST, 4, half, LANES), F32),
-            pltpu.VMEM((MOST, freq_y, -(-kern_count * 4 // QUARTER) * LANES), F32),
             pltpu.VMEM((MOST, freq_y, -(-kern_count * RIM_WIDTH // LANES) * LANES), F32),
             pltpu.VMEM((MOST, 2, half, LANES), F32),
             pltpu.VMEM((2, 2 * split - 8, LANES), F32),

time: 63.5 us -> 63.5 us (level)
  no operation moved by 1% of the time
where the time goes in v8:
time: 63.5 us; the launch traced here: 63.2 us
  blocking collectives  43.6 us (69%)
  Pallas kernels  17.6 us (28%)
  waiting for transfers between devices  1.12 us (2%)
  between operations  0.69 us (1%)
    all_to_all x1, blocking collectives, on_device(): pieces, edges = (lax.all_to_all(pieces, 'tile', 0, 0, tiled=True), None)  16.2 us
    all_to_all x1, blocking collectives, on_device(): slopes = lax.all_to_all(slopes, 'tile', 0, 0, tiled=True)  15.9 us
    all_to_all x1, blocking collectives, on_device(): lax.all_to_all(route(owner_list, pieces, edges), 'tile', 0, 0, tiled=True)  11.6 us
    pallas_call x1, Pallas kernels, owner_imaging(): pl.pallas_call(functools.partial(imaging_kernel, places, freq_x + 1, len(...  9.99 us
    pallas_call x1, Pallas kernels, mask_spectrum(): pl.pallas_call(functools.partial(spectrum_kernel, freq_x + 1), in_specs=[...  4.01 us
    pallas_call x1, Pallas kernels, mask_update(): pl.pallas_call(functools.partial(update_kernel, freq_x + 1), in_specs=[vm...  3 us
  transfers between devices with their start and end apart: 1, of which 1 were waited for; matrix products, arithmetic and copies ran while one was open for 0% of the time, Pallas kernels for 0%

profile of v8, /device:TPU:0, one launch (start us, length us, event | category | flops | bytes accessed | tf_op | source)
XLA Modules:
  0.0 63.2 jit_solution(10767708175113833292)
XLA Ops:
  0.6 0.0 copy-start
  0.6 0.0 copy-start.2
  0.7 0.0 copy-start.3
  0.7 0.0 copy-start.1
  0.7 4.0 %mask_spectrum.1 = f32[16,24,128]{2,1,0:T(8,128)S(1)} custom-call(f32[1,1024,1024]{2,1,0:T(8,128)} %refs_5_.1, bf16[256,256]{1,0:T(8,128)(2,1)} %constant.12.clone.cols_hbm, f32[12,1,128]{2,1,0:T(1,128)} %constant.13.clone.turns_hbm.refs_7_, bf16[160,1024]{1,0:T(8,128)(2,1)} %constant.14.clone.rows_hbm, f32[128,128]{1,0:T(8,128)} %bitcast.8), custom_call_target="tpu_custom_call" | custom-call | tf_op jit(solution)/shard_map/mask_spectrum/pallas_call | solution.py:200
  4.7 16.2 %all_to_all.15.pieces_ref = f32[16,24,128]{2,1,0:T(8,128)S(1)} all-to-all(f32[16,24,128]{2,1,0:T(8,128)S(1)} %mask_spectrum.1), channel_id=1, replica_groups=mesh['stripe'=2,'tile'=16] {'tile'}, dimensions={0} | all-to-all | bytes 393216 | tf_op jit(solution)/shard_map/all_to_all | solution.py:934
  20.9 0.0 copy-done.2
  20.9 0.3 route.1
  21.2 11.6 %all_to_all.16.refs_2_ = f32[16,24,128]{2,1,0:T(8,128)S(1)} all-to-all(f32[16,24,128]{2,1,0:T(8,128)S(1)} %route.1), channel_id=1, replica_groups=mesh['stripe'=2,'tile'=16] {'tile'}, dimensions={0} | all-to-all | bytes 393216 | tf_op jit(solution)/shard_map/all_to_all | solution.py:943
  32.8 0.0 copy-done
  32.8 0.0 copy-done.3
  32.8 0.0 copy-done.1
  32.8 10.0 %owner_imaging.1 = (f32[16,56,128]{2,1,0:T(8,128)S(1)}, f32[1]{0:T(128)}, f32[1,1024,1024]{2,1,0:T(8,128)S(1)}, bf16[256,256]{1,0:T(8,128)(2,1)S(1)}, f32[12,1,1...) custom-call(s32[1,16]{1,0:T(1,128)S(1)} %bitcast.4, f32[1,24]{1,0:T(1,128)S(1)} %bitcast.7, ...), custom_call_target="tpu_custom_call" | custom-call | tf_op jit(solution)/shard_map/owner_imaging/pallas_call | solution.py:895
  42.8 15.9 %all_to_all.17.slopes_ref = f32[16,56,128]{2,1,0:T(8,128)S(1)} all-to-all(f32[16,56,128]{2,1,0:T(8,128)S(1)} %get-tuple-element.12), channel_id=1, replica_groups=mesh['stripe'=2,'tile'=16] {'tile'}, dimensions={0} | all-to-all | bytes 917504 | tf_op jit(solution)/shard_map/all_to_all | solution.py:948
  58.7 0.3 tile_pick.1
  59.0 0.1 collective-permute-start
  59.1 1.1 %collective-permute-done.other_ref = f32[3,32,128]{2,1,0:T(8,128)S(1)} collective-permute-done((f32[3,32,128]{2,1,0:T(8,128)S(1)}, f32[3,32,128]{2,1,0:T(8,128)S(1)}, u32[]{:S(2)}, u32[]{:S(2)}) %collective-permute-start) | collective-permute-done | bytes 49184 | tf_op jit(solution)/shard_map/ppermute | solution.py:949
  60.2 3.0 %mask_update.1 = f32[1,1024,1024]{2,1,0:T(8,128)} custom-call(s32[1,16]{1,0:T(1,128)S(1)} %bitcast.6, f32[16,56,128]{2,1,0:T(8,128)S(1)} %all_to_all.17.slopes_ref, f32[3,32,128]{2,1,0:T(8,128)S(1)} %collective-permute-done.other_ref, f32[1,1024,1024]{2,1,0:T(8,128)S(1)} %get-tuple-element.13.mask_ref, bf16[256,256]{1,0:T(8,128)(2,1)S(1)} %get-tuple-element.14.cols, ...), custom_call_target="tpu_custom_call" | custom-call | tf_op jit(solution)/shard_map/mask_update/pallas_call | solution.py:415
Async XLA Ops:
  0.6 32.2 %copy-start = (bf16[3872,256]{1,0:T(8,128)(2,1)S(1)}, bf16[3872,256]{1,0:T(8,128)(2,1)}, u32[]{:S(2)}) copy-start(bf16[3872,256]{1,0:T(8,128)(2,1)} %constant.15.clone.refs_4_) | copy-start | bytes 5947396
  0.6 20.2 %copy-start.2 = (s32[16,1]{0,1:T(1,128)S(1)}, s32[16,1]{0,1:T(1,128)}, u32[]{:S(2)}) copy-start(s32[16,1]{0,1:T(1,128)} %param.15) | copy-start | bytes 196
  0.7 32.2 %copy-start.3 = (f32[24]{0:T(128)S(1)}, f32[24]{0:T(128)}, u32[]{:S(2)}) copy-start(f32[24]{0:T(128)} %param.14) | copy-start | bytes 292
  0.7 32.1 %copy-start.1 = (f32[1,2,24,64,96]{4,3,2,1,0:T(8,128)S(1)}, f32[1,2,24,64,96]{4,3,2,1,0:T(8,128)}, u32[]{:S(2)}) copy-start(f32[1,2,24,64,96]{4,3,2,1,0:T(8,128)} %refs_3_.1) | copy-start | bytes 3538948
  59.0 1.3 %collective-permute-start = (f32[3,32,128]{2,1,0:T(8,128)S(1)}, f32[3,32,128]{2,1,0:T(8,128)S(1)}, u32[]{:S(2)}, u32[]{:S(2)}) collective-permute-start(f32[3,32,128]{2,1,0:T(8,128)S(1)} %tile_pick.1), channel_id=1, source_target_pairs={{0,1},{1,0},{2,3},{3,2},{4,5},{5,4},{6,7},{7,6},{8,9},{9,8},{10,11... | collective-permute-start | bytes 147464 | tf_op jit(solution)/shard_map/ppermute | solution.py:949

commit v9 on v7

--- a/solution.py
+++ b/solution.py
@@ -19,7 +19,7 @@
 
 LANES = 128
 MOST = 2
-BLOCKS = 4
+BLOCKS = 8
 PIECES = 16
 CHUNK = 6
 QUARTER = 32

time: 63.5 us -> 63.4 us (level)
  no operation moved by 1% of the time
where the time goes in v9:
time: 63.4 us; the launch traced here: 63.2 us
  blocking collectives  43.6 us (69%)
  Pallas kernels  17.6 us (28%)
  waiting for transfers between devices  1.12 us (2%)
  between operations  0.69 us (1%)
    all_to_all x1, blocking collectives, on_device(): pieces, edges = (lax.all_to_all(pieces, 'tile', 0, 0, tiled=True), None)  16.2 us
    all_to_all x1, blocking collectives, on_device(): slopes = lax.all_to_all(slopes, 'tile', 0, 0, tiled=True)  15.9 us
    all_to_all x1, blocking collectives, on_device(): lax.all_to_all(route(owner_list, pieces, edges), 'tile', 0, 0, tiled=True)  11.6 us
    pallas_call x1, Pallas kernels, owner_imaging(): pl.pallas_call(functools.partial(imaging_kernel, places, freq_x + 1, len(...  9.99 us
    pallas_call x1, Pallas kernels, mask_spectrum(): pl.pallas_call(functools.partial(spectrum_kernel, freq_x + 1), in_specs=[...  4.01 us
    pallas_call x1, Pallas kernels, mask_update(): pl.pallas_call(functools.partial(update_kernel, freq_x + 1), in_specs=[vm...  2.96 us
  transfers between devices with their start and end apart: 1, of which 1 were waited for; matrix products, arithmetic and copies ran while one was open for 0% of the time, Pallas kernels for 0%

profile of v9, /device:TPU:0, one launch (start us, length us, event | category | flops | bytes accessed | tf_op | source)
XLA Modules:
  0.0 63.2 jit_solution(13221754107382798197)
XLA Ops:
  0.6 0.0 copy-start
  0.6 0.0 copy-start.2
  0.7 0.0 copy-start.3
  0.7 0.0 copy-start.1
  0.7 4.0 %mask_spectrum.1 = f32[16,24,128]{2,1,0:T(8,128)S(1)} custom-call(f32[1,1024,1024]{2,1,0:T(8,128)} %refs_5_.1, bf16[256,256]{1,0:T(8,128)(2,1)} %constant.12.clone.cols_hbm, f32[12,1,128]{2,1,0:T(1,128)} %constant.13.clone.turns_hbm.refs_7_, bf16[160,1024]{1,0:T(8,128)(2,1)} %constant.14.clone.rows_hbm, f32[128,128]{1,0:T(8,128)} %bitcast.8), custom_call_target="tpu_custom_call" | custom-call | tf_op jit(solution)/shard_map/mask_spectrum/pallas_call | solution.py:200
  4.7 16.2 %all_to_all.15.pieces_ref = f32[16,24,128]{2,1,0:T(8,128)S(1)} all-to-all(f32[16,24,128]{2,1,0:T(8,128)S(1)} %mask_spectrum.1), channel_id=1, replica_groups=mesh['stripe'=2,'tile'=16] {'tile'}, dimensions={0} | all-to-all | bytes 393216 | tf_op jit(solution)/shard_map/all_to_all | solution.py:935
  20.9 0.0 copy-done.2
  20.9 0.3 route.1
  21.2 11.6 %all_to_all.16.refs_2_ = f32[16,24,128]{2,1,0:T(8,128)S(1)} all-to-all(f32[16,24,128]{2,1,0:T(8,128)S(1)} %route.1), channel_id=1, replica_groups=mesh['stripe'=2,'tile'=16] {'tile'}, dimensions={0} | all-to-all | bytes 393216 | tf_op jit(solution)/shard_map/all_to_all | solution.py:944
  32.8 0.0 copy-done
  32.8 0.0 copy-done.3
  32.8 0.0 copy-done.1
  32.8 10.0 %owner_imaging.1 = (f32[16,56,128]{2,1,0:T(8,128)S(1)}, f32[1]{0:T(128)}, f32[1,1024,1024]{2,1,0:T(8,128)S(1)}, bf16[256,256]{1,0:T(8,128)(2,1)S(1)}, f32[12,1,1...) custom-call(s32[1,16]{1,0:T(1,128)S(1)} %bitcast.4, f32[1,24]{1,0:T(1,128)S(1)} %bitcast.7, ...), custom_call_target="tpu_custom_call" | custom-call | tf_op jit(solution)/shard_map/owner_imaging/pallas_call | solution.py:895
  42.8 15.9 %all_to_all.17.slopes_ref = f32[16,56,128]{2,1,0:T(8,128)S(1)} all-to-all(f32[16,56,128]{2,1,0:T(8,128)S(1)} %get-tuple-element.12), channel_id=1, replica_groups=mesh['stripe'=2,'tile'=16] {'tile'}, dimensions={0} | all-to-all | bytes 917504 | tf_op jit(solution)/shard_map/all_to_all | solution.py:949
  58.7 0.3 tile_pick.1
  59.0 0.1 collective-permute-start
  59.1 1.1 %collective-permute-done.other_ref = f32[3,32,128]{2,1,0:T(8,128)S(1)} collective-permute-done((f32[3,32,128]{2,1,0:T(8,128)S(1)}, f32[3,32,128]{2,1,0:T(8,128)S(1)}, u32[]{:S(2)}, u32[]{:S(2)}) %collective-permute-start) | collective-permute-done | bytes 49184 | tf_op jit(solution)/shard_map/ppermute | solution.py:950
  60.2 3.0 %mask_update.1 = f32[1,1024,1024]{2,1,0:T(8,128)} custom-call(s32[1,16]{1,0:T(1,128)S(1)} %bitcast.6, f32[16,56,128]{2,1,0:T(8,128)S(1)} %all_to_all.17.slopes_ref, f32[3,32,128]{2,1,0:T(8,128)S(1)} %collective-permute-done.other_ref, f32[1,1024,1024]{2,1,0:T(8,128)S(1)} %get-tuple-element.13.mask_ref, bf16[256,256]{1,0:T(8,128)(2,1)S(1)} %get-tuple-element.14.cols, ...), custom_call_target="tpu_custom_call" | custom-call | tf_op jit(solution)/shard_map/mask_update/pallas_call | solution.py:415
Async XLA Ops:
  0.6 32.2 %copy-start = (bf16[3872,256]{1,0:T(8,128)(2,1)S(1)}, bf16[3872,256]{1,0:T(8,128)(2,1)}, u32[]{:S(2)}) copy-start(bf16[3872,256]{1,0:T(8,128)(2,1)} %constant.15.clone.refs_4_) | copy-start | bytes 5947396
  0.6 20.2 %copy-start.2 = (s32[16,1]{0,1:T(1,128)S(1)}, s32[16,1]{0,1:T(1,128)}, u32[]{:S(2)}) copy-start(s32[16,1]{0,1:T(1,128)} %param.15) | copy-start | bytes 196
  0.7 32.2 %copy-start.3 = (f32[24]{0:T(128)S(1)}, f32[24]{0:T(128)}, u32[]{:S(2)}) copy-start(f32[24]{0:T(128)} %param.14) | copy-start | bytes 292
  0.7 32.1 %copy-start.1 = (f32[1,2,24,64,96]{4,3,2,1,0:T(8,128)S(1)}, f32[1,2,24,64,96]{4,3,2,1,0:T(8,128)}, u32[]{:S(2)}) copy-start(f32[1,2,24,64,96]{4,3,2,1,0:T(8,128)} %refs_3_.1) | copy-start | bytes 3538948
  59.0 1.3 %collective-permute-start = (f32[3,32,128]{2,1,0:T(8,128)S(1)}, f32[3,32,128]{2,1,0:T(8,128)S(1)}, u32[]{:S(2)}, u32[]{:S(2)}) collective-permute-start(f32[3,32,128]{2,1,0:T(8,128)S(1)} %tile_pick.1), channel_id=1, source_target_pairs={{0,1},{1,0},{2,3},{3,2},{4,5},{5,4},{6,7},{7,6},{8,9},{9,8},{10,11... | collective-permute-start | bytes 147464 | tf_op jit(solution)/shard_map/ppermute | solution.py:950
